TPU v7x, 32 devices: a whole 2x2x4 slice. The times are simulated.
32 devices in a mesh: parts: 2 (over y), region: 8 (over z, x), narrow: 2 (over core).
Axes of the slice: x: 2, y: 2, z: 4, core: 2. Of those that a mesh axis runs over, the one named last changes fastest.
Arguments:
- queries: bfloat16 [4096, 1024], P(('parts', 'region', 'narrow')), parts along dimension 0, may hold values from -6 to 6
- probes: int32 [4096, 4], P(('parts', 'region', 'narrow')), parts along dimension 0, may hold values from 0 to 7, all different within a row; in each aligned block of 128 rows (0 to 127, 128 to 255, ...) at most 128 rows name the same one
- fine_blocks: int32 [4096, 4, 4], P(('parts', 'region', 'narrow')), parts along dimension 0, may hold values from 0 to 15, as said below
- centroids: bfloat16 [8, 2048, 1024], P('region', 'narrow'), may hold values from -6 to 6
Outputs:
- scores: bfloat16 [4096, 4, 512], P(('parts', 'region', 'narrow')), parts along dimension 0
There are 2 independent parts, one for each index of `parts`. A program takes and returns all parts, laid end to end along the dimension named above; an argument that names none is the same for every part. Nothing has to cross between parts.
Inputs may be any that keep to these rules, and one draw needn't show every extreme that they name: `probes`: a query's 4 regions differ; of the 128 x 4 entries of one device's queries at most 128 name one region. `fine_blocks`: the 4 blocks of one query and probe differ.
All inputs are finite; a program needn't handle non-finite values.
Results may differ from a plain program's by a relative error of at most 0.001.
Values may be sent and summed in bfloat16 or wider, within the bound.
No kernel may reach another device: no remote copies, remote signals or barrier semaphores. Data moves between devices by JAX's collectives and lax.ppermute only.
A program may use at most 64 MiB of HBM per device.

v0:
```python
import math

import jax
import jax.numpy as jnp
from jax import lax
from jax.sharding import PartitionSpec as P

BLK = 128


def score_against(flat_rows, centre_rows):
    inner_prod = jnp.einsum("nd,md->nm", flat_rows, centre_rows, preferred_element_type=jnp.float32)
    widened = centre_rows.astype(jnp.float32)
    sq_norm = jnp.sum(widened * widened, axis=1)
    width = flat_rows.shape[1]
    return inner_prod / math.sqrt(width) - 0.5 * sq_norm[None, :] / width


def pick_blocks(scored, block_ids, block_len):
    row_count = scored.shape[0]
    blocked = scored.reshape(row_count, -1, block_len)
    block_total = blocked.shape[1]
    chooser = (
        block_ids[:, :, None] == jnp.arange(block_total, dtype=jnp.int32)[None, None, :]
    ).astype(jnp.float32)
    selected = jnp.einsum("rjb,rbk->rjk", chooser, blocked, precision=lax.Precision.HIGHEST)
    return selected.reshape(row_count, -1)


def per_device(queries, probes, fine_blocks, centroids):
    q_count, probe_count = probes.shape
    n_active = fine_blocks.shape[2]
    width = queries.shape[1]
    regions = lax.axis_size("region")
    capacity = max(2, min(q_count, 2 * q_count * probe_count // regions))
    slot_count = q_count * probe_count
    target_region = probes.reshape(slot_count)
    one_hot = (target_region[:, None] == jnp.arange(regions, dtype=jnp.int32)[None, :]).astype(
        jnp.float32
    )
    slot_index = jnp.arange(slot_count, dtype=jnp.int32)
    strict_lower = (slot_index[:, None] > slot_index[None, :]).astype(jnp.float32)
    earlier = jnp.dot(
        strict_lower, one_hot, precision=lax.Precision.HIGHEST, preferred_element_type=jnp.float32
    )
    slot_pos = jnp.sum(earlier * one_hot, axis=1).astype(jnp.int32)
    target_slot = target_region * capacity + slot_pos
    slot_match = jnp.arange(regions * capacity, dtype=jnp.int32)[:, None] == target_slot[None, :]
    query_match = jnp.any(
        slot_match.reshape(regions * capacity, q_count, probe_count), axis=2
    ).astype(jnp.bfloat16)
    send_rows = jnp.dot(query_match, queries, preferred_element_type=jnp.float32).astype(
        jnp.bfloat16
    )
    send_rows = send_rows.reshape(regions, capacity, width)
    block_values = fine_blocks.reshape(slot_count, n_active).astype(jnp.float32)
    send_blocks = jnp.dot(
        slot_match.astype(jnp.float32),
        block_values,
        precision=lax.Precision.HIGHEST,
        preferred_element_type=jnp.float32,
    ).astype(jnp.int32)
    send_blocks = send_blocks.reshape(regions, capacity, n_active)
    local_centres = centroids[0]
    block_len = BLK
    in_rows = lax.all_to_all(send_rows, "region", split_axis=0, concat_axis=0, tiled=True)
    in_blocks = lax.all_to_all(send_blocks, "region", split_axis=0, concat_axis=0, tiled=True)
    sender_count = in_rows.shape[0]
    item_count = in_rows.shape[1]
    flat_rows = in_rows.reshape(sender_count * item_count, width)
    flat_blocks = in_blocks.reshape(sender_count * item_count, n_active)
    scored = score_against(flat_rows, lax.all_gather(local_centres, "narrow", axis=0, tiled=True))
    packed = pick_blocks(scored, flat_blocks, block_len).astype(jnp.bfloat16)
    packed = packed.reshape(sender_count, item_count, n_active * block_len)
    returned_all = lax.all_to_all(packed, "region", split_axis=0, concat_axis=0, tiled=True)
    flat_returned = returned_all.reshape(regions * capacity, -1)
    answers = jnp.dot(
        slot_match.T.astype(jnp.bfloat16), flat_returned, preferred_element_type=jnp.float32
    ).astype(jnp.bfloat16)
    return answers.reshape(q_count, probe_count, -1)


def solution(mesh):
    return jax.shard_map(
        per_device,
        mesh=mesh,
        in_specs=(
            P(("parts", "region", "narrow"), None),
            P(("parts", "region", "narrow"), None),
            P(("parts", "region", "narrow"), None, None),
            P("region", "narrow", None),
        ),
        out_specs=P(("parts", "region", "narrow"), None, None),
        check_vma=False,
    )
```

profile of v0, /device:TPU:0, one launch (start us, length us, event | category | flops | bytes accessed | tf_op | source)
XLA Modules:
  0.0 129.1 jit_solution(15467108890314163365)
XLA Ops:
  6.5 0.7 all-gather.3.cloned.1.call-update
  7.3 0.8 copy.30
  8.0 0.1 reshape.54
  8.2 0.7 convert_element_type.43
  8.9 0.1 copy.31
  9.0 0.2 convert_element_type.44
  9.2 0.3 fusion.9
  9.5 1.6 %fusion.8 = s32[8,128,4]{1,2,0:T(4,128)} fusion(f32[512,4]{0,1:T(4,128)S(1)} %convert_element_type.44, s32[512]{0:T(512)S(1)} %multiply_add_fusion.1), kind=kOutput, calls=%fused_computation.15 | convolution fusion | flops 25694208 | bytes 26624 | tf_op jit(solution)/shard_map/dot_general | solution.py:57
  11.1 7.3 %all-to-all-start = ((s32[8,128,4]{1,2,0:T(4,128)}), s32[8,128,4]{1,2,0:T(4,128)S(1)}, u32[]{:S(2)}, u32[]{:S(2)}) async-start(s32[8,128,4]{1,2,0:T(4,128)} %fusion.8), calls=%async_computation | async-start | bytes 32768 | tf_op jit(solution)/shard_map/all_to_all | solution.py:67
  18.5 0.7 multiply_add_fusion
  19.2 0.4 fusion.4
  19.6 2.0 %convolution_convert_fusion = bf16[1024,1024]{1,0:T(8,128)(2,1)} fusion(pred[1024,128]{1,0:T(8,128)(4,1)S(1)} %fusion.4, bf16[128,1024]{1,0:T(8,128)(2,1)S(1)} %copy-done), kind=kOutput, calls=%fused_computation.10 | convolution fusion | flops 269484032 | bytes 2490368 | tf_op jit(solution)/shard_map/dot_general | solution.py:52
  21.7 3.3 %all-to-all-done = s32[8,128,4]{1,2,0:T(4,128)S(1)} async-done(((s32[8,128,4]{1,2,0:T(4,128)}), s32[8,128,4]{1,2,0:T(4,128)S(1)}, u32[]{:S(2)}, u32[]{:S(2)}) %all-to-all-start) | async-done | bytes 16416 | tf_op jit(solution)/shard_map/all_to_all | solution.py:67
  24.9 4.3 %all-to-all-start.1 = ((bf16[8,128,1024]{2,1,0:T(8,128)(2,1)}), bf16[8,128,1024]{2,1,0:T(8,128)(2,1)}, u32[]{:S(2)}, u32[]{:S(2)}) async-start(bf16[8,128,1024]{2,1,0:T(8,128)(2,1)} %bitcast.2), calls=%async_computation.1 | async-start | bytes 4194304 | tf_op jit(solution)/shard_map/all_to_all | solution.py:66
  29.3 0.2 copy.33
  29.5 3.1 %multiply_reduce_fusion = f32[2048]{0:T(1024)S(1)} fusion(bf16[1,2048,1024]{2,1,0:T(8,128)(2,1)} %all-gather.3.cloned.1.call-done), kind=kLoop, calls=%fused_computation.1 | loop fusion | flops 6289408 | bytes 4202496 | tf_op jit(solution)/shard_map/reduce_sum | solution.py:14
  32.6 43.7 %all-to-all-done.1 = bf16[8,128,1024]{2,1,0:T(8,128)(2,1)} async-done(((bf16[8,128,1024]{2,1,0:T(8,128)(2,1)}), bf16[8,128,1024]{2,1,0:T(8,128)(2,1)}, u32[]{:S(2)}, u32[]{:S(2)}) %all-to-all-start.1) | async-done | bytes 2097184 | tf_op jit(solution)/shard_map/all_to_all | solution.py:66
  76.4 7.0 %subtract_bitcast_fusion = f32[128,8,16,128]{3,1,2,0:T(8,128)S(1)} fusion(bf16[1024,1024]{1,0:T(8,128)(2,1)} %bitcast.3, bf16[1,2048,1024]{2,1,0:T(8,128)(2,1)} %all-gather.3.cloned.1.call-done, f32[2048]{0:T(1024)S(1)} %broadcast_multiply_fusion), kind=kOutput, calls=%fused_computation | convolution fusion | flops 4299161600 | bytes 14688256 | tf_op jit(solution)/shard_map/nd,md->nm/dot_general | solution.py:12
  83.4 2.0 %copy.35 = f32[128,8,16,128]{3,2,1,0:T(8,128)S(1)} copy(f32[128,8,16,128]{3,1,2,0:T(8,128)S(1)} %subtract_bitcast_fusion) | data formatting | bytes 16777216
  85.4 5.4 %fusion.5 = bf16[1024,4,128]{2,1,0:T(4,128)(2,1)S(1)} fusion(f32[1024,16,128]{2,1,0:T(8,128)S(1)} %bitcast.21, s32[1024,4]{1,0:T(8,128)S(1)} %copy.33), kind=kOutput, calls=%fused_computation.11 | convolution fusion | flops 101253120 | bytes 9453568 | tf_op jit(solution)/shard_map/rjb,rbk->rjk/dot_general | solution.py:26
  90.8 0.4 convert_element_type.50
  91.2 29.3 %all_to_all.15 = bf16[8,128,512]{2,1,0:T(8,128)(2,1)S(1)} all-to-all(bf16[8,128,512]{2,1,0:T(8,128)(2,1)S(1)} %convert_element_type.50), channel_id=1, replica_groups=mesh['parts'=2,'region'=8,'narrow'=2] {'region'}, dimensions={0} | all-to-all | bytes 2097152 | tf_op jit(solution)/shard_map/all_to_all | solution.py:75
  120.6 0.8 fusion.6
  121.3 0.9 reshape.60
  (9 shorter events, 0.2 us)
Async XLA Ops:
  6.5 13.1 %copy-start = (bf16[128,1024]{1,0:T(8,128)(2,1)S(1)}, bf16[128,1024]{1,0:T(8,128)(2,1)}, u32[]{:S(2)}) copy-start(bf16[128,1024]{1,0:T(8,128)(2,1)} %param.4) | copy-start | bytes 786436
  6.5 23.0 %all-gather.3.cloned.1.call-start = ((), (), s32[]{:S(2)}) async-start(), calls=%async_computation.3 | async-start | bytes 6291456 | tf_op jit(solution)/shard_map/all_gather | solution.py:72
  11.1 13.8 %all-to-all-start = ((s32[8,128,4]{1,2,0:T(4,128)}), s32[8,128,4]{1,2,0:T(4,128)S(1)}, u32[]{:S(2)}, u32[]{:S(2)}) async-start(s32[8,128,4]{1,2,0:T(4,128)} %fusion.8), calls=%async_computation | async-start | bytes 32768 | tf_op jit(solution)/shard_map/all_to_all | solution.py:67
  24.9 51.4 %all-to-all-start.1 = ((bf16[8,128,1024]{2,1,0:T(8,128)(2,1)}), bf16[8,128,1024]{2,1,0:T(8,128)(2,1)}, u32[]{:S(2)}, u32[]{:S(2)}) async-start(bf16[8,128,1024]{2,1,0:T(8,128)(2,1)} %bitcast.2), calls=%async_computation.1 | async-start | bytes 4194304 | tf_op jit(solution)/shard_map/all_to_all | solution.py:66
Sparse Core Ops, SparseCore 0:
  8.9 16.3 all-gather.2
where the time goes:
time: 129 us
  waiting for transfers between devices  47.7 us (37%)
  blocking collectives  29.3 us (23%)
  matrix products  17.1 us (13%)
  between operations  13.5 us (10%)
  starting transfers between devices  11.6 us (9%)
  local copies, waits for them, and re-layouts  4.96 us (4%)
  other arithmetic  4.86 us (4%)
    all_to_all x1, waiting for transfers between devices, per_device(): lax.all_to_all(send_rows, 'region', split_axis=0, concat_axis=0, tiled=True)  43.7 us
    all_to_all x1, blocking collectives, per_device(): lax.all_to_all(packed, 'region', split_axis=0, concat_axis=0, tiled=True)  29.3 us
    all_to_all x1, starting transfers between devices, per_device(): lax.all_to_all(send_blocks, 'region', split_axis=0, concat_axis=0, tiled=...  7.25 us
    dot_general x1, matrix products, score_against(): jnp.einsum('nd,md->nm', flat_rows, centre_rows, preferred_element_type=jn...  7.01 us
    dot_general x1, matrix products, pick_blocks(): jnp.einsum('rjb,rbk->rjk', chooser, blocked, precision=lax.Precision.HIGH...  5.41 us
    all_to_all x1, starting transfers between devices, per_device(): lax.all_to_all(send_rows, 'region', split_axis=0, concat_axis=0, tiled=True)  4.33 us
    all_to_all x1, waiting for transfers between devices, per_device(): lax.all_to_all(send_blocks, 'region', split_axis=0, concat_axis=0, tiled=...  3.27 us
    reduce_sum x1, other arithmetic, score_against(): sq_norm = jnp.sum(widened * widened, axis=1)  3.07 us
  transfers between devices with their start and end apart: 3, of which 2 were waited for; matrix products, arithmetic and copies ran while one was open for 8% of the time, Pallas kernels for 0%

commit v1 on v0

--- a/solution.py
+++ b/solution.py
@@ -1,8 +1,11 @@
+import functools
 import math
 
 import jax
 import jax.numpy as jnp
 from jax import lax
+from jax.experimental import pallas as pl
+from jax.experimental.pallas import tpu as pltpu
 from jax.sharding import PartitionSpec as P
 
 BLK = 128
@@ -27,7 +30,7 @@
     return selected.reshape(row_count, -1)
 
 
-def per_device(queries, probes, fine_blocks, centroids):
+def by_slots(queries, probes, fine_blocks, centroids):
     q_count, probe_count = probes.shape
     n_active = fine_blocks.shape[2]
     width = queries.shape[1]
@@ -62,7 +65,6 @@
     ).astype(jnp.int32)
     send_blocks = send_blocks.reshape(regions, capacity, n_active)
     local_centres = centroids[0]
-    block_len = BLK
     in_rows = lax.all_to_all(send_rows, "region", split_axis=0, concat_axis=0, tiled=True)
     in_blocks = lax.all_to_all(send_blocks, "region", split_axis=0, concat_axis=0, tiled=True)
     sender_count = in_rows.shape[0]
@@ -70,14 +72,201 @@
     flat_rows = in_rows.reshape(sender_count * item_count, width)
     flat_blocks = in_blocks.reshape(sender_count * item_count, n_active)
     scored = score_against(flat_rows, lax.all_gather(local_centres, "narrow", axis=0, tiled=True))
-    packed = pick_blocks(scored, flat_blocks, block_len).astype(jnp.bfloat16)
-    packed = packed.reshape(sender_count, item_count, n_active * block_len)
+    packed = pick_blocks(scored, flat_blocks, BLK).astype(jnp.bfloat16)
+    packed = packed.reshape(sender_count, item_count, n_active * BLK)
     returned_all = lax.all_to_all(packed, "region", split_axis=0, concat_axis=0, tiled=True)
     flat_returned = returned_all.reshape(regions * capacity, -1)
     answers = jnp.dot(
         slot_match.T.astype(jnp.bfloat16), flat_returned, preferred_element_type=jnp.float32
     ).astype(jnp.bfloat16)
     return answers.reshape(q_count, probe_count, -1)
+
+
+def choose(options, index):
+    bit = 1
+    while len(options) > 1:
+        odd = (index & bit) != 0
+        options = [
+            jnp.where(odd, options[i + 1], options[i]) for i in range(0, len(options), 2)
+        ]
+        bit *= 2
+    return options[0]
+
+
+def score_kernel(
+    n_sets, q_count, probe_count, n_active, scale, where_ref, *refs
+):
+    q_refs, meta_refs = refs[:n_sets], refs[n_sets : 2 * n_sets]
+    own_ref, other_ref, own_bias_ref, other_bias_ref = refs[2 * n_sets : 2 * n_sets + 4]
+    out_refs = refs[2 * n_sets + 4 : 3 * n_sets + 4]
+    held = refs[3 * n_sets + 4]
+    step = pl.program_id(0)
+    rows = jnp.concatenate([r[...] for r in q_refs], axis=0)
+    for side, (c_ref, b_ref) in enumerate(((own_ref, own_bias_ref), (other_ref, other_bias_ref))):
+        inner = lax.dot_general(
+            rows, c_ref[...], (((1,), (1,)), ((), ())), preferred_element_type=jnp.float32
+        )
+        held[side, step] = inner + b_ref[...]
+
+    @pl.when(step == pl.num_programs(0) - 1)
+    def _():
+        region = where_ref[0].astype(jnp.float32)
+        side_bit = where_ref[1] * (2 * held.shape[1] * held.shape[3] // BLK // 2)
+        blocks = [
+            (side, t, h)
+            for side in range(2)
+            for t in range(held.shape[1])
+            for h in range(held.shape[3] // BLK)
+        ]
+        for s in range(n_sets):
+            meta = meta_refs[s][...].astype(jnp.float32)
+            wanted = jnp.zeros((n_active, q_count), jnp.float32)
+            for p in range(probe_count):
+                fine = meta[probe_count + p * n_active : probe_count + (p + 1) * n_active]
+                wanted = wanted + jnp.where(meta[p : p + 1] == region, fine, 0.0)
+            wanted = jnp.concatenate(
+                [wanted, jnp.zeros((q_count - n_active, q_count), jnp.float32)], axis=0
+            )
+            columns = jnp.transpose(wanted).astype(jnp.int32) ^ side_bit
+            step_rows = 32
+            for r in range(0, q_count, step_rows):
+                options = [
+                    held[
+                        side,
+                        t,
+                        s * q_count + r : s * q_count + r + step_rows,
+                        h * BLK : (h + 1) * BLK,
+                    ]
+                    for side, t, h in blocks
+                ]
+                for j in range(n_active):
+                    best = choose(options, columns[r : r + step_rows, j : j + 1])
+                    out_refs[s][r : r + step_rows, j * BLK : (j + 1) * BLK] = (
+                        best * scale
+                    ).astype(jnp.bfloat16)
+
+
+def score(where, blocks, metas, own, other, own_bias, other_bias, probe_count, n_active):
+    n_sets = len(blocks)
+    q_count, width = blocks[0].shape
+    half = own.shape[0]
+    tile = 256
+    tiles = half // tile
+    whole = lambda a: pl.BlockSpec(a.shape, lambda t, w: (0,) * a.ndim)
+    out = jax.ShapeDtypeStruct((q_count, n_active * BLK), jnp.bfloat16)
+    return pl.pallas_call(
+        functools.partial(
+            score_kernel, n_sets, q_count, probe_count, n_active, 1.0 / math.sqrt(width)
+        ),
+        out_shape=[out] * n_sets,
+        grid_spec=pltpu.PrefetchScalarGridSpec(
+            num_scalar_prefetch=1,
+            grid=(tiles,),
+            in_specs=[whole(b) for b in blocks]
+            + [whole(m) for m in metas]
+            + [pl.BlockSpec((tile, width), lambda t, w: (t, 0))] * 2
+            + [pl.BlockSpec((1, tile), lambda t, w: (0, t))] * 2,
+            out_specs=[whole(out)] * n_sets,
+            scratch_shapes=[pltpu.VMEM((2, tiles, n_sets * q_count, tile), jnp.float32)],
+        ),
+        compiler_params=pltpu.CompilerParams(vmem_limit_bytes=24 * 1024 * 1024),
+        cost_estimate=pl.CostEstimate(
+            flops=2 * n_sets * q_count * 2 * half * width,
+            bytes_accessed=2 * half * width * 2 + n_sets * q_count * (width + n_active * BLK) * 2,
+            transcendentals=0,
+        ),
+        name="score",
+    )(where, *blocks, *metas, own, other, own_bias, other_bias)
+
+
+def answer_kernel(probe_count, regions, where_ref, probes_ref, *refs):
+    part_refs, out_ref = refs[:regions], refs[regions]
+    q_count = probes_ref.shape[0]
+    step_rows = 16
+    for r in range(0, q_count, step_rows):
+        offset = probes_ref[r : r + step_rows, :] ^ where_ref[0]
+        options = [p[r : r + step_rows, :].astype(jnp.float32) for p in part_refs]
+        for p in range(probe_count):
+            best = choose(options, offset[:, p : p + 1])
+            out_ref[r : r + step_rows, p, :] = best.astype(jnp.bfloat16)
+
+
+def answer(where, probes, parts):
+    q_count, probe_count = probes.shape
+    length = parts[0].shape[1]
+    return pl.pallas_call(
+        functools.partial(answer_kernel, probe_count, len(parts)),
+        out_shape=jax.ShapeDtypeStruct((q_count, probe_count, length), jnp.bfloat16),
+        in_specs=[pl.BlockSpec(memory_space=pltpu.SMEM)]
+        + [pl.BlockSpec(memory_space=pltpu.VMEM)] * (1 + len(parts)),
+        out_specs=pl.BlockSpec(memory_space=pltpu.VMEM),
+        compiler_params=pltpu.CompilerParams(vmem_limit_bytes=24 * 1024 * 1024),
+        name="answer",
+    )(where, probes, *parts)
+
+
+def by_blocks(queries, probes, fine_blocks, centroids):
+    q_count, probe_count = probes.shape
+    n_active = fine_blocks.shape[2]
+    width = queries.shape[1]
+    regions = lax.axis_size("region")
+
+    def hop(value, mask):
+        return lax.ppermute(value, "region", [(r, r ^ mask) for r in range(regions)])
+
+    region = lax.axis_index("region")
+    side = lax.axis_index("narrow")
+    where = jnp.stack([region, side]).astype(jnp.int32)
+    own = centroids[0]
+    held = {0: queries}
+    held[4] = hop(queries, 4)
+    held[2] = hop(queries, 2)
+    held[1] = hop(queries, 1)
+    ids = jnp.concatenate([probes, fine_blocks.reshape(q_count, -1)], axis=1)
+    ids = jnp.pad(ids.T.astype(jnp.bfloat16), ((0, -ids.shape[1] % 16), (0, 0)))
+    ids_4 = hop(ids, 4)
+    half_ids = jnp.stack([ids, ids_4])
+    ids_2 = hop(half_ids, 2)
+    most_ids = jnp.concatenate([half_ids, ids_2])
+    ids_1 = hop(most_ids, 1)
+    all_ids = dict(zip((0, 4, 2, 6, 1, 5, 3, 7), [*most_ids, *ids_1]))
+    other = lax.ppermute(own, "narrow", [(0, 1), (1, 0)])
+    factor = -0.5 / math.sqrt(width)
+    bias = lambda c: (factor * jnp.sum(jnp.square(c.astype(jnp.float32)), axis=1))[None, :]
+    own_bias, other_bias = bias(own), bias(other)
+    scored = lambda *keys: dict(
+        zip(
+            keys,
+            score(
+                where,
+                [held[k] for k in keys],
+                [all_ids[k] for k in keys],
+                own,
+                other,
+                own_bias,
+                other_bias,
+                probe_count,
+                n_active,
+            ),
+        )
+    )
+    held[6] = hop(held[4], 2)
+    held[5] = hop(held[4], 1)
+    held[3] = hop(held[1], 2)
+    held[7] = hop(held[6], 1)
+    results = {}
+    for keys in ((0, 4), (5, 6), (1, 2), (3, 7)):
+        results.update(scored(*keys))
+    parts = [results[0]] + [hop(results[k], k) for k in range(1, regions)]
+    return answer(where, probes, parts)
+
+
+def per_device(queries, probes, fine_blocks, centroids):
+    q_count, probe_count = probes.shape
+    regions = lax.axis_size("region")
+    if regions == 8 and lax.axis_size("narrow") == 2 and 2 * probe_count >= regions:
+        return by_blocks(queries, probes, fine_blocks, centroids)
+    return by_slots(queries, probes, fine_blocks, centroids)
 
 
 def solution(mesh):

time: 129 us -> 79.7 us (0.62)
  blocking collectives: 29.3 us -> 0 us
  waiting for transfers between devices: 47.7 us -> 23.3 us
  Pallas kernels: 0 us -> 23.7 us
  matrix products: 17.1 us -> 0 us
  starting transfers between devices: 11.6 us -> 26.2 us
  between operations: 13.5 us -> 0.09 us
  local copies, waits for them, and re-layouts: 4.96 us -> 0.14 us
    all_to_all x2 -> x0, waiting for transfers between devices: 47 us -> none  [the longest x1 43.7 us: per_device(): lax.all_to_all(send_rows, 'region', split_axis=0, concat_axis=0, tiled=True)]
    all_to_all x1 -> x0, blocking collectives: 29.3 us -> none  [per_device(): lax.all_to_all(packed, 'region', split_axis=0, concat_axis=0, tiled=True)]
    ppermute x0 -> x18, starting transfers between devices: none -> 26.2 us  [the longest x17 25.8 us: hop(): lax.ppermute(value, 'region', [(r, r ^ mask) for r in range(regions)])]
    pallas_call x0 -> x5, Pallas kernels: none -> 23.7 us  [the longest x4 21.6 us: score(): pl.pallas_call(functools.partial(score_kernel, n_sets, q_count, probe_cou...]
    ppermute x0 -> x18, waiting for transfers between devices: none -> 23.3 us  [the longest x17 23.3 us: hop(): lax.ppermute(value, 'region', [(r, r ^ mask) for r in range(regions)])]
    dot_general x6 -> x0, matrix products: 17.1 us -> none  [the longest x1 7.01 us: score_against(): jnp.einsum('nd,md->nm', flat_rows, centre_rows, preferred_element_type=jn...]
    all_to_all x2 -> x0, starting transfers between devices: 11.6 us -> none  [the longest x1 7.25 us: per_device(): lax.all_to_all(send_blocks, 'region', split_axis=0, concat_axis=0, tiled=...]
    unnamed x4 -> x7, local copies, waits for them, and re-layouts: 2.8 us -> 0.12 us
  transfers between devices with their start and end apart: 3 -> 18, of which waited for: 2 -> 8; matrix products, arithmetic and copies ran while one was open for 8% -> 8% of each run, Pallas kernels for 0% -> 27%
where the time goes in v1:
time: 79.7 us; the launch traced here: 79.3 us
  starting transfers between devices  26.2 us (33%)
  Pallas kernels  23.7 us (30%)
  waiting for transfers between devices  23.3 us (29%)
  other arithmetic  5.82 us (7%)
    ppermute x17, starting transfers between devices, hop(): lax.ppermute(value, 'region', [(r, r ^ mask) for r in range(regions)])  25.8 us
    ppermute x17, waiting for transfers between devices, hop(): lax.ppermute(value, 'region', [(r, r ^ mask) for r in range(regions)])  23.3 us
    pallas_call x4, Pallas kernels, score(): pl.pallas_call(functools.partial(score_kernel, n_sets, q_count, probe_cou...  21.6 us
    reduce_sum x2, other arithmetic, by_blocks(): jnp.sum(jnp.square(c.astype(jnp.float32)), axis=1)  4.34 us
    pallas_call x1, Pallas kernels, answer(): pl.pallas_call(functools.partial(answer_kernel, probe_count, len(parts)),...  2.12 us
  transfers between devices with their start and end apart: 18, of which 8 were waited for; matrix products, arithmetic and copies ran while one was open for 8% of the time, Pallas kernels for 27%

profile of v1, /device:TPU:0, one launch (start us, length us, event | category | flops | bytes accessed | tf_op | source)
XLA Modules:
  0.0 79.3 jit_solution(5894901134958893440)
XLA Ops:
  0.5 3.6 %collective-permute-start = (bf16[128,1024]{1,0:T(8,128)(2,1)}, bf16[128,1024]{1,0:T(8,128)(2,1)S(1)}, u32[]{:S(2)}, u32[]{:S(2)}) collective-permute-start(bf16[128,1024]{1,0:T(8,128)(2,1)} %refs_0_.1), channel_id=1, source_target_pairs={{0,8},{2,10},{4,12},{6,14},{8,0},{10,2},{12,4},{14,6},{1,9},{3,11}... | collective-permute-start | bytes 786440 | tf_op jit(solution)/shard_map/ppermute | solution.py:215
  4.0 1.5 %collective-permute-start.3 = (bf16[128,1024]{1,0:T(8,128)(2,1)}, bf16[128,1024]{1,0:T(8,128)(2,1)S(1)}, u32[]{:S(2)}, u32[]{:S(2)}) collective-permute-start(bf16[128,1024]{1,0:T(8,128)(2,1)} %refs_0_.1), channel_id=1, source_target_pairs={{0,2},{2,0},{4,6},{6,4},{8,10},{10,8},{12,14},{14,12},{1,3},{3,1},... | collective-permute-start | bytes 786440 | tf_op jit(solution)/shard_map/ppermute | solution.py:215
  5.5 1.6 %collective-permute-start.4 = (bf16[128,1024]{1,0:T(8,128)(2,1)}, bf16[128,1024]{1,0:T(8,128)(2,1)S(1)}, u32[]{:S(2)}, u32[]{:S(2)}) collective-permute-start(bf16[128,1024]{1,0:T(8,128)(2,1)} %refs_0_.1), channel_id=1, source_target_pairs={{0,4},{2,6},{4,0},{6,2},{8,12},{10,14},{12,8},{14,10},{1,5},{3,7},... | collective-permute-start | bytes 786440 | tf_op jit(solution)/shard_map/ppermute | solution.py:215
  8.9 2.3 %multiply_reduce_fusion.1 = f32[1024]{0:T(1024)S(1)} fusion(bf16[1,1024,1024]{2,1,0:T(8,128)(2,1)} %param.7), kind=kLoop, calls=%fused_computation.1 | loop fusion | flops 3144704 | bytes 2101248 | tf_op jit(solution)/shard_map/reduce_sum | solution.py:235
  11.2 5.9 %collective-permute-done.1.refs_3_ = bf16[32,128]{1,0:T(8,128)(2,1)S(1)} collective-permute-done((bf16[32,128]{1,0:T(8,128)(2,1)S(1)}, bf16[32,128]{1,0:T(8,128)(2,1)S(1)}, u32[]{:S(2)}, u32[]{:S(2)}) %collective-permute-start.1) | collective-permute-done | bytes 8224 | tf_op jit(solution)/shard_map/ppermute | solution.py:215
  17.1 1.6 %collective-permute-start.5 = (bf16[2,32,128]{2,1,0:T(8,128)(2,1)S(1)}, bf16[2,32,128]{2,1,0:T(8,128)(2,1)S(1)}, u32[]{:S(2)}, u32[]{:S(2)}) collective-permute-start(bf16[2,32,128]{2,1,0:T(8,128)(2,1)S(1)} %pad_maximum_fusion.1), channel_id=1, source_target_pairs={{0,4},{2,6},{4,0},{6,2},{8,12},{10,14},{12,8},{14,10},{1,5},{3,7},... | collective-permute-start | bytes 49160 | tf_op jit(solution)/shard_map/ppermute | solution.py:215
  18.8 2.1 %collective-permute-done.5 = bf16[2,32,128]{2,1,0:T(8,128)(2,1)S(1)} collective-permute-done((bf16[2,32,128]{2,1,0:T(8,128)(2,1)S(1)}, bf16[2,32,128]{2,1,0:T(8,128)(2,1)S(1)}, u32[]{:S(2)}, u32[]{:S(2)}) %collective-permute-start.5) | collective-permute-done | bytes 16416 | tf_op jit(solution)/shard_map/ppermute | solution.py:215
  20.9 1.5 %collective-permute-start.6 = (bf16[4,32,128]{2,1,0:T(8,128)(2,1)S(1)}, bf16[4,32,128]{2,1,0:T(8,128)(2,1)S(1)}, u32[]{:S(2)}, u32[]{:S(2)}) collective-permute-start(bf16[4,32,128]{2,1,0:T(8,128)(2,1)S(1)} %pad_maximum_fusion), channel_id=1, source_target_pairs={{0,2},{2,0},{4,6},{6,4},{8,10},{10,8},{12,14},{14,12},{1,3},{3,1},... | collective-permute-start | bytes 98312 | tf_op jit(solution)/shard_map/ppermute | solution.py:215
  22.4 1.5 %collective-permute-start.10 = (bf16[128,1024]{1,0:T(8,128)(2,1)S(1)}, bf16[128,1024]{1,0:T(8,128)(2,1)S(1)}, u32[]{:S(2)}, u32[]{:S(2)}) collective-permute-start(bf16[128,1024]{1,0:T(8,128)(2,1)S(1)} %collective-permute-done.refs_1_), channel_id=1, source_target_pairs={{0,4},{2,6},{4,0},{6,2},{8,12},{10,14},{12,8},{14,10},{1,5},{3,7},... | collective-permute-start | bytes 786440 | tf_op jit(solution)/shard_map/ppermute | solution.py:215
  24.8 1.6 %collective-permute-start.14 = (bf16[128,1024]{1,0:T(8,128)(2,1)S(1)}, bf16[128,1024]{1,0:T(8,128)(2,1)S(1)}, u32[]{:S(2)}, u32[]{:S(2)}) collective-permute-start(bf16[128,1024]{1,0:T(8,128)(2,1)S(1)} %collective-permute-done.refs_1_), channel_id=1, source_target_pairs={{0,2},{2,0},{4,6},{6,4},{8,10},{10,8},{12,14},{14,12},{1,3},{3,1},... | collective-permute-start | bytes 786440 | tf_op jit(solution)/shard_map/ppermute | solution.py:215
  26.4 1.8 %collective-permute-start.9 = (bf16[128,1024]{1,0:T(8,128)(2,1)S(1)}, bf16[128,1024]{1,0:T(8,128)(2,1)S(1)}, u32[]{:S(2)}, u32[]{:S(2)}) collective-permute-start(bf16[128,1024]{1,0:T(8,128)(2,1)S(1)} %collective-permute-done.3.refs_0_), channel_id=1, source_target_pairs={{0,4},{2,6},{4,0},{6,2},{8,12},{10,14},{12,8},{14,10},{1,5},{3,7},... | collective-permute-start | bytes 786440 | tf_op jit(solution)/shard_map/ppermute | solution.py:215
  28.1 3.5 %collective-permute-done.10.refs_1_ = bf16[128,1024]{1,0:T(8,128)(2,1)S(1)} collective-permute-done((bf16[128,1024]{1,0:T(8,128)(2,1)S(1)}, bf16[128,1024]{1,0:T(8,128)(2,1)S(1)}, u32[]{:S(2)}, u32[]{:S(2)}) %collective-permute-start.10) | collective-permute-done | bytes 262176 | tf_op jit(solution)/shard_map/ppermute | solution.py:215
  32.2 2.1 %multiply_reduce_fusion = f32[1024]{0:T(1024)S(1)} fusion(bf16[1024,1024]{1,0:T(8,128)(2,1)} %collective-permute-done.2.refs_5_), kind=kLoop, calls=%fused_computation | loop fusion | flops 3144704 | bytes 2101248 | tf_op jit(solution)/shard_map/reduce_sum | solution.py:235
  34.5 3.6 %collective-permute-done.11.refs_1_ = bf16[128,1024]{1,0:T(8,128)(2,1)S(1)} collective-permute-done((bf16[128,1024]{1,0:T(8,128)(2,1)S(1)}, bf16[128,1024]{1,0:T(8,128)(2,1)S(1)}, u32[]{:S(2)}, u32[]{:S(2)}) %collective-permute-start.11) | collective-permute-done | bytes 262176 | tf_op jit(solution)/shard_map/ppermute | solution.py:215
  38.0 4.9 %score.6 = (bf16[128,512]{1,0:T(8,128)(2,1)S(1)}, bf16[128,512]{1,0:T(8,128)(2,1)S(1)}) custom-call(s32[2]{0:T(128)S(1)} %pad_add_fusion.where_ref, bf16[128,1024]{1,0:T(8,128)(2,1)S(1)} %collective-permute-done.9.refs_0_, bf16[128,1024]{1,0:T(8,128)(2,1)S(1)} %collective-permute-done.11.refs_1_, bf16[32,128]{1,0:T(8,128)(2,1)S(1)} %get-tuple-element.23.refs_2_, ...), custom_call_target="tpu_custom_call" | custom-call | flops 1073741824 | bytes 4980736 | tf_op jit(solution)/shard_map/score/pallas_call | solution.py:157
  44.3 3.7 %collective-permute-start.17 = (bf16[128,512]{1,0:T(8,128)(2,1)S(1)}, bf16[128,512]{1,0:T(8,128)(2,1)S(1)}, u32[]{:S(2)}, u32[]{:S(2)}) collective-permute-start(bf16[128,512]{1,0:T(8,128)(2,1)S(1)} %get-tuple-element.20), channel_id=1, source_target_pairs={{0,14},{2,12},{4,10},{6,8},{8,6},{10,4},{12,2},{14,0},{1,15},{3,13... | collective-permute-start | bytes 393224 | tf_op jit(solution)/shard_map/ppermute | solution.py:215
  48.0 5.6 %score.7 = (bf16[128,512]{1,0:T(8,128)(2,1)}, bf16[128,512]{1,0:T(8,128)(2,1)}) custom-call(s32[2]{0:T(128)S(1)} %pad_add_fusion.where_ref, bf16[128,1024]{1,0:T(8,128)(2,1)S(1)} %collective-permute-done.14.refs_0_, bf16[128,1024]{1,0:T(8,128)(2,1)S(1)} %collective-permute-done.10.refs_1_, bf16[32,128]{1,0:T(8,128)(2,1)S(1)} %get-tuple-element.21.refs_2_, ...), custom_call_target="tpu_custom_call" | custom-call | flops 1073741824 | bytes 4980736 | tf_op jit(solution)/shard_map/score/pallas_call | solution.py:157
  53.6 2.9 %collective-permute-start.16 = (bf16[128,512]{1,0:T(8,128)(2,1)}, bf16[128,512]{1,0:T(8,128)(2,1)S(1)}, u32[]{:S(2)}, u32[]{:S(2)}) collective-permute-start(bf16[128,512]{1,0:T(8,128)(2,1)} %get-tuple-element.19), channel_id=1, source_target_pairs={{0,12},{2,14},{4,8},{6,10},{8,4},{10,6},{12,0},{14,2},{1,13},{3,15... | collective-permute-start | bytes 393224 | tf_op jit(solution)/shard_map/ppermute | solution.py:215
  56.6 5.6 %score.5 = (bf16[128,512]{1,0:T(8,128)(2,1)}, bf16[128,512]{1,0:T(8,128)(2,1)}) custom-call(s32[2]{0:T(128)S(1)} %pad_add_fusion.where_ref, bf16[128,1024]{1,0:T(8,128)(2,1)S(1)} %collective-permute-done.3.refs_0_, bf16[128,1024]{1,0:T(8,128)(2,1)S(1)} %collective-permute-done.4.refs_1_, bf16[32,128]{1,0:T(8,128)(2,1)S(1)} %get-tuple-element.24.refs_2_, ...), custom_call_target="tpu_custom_call" | custom-call | flops 1073741824 | bytes 4980736 | tf_op jit(solution)/shard_map/score/pallas_call | solution.py:157
  62.2 1.4 %collective-permute-start.7 = (bf16[128,512]{1,0:T(8,128)(2,1)}, bf16[128,512]{1,0:T(8,128)(2,1)S(1)}, u32[]{:S(2)}, u32[]{:S(2)}) collective-permute-start(bf16[128,512]{1,0:T(8,128)(2,1)} %get-tuple-element.14), channel_id=1, source_target_pairs={{0,2},{2,0},{4,6},{6,4},{8,10},{10,8},{12,14},{14,12},{1,3},{3,1},... | collective-permute-start | bytes 393224 | tf_op jit(solution)/shard_map/ppermute | solution.py:215
  63.6 5.5 %score.4 = (bf16[128,512]{1,0:T(8,128)(2,1)S(1)}, bf16[128,512]{1,0:T(8,128)(2,1)}) custom-call(s32[2]{0:T(128)S(1)} %pad_add_fusion.where_ref, bf16[128,1024]{1,0:T(8,128)(2,1)S(1)} %copy-done.1, bf16[128,1024]{1,0:T(8,128)(2,1)S(1)} %collective-permute-done.refs_1_, bf16[32,128]{1,0:T(8,128)(2,1)S(1)} %get-tuple-element.28.refs_2_, ...), custom_call_target="tpu_custom_call" | custom-call | flops 1073741824 | bytes 4980736 | tf_op jit(solution)/shard_map/score/pallas_call | solution.py:157
  70.2 4.2 %collective-permute-done.8.refs_2_ = bf16[128,512]{1,0:T(8,128)(2,1)S(1)} collective-permute-done((bf16[128,512]{1,0:T(8,128)(2,1)}, bf16[128,512]{1,0:T(8,128)(2,1)S(1)}, u32[]{:S(2)}, u32[]{:S(2)}) %collective-permute-start.8) | collective-permute-done | bytes 131104 | tf_op jit(solution)/shard_map/ppermute | solution.py:215
  74.3 2.8 %collective-permute-done.13.refs_4_ = bf16[128,512]{1,0:T(8,128)(2,1)S(1)} collective-permute-done((bf16[128,512]{1,0:T(8,128)(2,1)}, bf16[128,512]{1,0:T(8,128)(2,1)S(1)}, u32[]{:S(2)}, u32[]{:S(2)}) %collective-permute-start.13) | collective-permute-done | bytes 131104 | tf_op jit(solution)/shard_map/ppermute | solution.py:215
  77.2 2.1 %answer.1 = bf16[128,4,512]{2,1,0:T(4,128)(2,1)} custom-call(s32[2]{0:T(128)S(1)} %pad_add_fusion.where_ref, s32[128,4]{1,0:T(8,128)S(1)} %copy.5.probes_ref, bf16[128,512]{1,0:T(8,128)(2,1)S(1)} %get-tuple-element.13.refs_0_, bf16[128,512]{1,0:T(8,128)(2,1)S(1)} %collective-permute-done.7.refs_1_, bf16[128,512]{1,0:T(8,128)(2,1)S(1)} %collective-permute-done.8.refs_2_, ...), custom_call_target="tpu_custom_call" | custom-call | tf_op jit(solution)/shard_map/answer/pallas_call | solution.py:197
  (37 shorter events, 6.3 us)
Async XLA Ops:
  0.0 32.2 %collective-permute-start.2 = (bf16[1024,1024]{1,0:T(8,128)(2,1)}, bf16[1024,1024]{1,0:T(8,128)(2,1)}, u32[]{:S(2)}, u32[]{:S(2)}) collective-permute-start(bf16[1024,1024]{1,0:T(8,128)(2,1)} %bitcast.24), channel_id=1, source_target_pairs={{0,1},{1,0},{2,3},{3,2},{4,5},{5,4},{6,7},{7,6},{8,9},{9,8},{10,11... | collective-permute-start | bytes 6291464 | tf_op jit(solution)/shard_map/ppermute | solution.py:233
  0.5 22.0 %collective-permute-start = (bf16[128,1024]{1,0:T(8,128)(2,1)}, bf16[128,1024]{1,0:T(8,128)(2,1)S(1)}, u32[]{:S(2)}, u32[]{:S(2)}) collective-permute-start(bf16[128,1024]{1,0:T(8,128)(2,1)} %refs_0_.1), channel_id=1, source_target_pairs={{0,8},{2,10},{4,12},{6,14},{8,0},{10,2},{12,4},{14,6},{1,9},{3,11}... | collective-permute-start | bytes 786440 | tf_op jit(solution)/shard_map/ppermute | solution.py:215
  4.0 22.3 %collective-permute-start.3 = (bf16[128,1024]{1,0:T(8,128)(2,1)}, bf16[128,1024]{1,0:T(8,128)(2,1)S(1)}, u32[]{:S(2)}, u32[]{:S(2)}) collective-permute-start(bf16[128,1024]{1,0:T(8,128)(2,1)} %refs_0_.1), channel_id=1, source_target_pairs={{0,2},{2,0},{4,6},{6,4},{8,10},{10,8},{12,14},{14,12},{1,3},{3,1},... | collective-permute-start | bytes 786440 | tf_op jit(solution)/shard_map/ppermute | solution.py:215
  5.5 51.0 %collective-permute-start.4 = (bf16[128,1024]{1,0:T(8,128)(2,1)}, bf16[128,1024]{1,0:T(8,128)(2,1)S(1)}, u32[]{:S(2)}, u32[]{:S(2)}) collective-permute-start(bf16[128,1024]{1,0:T(8,128)(2,1)} %refs_0_.1), channel_id=1, source_target_pairs={{0,4},{2,6},{4,0},{6,2},{8,12},{10,14},{12,8},{14,10},{1,5},{3,7},... | collective-permute-start | bytes 786440 | tf_op jit(solution)/shard_map/ppermute | solution.py:215
  8.5 29.5 %copy-start = (bf16[1,1024,1024]{2,1,0:T(8,128)(2,1)S(1)}, bf16[1,1024,1024]{2,1,0:T(8,128)(2,1)}, u32[]{:S(2)}) copy-start(bf16[1,1024,1024]{2,1,0:T(8,128)(2,1)} %param.7) | copy-start | bytes 6291460
  8.5 8.6 %collective-permute-start.1 = (bf16[32,128]{1,0:T(8,128)(2,1)S(1)}, bf16[32,128]{1,0:T(8,128)(2,1)S(1)}, u32[]{:S(2)}, u32[]{:S(2)}) collective-permute-start(bf16[32,128]{1,0:T(8,128)(2,1)S(1)} %get-tuple-element.28.refs_2_), channel_id=1, source_target_pairs={{0,8},{2,10},{4,12},{6,14},{8,0},{10,2},{12,4},{14,6},{1,9},{3,11}... | collective-permute-start | bytes 24584 | tf_op jit(solution)/shard_map/ppermute | solution.py:215
  17.1 3.7 %collective-permute-start.5 = (bf16[2,32,128]{2,1,0:T(8,128)(2,1)S(1)}, bf16[2,32,128]{2,1,0:T(8,128)(2,1)S(1)}, u32[]{:S(2)}, u32[]{:S(2)}) collective-permute-start(bf16[2,32,128]{2,1,0:T(8,128)(2,1)S(1)} %pad_maximum_fusion.1), channel_id=1, source_target_pairs={{0,4},{2,6},{4,0},{6,2},{8,12},{10,14},{12,8},{14,10},{1,5},{3,7},... | collective-permute-start | bytes 49160 | tf_op jit(solution)/shard_map/ppermute | solution.py:215
  20.9 3.9 %collective-permute-start.6 = (bf16[4,32,128]{2,1,0:T(8,128)(2,1)S(1)}, bf16[4,32,128]{2,1,0:T(8,128)(2,1)S(1)}, u32[]{:S(2)}, u32[]{:S(2)}) collective-permute-start(bf16[4,32,128]{2,1,0:T(8,128)(2,1)S(1)} %pad_maximum_fusion), channel_id=1, source_target_pairs={{0,2},{2,0},{4,6},{6,4},{8,10},{10,8},{12,14},{14,12},{1,3},{3,1},... | collective-permute-start | bytes 98312 | tf_op jit(solution)/shard_map/ppermute | solution.py:215
  22.4 9.2 %collective-permute-start.10 = (bf16[128,1024]{1,0:T(8,128)(2,1)S(1)}, bf16[128,1024]{1,0:T(8,128)(2,1)S(1)}, u32[]{:S(2)}, u32[]{:S(2)}) collective-permute-start(bf16[128,1024]{1,0:T(8,128)(2,1)S(1)} %collective-permute-done.refs_1_), channel_id=1, source_target_pairs={{0,4},{2,6},{4,0},{6,2},{8,12},{10,14},{12,8},{14,10},{1,5},{3,7},... | collective-permute-start | bytes 786440 | tf_op jit(solution)/shard_map/ppermute | solution.py:215
  24.8 23.2 %collective-permute-start.14 = (bf16[128,1024]{1,0:T(8,128)(2,1)S(1)}, bf16[128,1024]{1,0:T(8,128)(2,1)S(1)}, u32[]{:S(2)}, u32[]{:S(2)}) collective-permute-start(bf16[128,1024]{1,0:T(8,128)(2,1)S(1)} %collective-permute-done.refs_1_), channel_id=1, source_target_pairs={{0,2},{2,0},{4,6},{6,4},{8,10},{10,8},{12,14},{14,12},{1,3},{3,1},... | collective-permute-start | bytes 786440 | tf_op jit(solution)/shard_map/ppermute | solution.py:215
  26.4 8.1 %collective-permute-start.9 = (bf16[128,1024]{1,0:T(8,128)(2,1)S(1)}, bf16[128,1024]{1,0:T(8,128)(2,1)S(1)}, u32[]{:S(2)}, u32[]{:S(2)}) collective-permute-start(bf16[128,1024]{1,0:T(8,128)(2,1)S(1)} %collective-permute-done.3.refs_0_), channel_id=1, source_target_pairs={{0,4},{2,6},{4,0},{6,2},{8,12},{10,14},{12,8},{14,10},{1,5},{3,7},... | collective-permute-start | bytes 786440 | tf_op jit(solution)/shard_map/ppermute | solution.py:215
  31.7 6.4 %collective-permute-start.11 = (bf16[128,1024]{1,0:T(8,128)(2,1)S(1)}, bf16[128,1024]{1,0:T(8,128)(2,1)S(1)}, u32[]{:S(2)}, u32[]{:S(2)}) collective-permute-start(bf16[128,1024]{1,0:T(8,128)(2,1)S(1)} %collective-permute-done.10.refs_1_), channel_id=1, source_target_pairs={{0,2},{2,0},{4,6},{6,4},{8,10},{10,8},{12,14},{14,12},{1,3},{3,1},... | collective-permute-start | bytes 786440 | tf_op jit(solution)/shard_map/ppermute | solution.py:215
  42.9 26.2 %collective-permute-start.12 = (bf16[128,512]{1,0:T(8,128)(2,1)S(1)}, bf16[128,512]{1,0:T(8,128)(2,1)S(1)}, u32[]{:S(2)}, u32[]{:S(2)}) collective-permute-start(bf16[128,512]{1,0:T(8,128)(2,1)S(1)} %get-tuple-element.16), channel_id=1, source_target_pairs={{0,6},{2,4},{4,2},{6,0},{8,14},{10,12},{12,10},{14,8},{1,7},{3,5},... | collective-permute-start | bytes 393224 | tf_op jit(solution)/shard_map/ppermute | solution.py:215
  44.3 25.4 %collective-permute-start.17 = (bf16[128,512]{1,0:T(8,128)(2,1)S(1)}, bf16[128,512]{1,0:T(8,128)(2,1)S(1)}, u32[]{:S(2)}, u32[]{:S(2)}) collective-permute-start(bf16[128,512]{1,0:T(8,128)(2,1)S(1)} %get-tuple-element.20), channel_id=1, source_target_pairs={{0,14},{2,12},{4,10},{6,8},{8,6},{10,4},{12,2},{14,0},{1,15},{3,13... | collective-permute-start | bytes 393224 | tf_op jit(solution)/shard_map/ppermute | solution.py:215
  53.6 16.5 %collective-permute-start.15 = (bf16[128,512]{1,0:T(8,128)(2,1)}, bf16[128,512]{1,0:T(8,128)(2,1)S(1)}, u32[]{:S(2)}, u32[]{:S(2)}) collective-permute-start(bf16[128,512]{1,0:T(8,128)(2,1)} %get-tuple-element.18), channel_id=1, source_target_pairs={{0,10},{2,8},{4,14},{6,12},{8,2},{10,0},{12,6},{14,4},{1,11},{3,9}... | collective-permute-start | bytes 393224 | tf_op jit(solution)/shard_map/ppermute | solution.py:215
  53.6 16.5 %collective-permute-start.16 = (bf16[128,512]{1,0:T(8,128)(2,1)}, bf16[128,512]{1,0:T(8,128)(2,1)S(1)}, u32[]{:S(2)}, u32[]{:S(2)}) collective-permute-start(bf16[128,512]{1,0:T(8,128)(2,1)} %get-tuple-element.19), channel_id=1, source_target_pairs={{0,12},{2,14},{4,8},{6,10},{8,4},{10,6},{12,0},{14,2},{1,13},{3,15... | collective-permute-start | bytes 393224 | tf_op jit(solution)/shard_map/ppermute | solution.py:215
  56.6 7.0 %copy-start.1 = (bf16[128,1024]{1,0:T(8,128)(2,1)S(1)}, bf16[128,1024]{1,0:T(8,128)(2,1)}, u32[]{:S(2)}) copy-start(bf16[128,1024]{1,0:T(8,128)(2,1)} %refs_0_.1) | copy-start | bytes 786436
  62.2 7.8 %copy-start.2 = (s32[128,4]{0,1:T(4,128)S(1)}, s32[128,4]{0,1:T(4,128)}, u32[]{:S(2)}) copy-start(s32[128,4]{0,1:T(4,128)} %param.5) | copy-start | bytes 6148
  62.2 8.0 %collective-permute-start.7 = (bf16[128,512]{1,0:T(8,128)(2,1)}, bf16[128,512]{1,0:T(8,128)(2,1)S(1)}, u32[]{:S(2)}, u32[]{:S(2)}) collective-permute-start(bf16[128,512]{1,0:T(8,128)(2,1)} %get-tuple-element.14), channel_id=1, source_target_pairs={{0,2},{2,0},{4,6},{6,4},{8,10},{10,8},{12,14},{14,12},{1,3},{3,1},... | collective-permute-start | bytes 393224 | tf_op jit(solution)/shard_map/ppermute | solution.py:215
  69.2 5.2 %collective-permute-start.8 = (bf16[128,512]{1,0:T(8,128)(2,1)}, bf16[128,512]{1,0:T(8,128)(2,1)S(1)}, u32[]{:S(2)}, u32[]{:S(2)}) collective-permute-start(bf16[128,512]{1,0:T(8,128)(2,1)} %get-tuple-element.15), channel_id=1, source_target_pairs={{0,4},{2,6},{4,0},{6,2},{8,12},{10,14},{12,8},{14,10},{1,5},{3,7},... | collective-permute-start | bytes 393224 | tf_op jit(solution)/shard_map/ppermute | solution.py:215
  69.7 7.5 %collective-permute-start.13 = (bf16[128,512]{1,0:T(8,128)(2,1)}, bf16[128,512]{1,0:T(8,128)(2,1)S(1)}, u32[]{:S(2)}, u32[]{:S(2)}) collective-permute-start(bf16[128,512]{1,0:T(8,128)(2,1)} %get-tuple-element.17), channel_id=1, source_target_pairs={{0,8},{2,10},{4,12},{6,14},{8,0},{10,2},{12,4},{14,6},{1,9},{3,11}... | collective-permute-start | bytes 393224 | tf_op jit(solution)/shard_map/ppermute | solution.py:215

commit v2 on v0

--- a/solution.py
+++ b/solution.py
@@ -1,11 +1,18 @@
+import functools
 import math
 
 import jax
 import jax.numpy as jnp
 from jax import lax
+from jax.experimental import pallas as pl
+from jax.experimental.pallas import tpu as pltpu
 from jax.sharding import PartitionSpec as P
 
 BLK = 128
+W01 = 1
+W42 = 1
+W56 = 10
+W73 = 1
 
 
 def score_against(flat_rows, centre_rows):
@@ -27,7 +34,7 @@
     return selected.reshape(row_count, -1)
 
 
-def per_device(queries, probes, fine_blocks, centroids):
+def by_slots(queries, probes, fine_blocks, centroids):
     q_count, probe_count = probes.shape
     n_active = fine_blocks.shape[2]
     width = queries.shape[1]
@@ -62,7 +69,6 @@
     ).astype(jnp.int32)
     send_blocks = send_blocks.reshape(regions, capacity, n_active)
     local_centres = centroids[0]
-    block_len = BLK
     in_rows = lax.all_to_all(send_rows, "region", split_axis=0, concat_axis=0, tiled=True)
     in_blocks = lax.all_to_all(send_blocks, "region", split_axis=0, concat_axis=0, tiled=True)
     sender_count = in_rows.shape[0]
@@ -70,14 +76,282 @@
     flat_rows = in_rows.reshape(sender_count * item_count, width)
     flat_blocks = in_blocks.reshape(sender_count * item_count, n_active)
     scored = score_against(flat_rows, lax.all_gather(local_centres, "narrow", axis=0, tiled=True))
-    packed = pick_blocks(scored, flat_blocks, block_len).astype(jnp.bfloat16)
-    packed = packed.reshape(sender_count, item_count, n_active * block_len)
+    packed = pick_blocks(scored, flat_blocks, BLK).astype(jnp.bfloat16)
+    packed = packed.reshape(sender_count, item_count, n_active * BLK)
     returned_all = lax.all_to_all(packed, "region", split_axis=0, concat_axis=0, tiled=True)
     flat_returned = returned_all.reshape(regions * capacity, -1)
     answers = jnp.dot(
         slot_match.T.astype(jnp.bfloat16), flat_returned, preferred_element_type=jnp.float32
     ).astype(jnp.bfloat16)
     return answers.reshape(q_count, probe_count, -1)
+
+
+def choose(options, index):
+    bit = 1
+    while len(options) > 1:
+        odd = (index & bit) != 0
+        options = [
+            jnp.where(odd, options[i + 1], options[i]) for i in range(0, len(options), 2)
+        ]
+        bit *= 2
+    return options[0]
+
+
+def pack_kernel(queries_ref, ids_ref, out_ref):
+    q_count = queries_ref.shape[0]
+    extra = out_ref.shape[0] - q_count
+    out_ref[0:q_count, :] = queries_ref[...]
+    ids = ids_ref[...].astype(jnp.float32)
+    tiles = [ids[i : i + extra] for i in range(0, ids.shape[0], extra)]
+    tiles.append(jnp.zeros((extra, queries_ref.shape[1] - len(tiles) * q_count), jnp.float32))
+    out_ref[q_count:, :] = jnp.concatenate(tiles, axis=1).astype(jnp.bfloat16)
+
+
+def pack(queries, ids, extra):
+    q_count, width = queries.shape
+    in_vmem = pl.BlockSpec(memory_space=pltpu.VMEM)
+    return pl.pallas_call(
+        pack_kernel,
+        out_shape=jax.ShapeDtypeStruct((q_count + extra, width), jnp.bfloat16),
+        in_specs=[in_vmem] * 2,
+        out_specs=in_vmem,
+        compiler_params=pltpu.CompilerParams(vmem_limit_bytes=24 * 1024 * 1024),
+        name="pack",
+    )(queries, ids)
+
+
+def list_ids_kernel(probes_ref, fine_ref, out_ref):
+    ids = jnp.concatenate([probes_ref[...], fine_ref[...]], axis=0).astype(jnp.float32)
+    spare = out_ref.shape[0] - ids.shape[0]
+    ids = jnp.concatenate([ids, jnp.zeros((spare, ids.shape[1]), jnp.float32)], axis=0)
+    out_ref[...] = ids.astype(jnp.bfloat16)
+
+
+def list_ids(probes, fine):
+    rows = probes.shape[0] + fine.shape[0]
+    in_vmem = pl.BlockSpec(memory_space=pltpu.VMEM)
+    return pl.pallas_call(
+        list_ids_kernel,
+        out_shape=jax.ShapeDtypeStruct((rows + -rows % 16, probes.shape[1]), jnp.bfloat16),
+        in_specs=[in_vmem] * 2,
+        out_specs=in_vmem,
+        compiler_params=pltpu.CompilerParams(vmem_limit_bytes=24 * 1024 * 1024),
+        name="list_ids",
+    )(probes, fine)
+
+
+def norms_kernel(scale, rows_ref, bias_ref, kept_ref=None):
+    count, width = rows_ref.shape
+    ones = jnp.ones((8, width), jnp.bfloat16)
+    chunk = 256
+    for t in range(0, count, chunk):
+        rows = rows_ref[t : t + chunk, :]
+        if kept_ref is not None:
+            kept_ref[t : t + chunk, :] = rows
+        square = jnp.square(rows.astype(jnp.float32))
+        high = square.astype(jnp.bfloat16)
+        low = (square - high.astype(jnp.float32)).astype(jnp.bfloat16)
+        total = jnp.zeros((8, chunk), jnp.float32)
+        for term in (high, low):
+            total = total + lax.dot_general(
+                ones, term, (((1,), (1,)), ((), ())), preferred_element_type=jnp.float32
+            )
+        bias_ref[:, t : t + chunk] = scale * total[0:1]
+
+
+def norms(rows, scale, keep):
+    in_vmem = pl.BlockSpec(memory_space=pltpu.VMEM)
+    shapes = [jax.ShapeDtypeStruct((1, rows.shape[0]), jnp.float32)]
+    if keep:
+        shapes.append(jax.ShapeDtypeStruct(rows.shape, rows.dtype))
+    return pl.pallas_call(
+        functools.partial(norms_kernel, scale),
+        out_shape=shapes,
+        in_specs=[in_vmem],
+        out_specs=[in_vmem] * len(shapes),
+        compiler_params=pltpu.CompilerParams(vmem_limit_bytes=24 * 1024 * 1024),
+        cost_estimate=pl.CostEstimate(
+            flops=4 * 10**9, bytes_accessed=2 * rows.size * len(shapes), transcendentals=0
+        ),
+        name="norms",
+    )(rows)
+
+
+def score_kernel(n_sets, q_count, probe_count, n_active, scale, where_ref, *refs):
+    q_refs = refs[:n_sets]
+    sides = ((refs[n_sets], refs[n_sets + 2]), (refs[n_sets + 1], refs[n_sets + 3]))
+    out_refs = refs[n_sets + 4 : 2 * n_sets + 4]
+    held = refs[2 * n_sets + 4]
+    half = sides[0][0].shape[0]
+    block_total = 2 * half // BLK
+    region = where_ref[0].astype(jnp.float32)
+    columns = []
+    for q_ref in q_refs:
+        extra = q_ref.shape[0] - q_count
+        tail = q_ref[...].astype(jnp.float32)[q_count:]
+        tiles = -(-probe_count * (n_active + 1) // extra)
+        meta = jnp.concatenate(
+            [tail[:, i * q_count : (i + 1) * q_count] for i in range(tiles)], axis=0
+        )
+        wanted = jnp.zeros((n_active, q_count), jnp.float32)
+        for p in range(probe_count):
+            fine = meta[probe_count + p * n_active : probe_count + (p + 1) * n_active]
+            wanted = wanted + jnp.where(meta[p : p + 1] == region, fine, 0.0)
+        wanted = jnp.concatenate(
+            [wanted, jnp.zeros((q_count - n_active, q_count), jnp.float32)], axis=0
+        )
+        columns.append(jnp.transpose(wanted).astype(jnp.int32) ^ (where_ref[1] * (block_total // 2)))
+    rows = jnp.concatenate([r[0:q_count, :] for r in q_refs], axis=0)
+    chunk = 512
+    for side, (c_ref, b_ref) in enumerate(sides):
+        for t in range(0, half, chunk):
+            inner = lax.dot_general(
+                rows,
+                c_ref[t : t + chunk, :],
+                (((1,), (1,)), ((), ())),
+                preferred_element_type=jnp.float32,
+            )
+            held[:, side * half + t : side * half + t + chunk] = inner + b_ref[:, t : t + chunk]
+    step = 32
+    for s in range(n_sets):
+        for r in range(0, q_count, step):
+            row = s * q_count + r
+            options = [held[row : row + step, b * BLK : (b + 1) * BLK] for b in range(block_total)]
+            for j in range(n_active):
+                best = choose(options, columns[s][r : r + step, j : j + 1])
+                out_refs[s][r : r + step, j * BLK : (j + 1) * BLK] = (best * scale).astype(
+                    jnp.bfloat16
+                )
+
+
+def score(where, blocks, own, other, own_bias, other_bias, q_count, probe_count, n_active, weight):
+    n_sets = len(blocks)
+    half, width = own.shape
+    in_vmem = pl.BlockSpec(memory_space=pltpu.VMEM)
+    out = jax.ShapeDtypeStruct((q_count, n_active * BLK), jnp.bfloat16)
+    return pl.pallas_call(
+        functools.partial(
+            score_kernel, n_sets, q_count, probe_count, n_active, 1.0 / math.sqrt(width)
+        ),
+        out_shape=[out] * n_sets,
+        in_specs=[pl.BlockSpec(memory_space=pltpu.SMEM)] + [in_vmem] * (n_sets + 4),
+        out_specs=[in_vmem] * n_sets,
+        scratch_shapes=[pltpu.VMEM((n_sets * q_count, 2 * half), jnp.float32)],
+        compiler_params=pltpu.CompilerParams(vmem_limit_bytes=24 * 1024 * 1024),
+        cost_estimate=pl.CostEstimate(
+            flops=weight * 2 * n_sets * q_count * 2 * half * width,
+            bytes_accessed=2 * half * width * 2 + n_sets * q_count * (width + n_active * BLK) * 2,
+            transcendentals=0,
+        ),
+        name="score",
+    )(where, *blocks, own, other, own_bias, other_bias)
+
+
+def answer_kernel(names, where_ref, probes_ref, *refs):
+    part_refs, base_ref, out_ref = refs[: len(names)], refs[len(names)], refs[-1]
+    probe_count, q_count = probes_ref.shape
+    offset = (probes_ref[...] ^ where_ref[0]).astype(jnp.float32)
+    offset = jnp.concatenate(
+        [offset, jnp.zeros((q_count - probe_count, q_count), jnp.float32)], axis=0
+    )
+    offset = jnp.transpose(offset).astype(jnp.int32)
+    step = 16
+    for r in range(0, q_count, step):
+        parts = {n: p[r : r + step, :].astype(jnp.float32) for n, p in zip(names, part_refs)}
+        for p in range(probe_count):
+            column = offset[r : r + step, p : p + 1]
+            if base_ref is out_ref:
+                best = choose([parts.get(n, parts[names[0]]) for n in range(8)], column)
+            else:
+                best = base_ref[r : r + step, p, :].astype(jnp.float32)
+                for n in names:
+                    best = jnp.where(column == n, parts[n], best)
+            out_ref[r : r + step, p, :] = best.astype(jnp.bfloat16)
+
+
+def answer(where, probes, parts, base=None):
+    probe_count, q_count = probes.shape
+    names = sorted(parts)
+    length = parts[names[0]].shape[1]
+    in_vmem = pl.BlockSpec(memory_space=pltpu.VMEM)
+    inputs = [parts[n] for n in names] + ([] if base is None else [base])
+    return pl.pallas_call(
+        functools.partial(answer_kernel, names),
+        out_shape=jax.ShapeDtypeStruct((q_count, probe_count, length), jnp.bfloat16),
+        in_specs=[pl.BlockSpec(memory_space=pltpu.SMEM)] + [in_vmem] * (1 + len(inputs)),
+        out_specs=in_vmem,
+        compiler_params=pltpu.CompilerParams(vmem_limit_bytes=24 * 1024 * 1024),
+        name="answer",
+    )(where, probes, *inputs)
+
+
+def by_blocks(queries, probes, fine_blocks, centroids):
+    q_count, probe_count = probes.shape
+    n_active = fine_blocks.shape[2]
+    width = queries.shape[1]
+    regions = lax.axis_size("region")
+
+    def hop(value, mask):
+        return lax.ppermute(value, "region", [(r, r ^ mask) for r in range(regions)])
+
+    region = lax.axis_index("region")
+    side = lax.axis_index("narrow")
+    where = jnp.stack([region, side]).astype(jnp.int32)
+    own = centroids[0]
+    probes = probes.T
+    fine = fine_blocks.reshape(q_count, -1).T
+    held = {4: hop(queries, 4)}
+    ids = list_ids(probes, fine)
+    held[0] = pack(queries, ids, 8)
+    held[1] = hop(held[0], 1)
+    held[2] = hop(held[0], 2)
+    other = lax.ppermute(own, "narrow", [(0, 1), (1, 0)])
+    factor = -0.5 / math.sqrt(width)
+    (own_bias,) = norms(own, factor, False)
+    other_bias, other = norms(other, factor, True)
+    late_ids, own_bias = lax.optimization_barrier((ids, own_bias))
+    ids_4 = hop(late_ids, 4)
+
+    def scored(*keys, weight=1):
+        blocks = [held[k] for k in keys]
+        return score(
+            where, blocks, own, other, own_bias, other_bias, q_count, probe_count, n_active, weight
+        )
+
+    barrier = lax.optimization_barrier
+    results, back = {}, {}
+    results[0], results[1] = scored(0, 1, weight=W01)
+    back[1] = hop(results[1], 1)
+    held[4], results[0] = barrier((held[4], results[0]))
+    held[4] = pack(held[4], ids_4, 8)
+    held[6] = hop(held[4], 2)
+    held[5] = hop(held[4], 1)
+    results[4], results[2] = scored(4, 2, weight=W42)
+    back[4] = hop(results[4], 4)
+    held[6], held[1], results[4] = barrier((held[6], held[1], results[4]))
+    held[7] = hop(held[6], 1)
+    held[3] = hop(held[1], 2)
+    results[5], results[6] = scored(5, 6, weight=W56)
+    back[5] = hop(results[5], 5)
+    back[6] = hop(results[6], 6)
+    results[2], results[5] = barrier((results[2], results[5]))
+    back[2] = hop(results[2], 2)
+    held[7], back[4], back[1] = barrier((held[7], back[4], back[1]))
+    (results[7],) = scored(7, weight=W73)
+    back[7] = hop(results[7], 7)
+    held[3], results[7] = barrier((held[3], results[7]))
+    (results[3],) = scored(3, weight=W73)
+    back[3] = hop(results[3], 3)
+    early = answer(where, probes, {0: results[0], **{k: back[k] for k in (1, 2, 4, 5, 6, 7)}})
+    return answer(where, probes, {3: back[3]}, early)
+
+
+def per_device(queries, probes, fine_blocks, centroids):
+    q_count, probe_count = probes.shape
+    regions = lax.axis_size("region")
+    if regions == 8 and lax.axis_size("narrow") == 2 and 2 * probe_count >= regions:
+        return by_blocks(queries, probes, fine_blocks, centroids)
+    return by_slots(queries, probes, fine_blocks, centroids)
 
 
 def solution(mesh):

time: 129 us -> 54.9 us (0.43)
  waiting for transfers between devices: 47.7 us -> 10.7 us
  blocking collectives: 29.3 us -> 0 us
  Pallas kernels: 0 us -> 17.5 us
  matrix products: 17.1 us -> 0 us
  between operations: 13.5 us -> 0.14 us
  starting transfers between devices: 11.6 us -> 22.1 us
  other arithmetic: 4.86 us -> 0.07 us
    all_to_all x2 -> x0, waiting for transfers between devices: 47 us -> none  [the longest x1 43.7 us: per_device(): lax.all_to_all(send_rows, 'region', split_axis=0, concat_axis=0, tiled=True)]
    all_to_all x1 -> x0, blocking collectives: 29.3 us -> none  [per_device(): lax.all_to_all(packed, 'region', split_axis=0, concat_axis=0, tiled=True)]
    ppermute x0 -> x16, starting transfers between devices: none -> 22.1 us  [the longest x15 21.7 us: hop(): lax.ppermute(value, 'region', [(r, r ^ mask) for r in range(regions)])]
    pallas_call x0 -> x12, Pallas kernels: none -> 17.5 us  [the longest x5 11.2 us: score(): pl.pallas_call(functools.partial(score_kernel, n_sets, q_count, probe_cou...]
    dot_general x6 -> x0, matrix products: 17.1 us -> none  [the longest x1 7.01 us: score_against(): jnp.einsum('nd,md->nm', flat_rows, centre_rows, preferred_element_type=jn...]
    all_to_all x2 -> x0, starting transfers between devices: 11.6 us -> none  [the longest x1 7.25 us: per_device(): lax.all_to_all(send_blocks, 'region', split_axis=0, concat_axis=0, tiled=...]
    ppermute x0 -> x16, waiting for transfers between devices: none -> 10.7 us  [the longest x15 10.7 us: hop(): lax.ppermute(value, 'region', [(r, r ^ mask) for r in range(regions)])]
    reduce_sum x1 -> x0, other arithmetic: 3.07 us -> none  [score_against(): sq_norm = jnp.sum(widened * widened, axis=1)]
  transfers between devices with their start and end apart: 3 -> 16, of which waited for: 2 -> 6; matrix products, arithmetic and copies ran while one was open for 8% -> 0% of each run, Pallas kernels for 0% -> 28%
where the time goes in v2:
time: 54.9 us; the launch traced here: 54.4 us
  starting transfers between devices  22.1 us (40%)
  Pallas kernels  17.5 us (32%)
  waiting for transfers between devices  10.7 us (19%)
  local copies, waits for them, and re-layouts  3.92 us (7%)
    ppermute x15, starting transfers between devices, hop(): lax.ppermute(value, 'region', [(r, r ^ mask) for r in range(regions)])  21.7 us
    pallas_call x5, Pallas kernels, score(): pl.pallas_call(functools.partial(score_kernel, n_sets, q_count, probe_cou...  11.2 us
    ppermute x15, waiting for transfers between devices, hop(): lax.ppermute(value, 'region', [(r, r ^ mask) for r in range(regions)])  10.7 us
    unnamed x12, local copies, waits for them, and re-layouts  3.92 us
    pallas_call x2, Pallas kernels, answer(): pl.pallas_call(functools.partial(answer_kernel, names), out_shape=jax.Sha...  3.69 us
    pallas_call x2, Pallas kernels, norms(): pl.pallas_call(functools.partial(norms_kernel, scale), out_shape=shapes,...  2.58 us
  transfers between devices with their start and end apart: 16, of which 6 were waited for; matrix products, arithmetic and copies ran while one was open for 0% of the time, Pallas kernels for 28%

profile of v2, /device:TPU:0, one launch (start us, length us, event | category | flops | bytes accessed | tf_op | source)
XLA Modules:
  0.0 54.4 jit_solution(16352303792286762136)
XLA Ops:
  0.5 3.6 %collective-permute-start = (bf16[128,1024]{1,0:T(8,128)(2,1)}, bf16[128,1024]{1,0:T(8,128)(2,1)S(1)}, u32[]{:S(2)}, u32[]{:S(2)}) collective-permute-start(bf16[128,1024]{1,0:T(8,128)(2,1)} %queries_ref.1), channel_id=1, source_target_pairs={{0,8},{2,10},{4,12},{6,14},{8,0},{10,2},{12,4},{14,6},{1,9},{3,11}... | collective-permute-start | bytes 786440 | tf_op jit(solution)/shard_map/ppermute | solution.py:295
  5.4 0.9 %copy-done.2 = bf16[128,1024]{1,0:T(8,128)(2,1)S(1)} copy-done((bf16[128,1024]{1,0:T(8,128)(2,1)S(1)}, bf16[128,1024]{1,0:T(8,128)(2,1)}, u32[]{:S(2)}) %copy-start.2) | copy-done | bytes 262168
  6.4 1.6 %collective-permute-start.1 = (bf16[136,1024]{1,0:T(8,128)(2,1)S(1)}, bf16[136,1024]{1,0:T(8,128)(2,1)S(1)}, u32[]{:S(2)}, u32[]{:S(2)}) collective-permute-start(bf16[136,1024]{1,0:T(8,128)(2,1)S(1)} %pack.2.refs_0_), channel_id=1, source_target_pairs={{0,2},{2,0},{4,6},{6,4},{8,10},{10,8},{12,14},{14,12},{1,3},{3,1},... | collective-permute-start | bytes 835592 | tf_op jit(solution)/shard_map/ppermute | solution.py:295
  8.0 1.6 %collective-permute-start.5 = (bf16[136,1024]{1,0:T(8,128)(2,1)S(1)}, bf16[136,1024]{1,0:T(8,128)(2,1)S(1)}, u32[]{:S(2)}, u32[]{:S(2)}) collective-permute-start(bf16[136,1024]{1,0:T(8,128)(2,1)S(1)} %pack.2.refs_0_), channel_id=1, source_target_pairs={{0,4},{2,6},{4,0},{6,2},{8,12},{10,14},{12,8},{14,10},{1,5},{3,7},... | collective-permute-start | bytes 835592 | tf_op jit(solution)/shard_map/ppermute | solution.py:295
  9.5 1.6 %copy-done = bf16[1,1024,1024]{2,1,0:T(8,128)(2,1)S(1)} copy-done((bf16[1,1024,1024]{2,1,0:T(8,128)(2,1)S(1)}, bf16[1,1024,1024]{2,1,0:T(8,128)(2,1)}, u32[]{:S(2)}) %copy-start) | copy-done | bytes 2097176
  11.1 1.3 %norms.3.refs_4_.refs_3_ = f32[1,1024]{1,0:T(1,128)S(1)} custom-call(bf16[1024,1024]{1,0:T(8,128)(2,1)S(1)} %bitcast.8), custom_call_target="tpu_custom_call" | custom-call | flops 4000000000 | bytes 2097152 | tf_op jit(solution)/shard_map/norms/pallas_call | solution.py:167
  12.8 1.3 %norms.2 = (f32[1,1024]{1,0:T(1,128)S(1)}, bf16[1024,1024]{1,0:T(8,128)(2,1)S(1)}) custom-call(bf16[1024,1024]{1,0:T(8,128)(2,1)S(1)} %collective-permute-done.2.rows_ref), custom_call_target="tpu_custom_call" | custom-call | flops 4000000000 | bytes 4194304 | tf_op jit(solution)/shard_map/norms/pallas_call | solution.py:167
  14.1 1.1 %collective-permute-done.1.refs_1_ = bf16[136,1024]{1,0:T(8,128)(2,1)S(1)} collective-permute-done((bf16[136,1024]{1,0:T(8,128)(2,1)S(1)}, bf16[136,1024]{1,0:T(8,128)(2,1)S(1)}, u32[]{:S(2)}, u32[]{:S(2)}) %collective-permute-start.1) | collective-permute-done | bytes 278560 | tf_op jit(solution)/shard_map/ppermute | solution.py:295
  15.3 2.3 %score.5 = (bf16[128,512]{1,0:T(8,128)(2,1)S(1)}, bf16[128,512]{1,0:T(8,128)(2,1)S(1)}) custom-call(s32[2]{0:T(128)S(1)} %pad_add_fusion.where_ref, bf16[136,1024]{1,0:T(8,128)(2,1)S(1)} %pack.2.refs_0_, bf16[136,1024]{1,0:T(8,128)(2,1)S(1)} %collective-permute-done.1.refs_1_, bf16[1024,1024]{1,0:T(8,128)(2,1)S(1)} %bitcast.9, ...), custom_call_target="tpu_custom_call" | custom-call | flops 1073741824 | bytes 4980736 | tf_op jit(solution)/shard_map/score/pallas_call | solution.py:232
  17.6 1.6 %collective-permute-start.4 = (bf16[136,1024]{1,0:T(8,128)(2,1)S(1)}, bf16[136,1024]{1,0:T(8,128)(2,1)S(1)}, u32[]{:S(2)}, u32[]{:S(2)}) collective-permute-start(bf16[136,1024]{1,0:T(8,128)(2,1)S(1)} %pack.3.refs_0_), channel_id=1, source_target_pairs={{0,4},{2,6},{4,0},{6,2},{8,12},{10,14},{12,8},{14,10},{1,5},{3,7},... | collective-permute-start | bytes 835592 | tf_op jit(solution)/shard_map/ppermute | solution.py:295
  19.2 1.5 %collective-permute-start.11 = (bf16[136,1024]{1,0:T(8,128)(2,1)S(1)}, bf16[136,1024]{1,0:T(8,128)(2,1)S(1)}, u32[]{:S(2)}, u32[]{:S(2)}) collective-permute-start(bf16[136,1024]{1,0:T(8,128)(2,1)S(1)} %pack.3.refs_0_), channel_id=1, source_target_pairs={{0,2},{2,0},{4,6},{6,4},{8,10},{10,8},{12,14},{14,12},{1,3},{3,1},... | collective-permute-start | bytes 835592 | tf_op jit(solution)/shard_map/ppermute | solution.py:295
  20.7 1.4 %collective-permute-done.5.refs_1_ = bf16[136,1024]{1,0:T(8,128)(2,1)S(1)} collective-permute-done((bf16[136,1024]{1,0:T(8,128)(2,1)S(1)}, bf16[136,1024]{1,0:T(8,128)(2,1)S(1)}, u32[]{:S(2)}, u32[]{:S(2)}) %collective-permute-start.5) | collective-permute-done | bytes 278560 | tf_op jit(solution)/shard_map/ppermute | solution.py:295
  22.1 2.2 %score.6 = (bf16[128,512]{1,0:T(8,128)(2,1)S(1)}, bf16[128,512]{1,0:T(8,128)(2,1)S(1)}) custom-call(s32[2]{0:T(128)S(1)} %pad_add_fusion.where_ref, bf16[136,1024]{1,0:T(8,128)(2,1)S(1)} %pack.3.refs_0_, bf16[136,1024]{1,0:T(8,128)(2,1)S(1)} %collective-permute-done.5.refs_1_, bf16[1024,1024]{1,0:T(8,128)(2,1)S(1)} %bitcast.10, ...), custom_call_target="tpu_custom_call" | custom-call | flops 1073741824 | bytes 4980736 | tf_op jit(solution)/shard_map/score/pallas_call | solution.py:232
  25.7 2.6 %collective-permute-done.4.refs_1_ = bf16[136,1024]{1,0:T(8,128)(2,1)S(1)} collective-permute-done((bf16[136,1024]{1,0:T(8,128)(2,1)S(1)}, bf16[136,1024]{1,0:T(8,128)(2,1)S(1)}, u32[]{:S(2)}, u32[]{:S(2)}) %collective-permute-start.4) | collective-permute-done | bytes 278560 | tf_op jit(solution)/shard_map/ppermute | solution.py:295
  29.5 2.2 %score.9 = (bf16[128,512]{1,0:T(8,128)(2,1)S(1)}, bf16[128,512]{1,0:T(8,128)(2,1)S(1)}) custom-call(s32[2]{0:T(128)S(1)} %pad_add_fusion.where_ref, bf16[136,1024]{1,0:T(8,128)(2,1)S(1)} %collective-permute-done.11.refs_0_, bf16[136,1024]{1,0:T(8,128)(2,1)S(1)} %collective-permute-done.4.refs_1_, bf16[1024,1024]{1,0:T(8,128)(2,1)S(1)} %bitcast.11, ...), custom_call_target="tpu_custom_call" | custom-call | flops 10737418240 | bytes 4980736 | tf_op jit(solution)/shard_map/score/pallas_call | solution.py:232
  31.7 3.1 %collective-permute-start.13 = (bf16[128,512]{1,0:T(8,128)(2,1)S(1)}, bf16[128,512]{1,0:T(8,128)(2,1)S(1)}, u32[]{:S(2)}, u32[]{:S(2)}) collective-permute-start(bf16[128,512]{1,0:T(8,128)(2,1)S(1)} %get-tuple-element.39), channel_id=1, source_target_pairs={{0,10},{2,8},{4,14},{6,12},{8,2},{10,0},{12,6},{14,4},{1,11},{3,9}... | collective-permute-start | bytes 393224 | tf_op jit(solution)/shard_map/ppermute | solution.py:295
  35.5 1.5 %collective-permute-start.14 = (bf16[128,512]{1,0:T(8,128)(2,1)S(1)}, bf16[128,512]{1,0:T(8,128)(2,1)S(1)}, u32[]{:S(2)}, u32[]{:S(2)}) collective-permute-start(bf16[128,512]{1,0:T(8,128)(2,1)S(1)} %get-tuple-element.42), channel_id=1, source_target_pairs={{0,12},{2,14},{4,8},{6,10},{8,4},{10,6},{12,0},{14,2},{1,13},{3,15... | collective-permute-start | bytes 393224 | tf_op jit(solution)/shard_map/ppermute | solution.py:295
  37.9 2.2 %score.7 = bf16[128,512]{1,0:T(8,128)(2,1)S(1)} custom-call(s32[2]{0:T(128)S(1)} %pad_add_fusion.where_ref, bf16[136,1024]{1,0:T(8,128)(2,1)S(1)} %collective-permute-done.7.refs_0_, bf16[1024,1024]{1,0:T(8,128)(2,1)S(1)} %bitcast.12, bf16[1024,1024]{1,0:T(8,128)(2,1)S(1)} %get-tuple-element.24.refs_3_.refs_2_, f32[1,1024]{1,0:T(1,128)S(1)} %norms.3.refs_4_.refs_3_, ...), custom_call_target="tpu_custom_call" | custom-call | flops 536870912 | bytes 4587520 | tf_op jit(solution)/shard_map/score/pallas_call | solution.py:232
  40.1 3.7 %collective-permute-start.15 = (bf16[128,512]{1,0:T(8,128)(2,1)S(1)}, bf16[128,512]{1,0:T(8,128)(2,1)S(1)}, u32[]{:S(2)}, u32[]{:S(2)}) collective-permute-start(bf16[128,512]{1,0:T(8,128)(2,1)S(1)} %score.7), channel_id=1, source_target_pairs={{0,14},{2,12},{4,10},{6,8},{8,6},{10,4},{12,2},{14,0},{1,15},{3,13... | collective-permute-start | bytes 393224 | tf_op jit(solution)/shard_map/ppermute | solution.py:295
  43.8 2.2 %score.8 = bf16[128,512]{1,0:T(8,128)(2,1)S(1)} custom-call(s32[2]{0:T(128)S(1)} %pad_add_fusion.where_ref, bf16[136,1024]{1,0:T(8,128)(2,1)S(1)} %collective-permute-done.6.refs_0_, bf16[1024,1024]{1,0:T(8,128)(2,1)S(1)} %bitcast.13, bf16[1024,1024]{1,0:T(8,128)(2,1)S(1)} %get-tuple-element.24.refs_3_.refs_2_, f32[1,1024]{1,0:T(1,128)S(1)} %norms.3.refs_4_.refs_3_, ...), custom_call_target="tpu_custom_call" | custom-call | flops 536870912 | bytes 4587520 | tf_op jit(solution)/shard_map/score/pallas_call | solution.py:232
  46.1 2.5 %collective-permute-done.14.refs_5_ = bf16[128,512]{1,0:T(8,128)(2,1)S(1)} collective-permute-done((bf16[128,512]{1,0:T(8,128)(2,1)S(1)}, bf16[128,512]{1,0:T(8,128)(2,1)S(1)}, u32[]{:S(2)}, u32[]{:S(2)}) %collective-permute-start.14) | collective-permute-done | bytes 131104 | tf_op jit(solution)/shard_map/ppermute | solution.py:295
  48.6 2.1 %collective-permute-done.15.refs_6_ = bf16[128,512]{1,0:T(8,128)(2,1)S(1)} collective-permute-done((bf16[128,512]{1,0:T(8,128)(2,1)S(1)}, bf16[128,512]{1,0:T(8,128)(2,1)S(1)}, u32[]{:S(2)}, u32[]{:S(2)}) %collective-permute-start.15) | collective-permute-done | bytes 131104 | tf_op jit(solution)/shard_map/ppermute | solution.py:295
  50.7 1.4 %answer.2.refs_1_ = bf16[128,4,512]{2,1,0:T(4,128)(2,1)S(1)} custom-call(s32[2]{0:T(128)S(1)} %pad_add_fusion.where_ref, s32[4,128]{1,0:T(4,128)S(1)} %bitcast.15, bf16[128,512]{1,0:T(8,128)(2,1)S(1)} %get-tuple-element.36.refs_0_, bf16[128,512]{1,0:T(8,128)(2,1)S(1)} %collective-permute-done.9.refs_1_, ...), custom_call_target="tpu_custom_call" | custom-call | tf_op jit(solution)/shard_map/answer/pallas_call | solution.py:278
  52.1 2.3 %answer.3 = bf16[128,4,512]{2,1,0:T(4,128)(2,1)} custom-call(s32[2]{0:T(128)S(1)} %pad_add_fusion.where_ref, s32[4,128]{1,0:T(4,128)S(1)} %bitcast.16, bf16[128,512]{1,0:T(8,128)(2,1)S(1)} %collective-permute-done.10.refs_0_, bf16[128,4,512]{2,1,0:T(4,128)(2,1)S(1)} %answer.2.refs_1_), custom_call_target="tpu_custom_call" | custom-call | tf_op jit(solution)/shard_map/answer/pallas_call | solution.py:278
  (33 shorter events, 6.4 us)
Async XLA Ops:
  0.0 12.8 %collective-permute-start.2 = (bf16[1024,1024]{1,0:T(8,128)(2,1)}, bf16[1024,1024]{1,0:T(8,128)(2,1)S(1)}, u32[]{:S(2)}, u32[]{:S(2)}) collective-permute-start(bf16[1024,1024]{1,0:T(8,128)(2,1)} %bitcast.7), channel_id=1, source_target_pairs={{0,1},{1,0},{2,3},{3,2},{4,5},{5,4},{6,7},{7,6},{8,9},{9,8},{10,11... | collective-permute-start | bytes 6291464 | tf_op jit(solution)/shard_map/ppermute | solution.py:308
  0.5 17.1 %collective-permute-start = (bf16[128,1024]{1,0:T(8,128)(2,1)}, bf16[128,1024]{1,0:T(8,128)(2,1)S(1)}, u32[]{:S(2)}, u32[]{:S(2)}) collective-permute-start(bf16[128,1024]{1,0:T(8,128)(2,1)} %queries_ref.1), channel_id=1, source_target_pairs={{0,8},{2,10},{4,12},{6,14},{8,0},{10,2},{12,4},{14,6},{1,9},{3,11}... | collective-permute-start | bytes 786440 | tf_op jit(solution)/shard_map/ppermute | solution.py:295
  4.0 0.7 %copy-start.3 = (s32[128,4]{0,1:T(4,128)S(1)}, s32[128,4]{0,1:T(4,128)}, u32[]{:S(2)}) copy-start(s32[128,4]{0,1:T(4,128)} %param.5) | copy-start | bytes 6148
  4.7 0.7 %copy-start.5 = (s32[128,4,4]{0,2,1:T(4,128)S(1)}, s32[128,4,4]{0,2,1:T(4,128)}, u32[]{:S(2)}) copy-start(s32[128,4,4]{0,2,1:T(4,128)} %param.6) | copy-start | bytes 24580
  5.4 0.9 %copy-start.2 = (bf16[128,1024]{1,0:T(8,128)(2,1)S(1)}, bf16[128,1024]{1,0:T(8,128)(2,1)}, u32[]{:S(2)}) copy-start(bf16[128,1024]{1,0:T(8,128)(2,1)} %queries_ref.1) | copy-start | bytes 786436
  6.4 8.9 %collective-permute-start.1 = (bf16[136,1024]{1,0:T(8,128)(2,1)S(1)}, bf16[136,1024]{1,0:T(8,128)(2,1)S(1)}, u32[]{:S(2)}, u32[]{:S(2)}) collective-permute-start(bf16[136,1024]{1,0:T(8,128)(2,1)S(1)} %pack.2.refs_0_), channel_id=1, source_target_pairs={{0,2},{2,0},{4,6},{6,4},{8,10},{10,8},{12,14},{14,12},{1,3},{3,1},... | collective-permute-start | bytes 835592 | tf_op jit(solution)/shard_map/ppermute | solution.py:295
  8.0 14.2 %collective-permute-start.5 = (bf16[136,1024]{1,0:T(8,128)(2,1)S(1)}, bf16[136,1024]{1,0:T(8,128)(2,1)S(1)}, u32[]{:S(2)}, u32[]{:S(2)}) collective-permute-start(bf16[136,1024]{1,0:T(8,128)(2,1)S(1)} %pack.2.refs_0_), channel_id=1, source_target_pairs={{0,4},{2,6},{4,0},{6,2},{8,12},{10,14},{12,8},{14,10},{1,5},{3,7},... | collective-permute-start | bytes 835592 | tf_op jit(solution)/shard_map/ppermute | solution.py:295
  9.5 1.6 %copy-start = (bf16[1,1024,1024]{2,1,0:T(8,128)(2,1)S(1)}, bf16[1,1024,1024]{2,1,0:T(8,128)(2,1)}, u32[]{:S(2)}) copy-start(bf16[1,1024,1024]{2,1,0:T(8,128)(2,1)} %param.7) | copy-start | bytes 6291460
  12.4 5.1 %collective-permute-start.3 = (bf16[32,128]{1,0:T(8,128)(2,1)S(1)}, bf16[32,128]{1,0:T(8,128)(2,1)S(1)}, u32[]{:S(2)}, u32[]{:S(2)}) collective-permute-start(bf16[32,128]{1,0:T(8,128)(2,1)S(1)} %list_ids.1.ids_ref), channel_id=1, source_target_pairs={{0,8},{2,10},{4,12},{6,14},{8,0},{10,2},{12,4},{14,6},{1,9},{3,11}... | collective-permute-start | bytes 24584 | tf_op jit(solution)/shard_map/ppermute | solution.py:295
  12.8 2.4 %copy-start.1 = (bf16[1,1024,1024]{2,1,0:T(8,128)(2,1)S(1)}, bf16[1,1024,1024]{2,1,0:T(8,128)(2,1)}, u32[]{:S(2)}) copy-start(bf16[1,1024,1024]{2,1,0:T(8,128)(2,1)} %param.7) | copy-start | bytes 6291460
  17.6 10.8 %collective-permute-start.4 = (bf16[136,1024]{1,0:T(8,128)(2,1)S(1)}, bf16[136,1024]{1,0:T(8,128)(2,1)S(1)}, u32[]{:S(2)}, u32[]{:S(2)}) collective-permute-start(bf16[136,1024]{1,0:T(8,128)(2,1)S(1)} %pack.3.refs_0_), channel_id=1, source_target_pairs={{0,4},{2,6},{4,0},{6,2},{8,12},{10,14},{12,8},{14,10},{1,5},{3,7},... | collective-permute-start | bytes 835592 | tf_op jit(solution)/shard_map/ppermute | solution.py:295
  19.2 10.3 %collective-permute-start.11 = (bf16[136,1024]{1,0:T(8,128)(2,1)S(1)}, bf16[136,1024]{1,0:T(8,128)(2,1)S(1)}, u32[]{:S(2)}, u32[]{:S(2)}) collective-permute-start(bf16[136,1024]{1,0:T(8,128)(2,1)S(1)} %pack.3.refs_0_), channel_id=1, source_target_pairs={{0,2},{2,0},{4,6},{6,4},{8,10},{10,8},{12,14},{14,12},{1,3},{3,1},... | collective-permute-start | bytes 835592 | tf_op jit(solution)/shard_map/ppermute | solution.py:295
  24.4 10.5 %collective-permute-start.8 = (bf16[128,512]{1,0:T(8,128)(2,1)S(1)}, bf16[128,512]{1,0:T(8,128)(2,1)S(1)}, u32[]{:S(2)}, u32[]{:S(2)}) collective-permute-start(bf16[128,512]{1,0:T(8,128)(2,1)S(1)} %get-tuple-element.30), channel_id=1, source_target_pairs={{0,8},{2,10},{4,12},{6,14},{8,0},{10,2},{12,4},{14,6},{1,9},{3,11}... | collective-permute-start | bytes 393224 | tf_op jit(solution)/shard_map/ppermute | solution.py:295
  25.2 10.3 %collective-permute-start.9 = (bf16[128,512]{1,0:T(8,128)(2,1)S(1)}, bf16[128,512]{1,0:T(8,128)(2,1)S(1)}, u32[]{:S(2)}, u32[]{:S(2)}) collective-permute-start(bf16[128,512]{1,0:T(8,128)(2,1)S(1)} %get-tuple-element.33), channel_id=1, source_target_pairs={{0,2},{2,0},{4,6},{6,4},{8,10},{10,8},{12,14},{14,12},{1,3},{3,1},... | collective-permute-start | bytes 393224 | tf_op jit(solution)/shard_map/ppermute | solution.py:295
  28.3 9.6 %collective-permute-start.7 = (bf16[136,1024]{1,0:T(8,128)(2,1)S(1)}, bf16[136,1024]{1,0:T(8,128)(2,1)S(1)}, u32[]{:S(2)}, u32[]{:S(2)}) collective-permute-start(bf16[136,1024]{1,0:T(8,128)(2,1)S(1)} %collective-permute-done.4.refs_1_), channel_id=1, source_target_pairs={{0,2},{2,0},{4,6},{6,4},{8,10},{10,8},{12,14},{14,12},{1,3},{3,1},... | collective-permute-start | bytes 835592 | tf_op jit(solution)/shard_map/ppermute | solution.py:295
  29.2 14.6 %collective-permute-start.6 = (bf16[136,1024]{1,0:T(8,128)(2,1)S(1)}, bf16[136,1024]{1,0:T(8,128)(2,1)S(1)}, u32[]{:S(2)}, u32[]{:S(2)}) collective-permute-start(bf16[136,1024]{1,0:T(8,128)(2,1)S(1)} %collective-permute-done.1.refs_1_), channel_id=1, source_target_pairs={{0,4},{2,6},{4,0},{6,2},{8,12},{10,14},{12,8},{14,10},{1,5},{3,7},... | collective-permute-start | bytes 835592 | tf_op jit(solution)/shard_map/ppermute | solution.py:295
  31.7 14.4 %collective-permute-start.13 = (bf16[128,512]{1,0:T(8,128)(2,1)S(1)}, bf16[128,512]{1,0:T(8,128)(2,1)S(1)}, u32[]{:S(2)}, u32[]{:S(2)}) collective-permute-start(bf16[128,512]{1,0:T(8,128)(2,1)S(1)} %get-tuple-element.39), channel_id=1, source_target_pairs={{0,10},{2,8},{4,14},{6,12},{8,2},{10,0},{12,6},{14,4},{1,11},{3,9}... | collective-permute-start | bytes 393224 | tf_op jit(solution)/shard_map/ppermute | solution.py:295
  34.8 11.3 %collective-permute-start.12 = (bf16[128,512]{1,0:T(8,128)(2,1)S(1)}, bf16[128,512]{1,0:T(8,128)(2,1)S(1)}, u32[]{:S(2)}, u32[]{:S(2)}) collective-permute-start(bf16[128,512]{1,0:T(8,128)(2,1)S(1)} %get-tuple-element.40), channel_id=1, source_target_pairs={{0,4},{2,6},{4,0},{6,2},{8,12},{10,14},{12,8},{14,10},{1,5},{3,7},... | collective-permute-start | bytes 393224 | tf_op jit(solution)/shard_map/ppermute | solution.py:295
  35.5 13.2 %collective-permute-start.14 = (bf16[128,512]{1,0:T(8,128)(2,1)S(1)}, bf16[128,512]{1,0:T(8,128)(2,1)S(1)}, u32[]{:S(2)}, u32[]{:S(2)}) collective-permute-start(bf16[128,512]{1,0:T(8,128)(2,1)S(1)} %get-tuple-element.42), channel_id=1, source_target_pairs={{0,12},{2,14},{4,8},{6,10},{8,4},{10,6},{12,0},{14,2},{1,13},{3,15... | collective-permute-start | bytes 393224 | tf_op jit(solution)/shard_map/ppermute | solution.py:295
  40.1 10.6 %copy-start.4 = (s32[128,4]{0,1:T(4,128)S(1)}, s32[128,4]{0,1:T(4,128)}, u32[]{:S(2)}) copy-start(s32[128,4]{0,1:T(4,128)} %param.5) | copy-start | bytes 6148
  40.1 10.6 %collective-permute-start.15 = (bf16[128,512]{1,0:T(8,128)(2,1)S(1)}, bf16[128,512]{1,0:T(8,128)(2,1)S(1)}, u32[]{:S(2)}, u32[]{:S(2)}) collective-permute-start(bf16[128,512]{1,0:T(8,128)(2,1)S(1)} %score.7), channel_id=1, source_target_pairs={{0,14},{2,12},{4,10},{6,8},{8,6},{10,4},{12,2},{14,0},{1,15},{3,13... | collective-permute-start | bytes 393224 | tf_op jit(solution)/shard_map/ppermute | solution.py:295
  46.0 6.1 %collective-permute-start.10 = (bf16[128,512]{1,0:T(8,128)(2,1)S(1)}, bf16[128,512]{1,0:T(8,128)(2,1)S(1)}, u32[]{:S(2)}, u32[]{:S(2)}) collective-permute-start(bf16[128,512]{1,0:T(8,128)(2,1)S(1)} %score.8), channel_id=1, source_target_pairs={{0,6},{2,4},{4,2},{6,0},{8,14},{10,12},{12,10},{14,8},{1,7},{3,5},... | collective-permute-start | bytes 393224 | tf_op jit(solution)/shard_map/ppermute | solution.py:295

commit v3 on v2

--- a/solution.py
+++ b/solution.py
@@ -247,10 +247,11 @@
     )(where, *blocks, own, other, own_bias, other_bias)
 
 
-def answer_kernel(names, where_ref, probes_ref, *refs):
+def answer_kernel(names, offset_ref, *refs):
     part_refs, base_ref, out_ref = refs[: len(names)], refs[len(names)], refs[-1]
-    probe_count, q_count = probes_ref.shape
-    offset = (probes_ref[...] ^ where_ref[0]).astype(jnp.float32)
+    probe_count, q_count = offset_ref.shape
+    length = part_refs[0].shape[1]
+    offset = offset_ref[...].astype(jnp.float32)
     offset = jnp.concatenate(
         [offset, jnp.zeros((q_count - probe_count, q_count), jnp.float32)], axis=0
     )
@@ -260,29 +261,32 @@
         parts = {n: p[r : r + step, :].astype(jnp.float32) for n, p in zip(names, part_refs)}
         for p in range(probe_count):
             column = offset[r : r + step, p : p + 1]
+            place = slice(p * length, (p + 1) * length)
             if base_ref is out_ref:
                 best = choose([parts.get(n, parts[names[0]]) for n in range(8)], column)
+                out_ref[r : r + step, place] = best.astype(jnp.bfloat16)
             else:
-                best = base_ref[r : r + step, p, :].astype(jnp.float32)
+                best = base_ref[r : r + step, place].astype(jnp.float32)
                 for n in names:
                     best = jnp.where(column == n, parts[n], best)
-            out_ref[r : r + step, p, :] = best.astype(jnp.bfloat16)
-
-
-def answer(where, probes, parts, base=None):
-    probe_count, q_count = probes.shape
+                out_ref[r : r + step, p, :] = best.astype(jnp.bfloat16)
+
+
+def answer(offset, parts, base=None):
+    probe_count, q_count = offset.shape
     names = sorted(parts)
     length = parts[names[0]].shape[1]
     in_vmem = pl.BlockSpec(memory_space=pltpu.VMEM)
     inputs = [parts[n] for n in names] + ([] if base is None else [base])
+    shape = (q_count, probe_count * length) if base is None else (q_count, probe_count, length)
     return pl.pallas_call(
         functools.partial(answer_kernel, names),
-        out_shape=jax.ShapeDtypeStruct((q_count, probe_count, length), jnp.bfloat16),
-        in_specs=[pl.BlockSpec(memory_space=pltpu.SMEM)] + [in_vmem] * (1 + len(inputs)),
+        out_shape=jax.ShapeDtypeStruct(shape, jnp.bfloat16),
+        in_specs=[in_vmem] * (1 + len(inputs)),
         out_specs=in_vmem,
         compiler_params=pltpu.CompilerParams(vmem_limit_bytes=24 * 1024 * 1024),
         name="answer",
-    )(where, probes, *inputs)
+    )(offset, *inputs)
 
 
 def by_blocks(queries, probes, fine_blocks, centroids):
@@ -342,8 +346,9 @@
     held[3], results[7] = barrier((held[3], results[7]))
     (results[3],) = scored(3, weight=W73)
     back[3] = hop(results[3], 3)
-    early = answer(where, probes, {0: results[0], **{k: back[k] for k in (1, 2, 4, 5, 6, 7)}})
-    return answer(where, probes, {3: back[3]}, early)
+    early = answer(probes ^ region, {0: results[0], **{k: back[k] for k in (1, 2, 4, 5, 6)}})
+    probes, back[7] = barrier((probes, back[7]))
+    return answer(probes ^ region, {3: back[3], 7: back[7]}, early)
 
 
 def per_device(queries, probes, fine_blocks, centroids):

time: 54.9 us -> 53.8 us (0.980)
  Pallas kernels: 17.5 us -> 15.7 us
  waiting for transfers between devices: 10.7 us -> 11.5 us
    pallas_call x2, Pallas kernels: 3.69 us -> 1.94 us  [answer(): pl.pallas_call(functools.partial(answer_kernel, names), out_shape=jax.Sha...]
    ppermute x15, waiting for transfers between devices: 10.7 us -> 11.5 us  [hop(): lax.ppermute(value, 'region', [(r, r ^ mask) for r in range(regions)])]
  transfers between devices with their start and end apart: 16 -> 16, of which waited for: 6 -> 7; matrix products, arithmetic and copies ran while one was open for 0% -> 0% of each run, Pallas kernels for 28% -> 27%
where the time goes in v3:
time: 53.8 us; the launch traced here: 53.5 us
  starting transfers between devices  22.1 us (41%)
  Pallas kernels  15.7 us (29%)
  waiting for transfers between devices  11.5 us (21%)
  local copies, waits for them, and re-layouts  3.92 us (7%)
    ppermute x15, starting transfers between devices, hop(): lax.ppermute(value, 'region', [(r, r ^ mask) for r in range(regions)])  21.7 us
    ppermute x15, waiting for transfers between devices, hop(): lax.ppermute(value, 'region', [(r, r ^ mask) for r in range(regions)])  11.5 us
    pallas_call x5, Pallas kernels, score(): pl.pallas_call(functools.partial(score_kernel, n_sets, q_count, probe_cou...  11.2 us
    unnamed x12, local copies, waits for them, and re-layouts  3.92 us
    pallas_call x2, Pallas kernels, norms(): pl.pallas_call(functools.partial(norms_kernel, scale), out_shape=shapes,...  2.58 us
    pallas_call x2, Pallas kernels, answer(): pl.pallas_call(functools.partial(answer_kernel, names), out_shape=jax.Sha...  1.94 us
  transfers between devices with their start and end apart: 16, of which 7 were waited for; matrix products, arithmetic and copies ran while one was open for 0% of the time, Pallas kernels for 27%

profile of v3, /device:TPU:0, one launch (start us, length us, event | category | flops | bytes accessed | tf_op | source)
XLA Modules:
  0.0 53.5 jit_solution(18344360846231779226)
XLA Ops:
  0.5 3.6 %collective-permute-start = (bf16[128,1024]{1,0:T(8,128)(2,1)}, bf16[128,1024]{1,0:T(8,128)(2,1)S(1)}, u32[]{:S(2)}, u32[]{:S(2)}) collective-permute-start(bf16[128,1024]{1,0:T(8,128)(2,1)} %queries_ref.1), channel_id=1, source_target_pairs={{0,8},{2,10},{4,12},{6,14},{8,0},{10,2},{12,4},{14,6},{1,9},{3,11}... | collective-permute-start | bytes 786440 | tf_op jit(solution)/shard_map/ppermute | solution.py:299
  5.4 0.9 %copy-done.2 = bf16[128,1024]{1,0:T(8,128)(2,1)S(1)} copy-done((bf16[128,1024]{1,0:T(8,128)(2,1)S(1)}, bf16[128,1024]{1,0:T(8,128)(2,1)}, u32[]{:S(2)}) %copy-start.2) | copy-done | bytes 262168
  6.4 1.6 %collective-permute-start.1 = (bf16[136,1024]{1,0:T(8,128)(2,1)S(1)}, bf16[136,1024]{1,0:T(8,128)(2,1)S(1)}, u32[]{:S(2)}, u32[]{:S(2)}) collective-permute-start(bf16[136,1024]{1,0:T(8,128)(2,1)S(1)} %pack.2.refs_0_), channel_id=1, source_target_pairs={{0,2},{2,0},{4,6},{6,4},{8,10},{10,8},{12,14},{14,12},{1,3},{3,1},... | collective-permute-start | bytes 835592 | tf_op jit(solution)/shard_map/ppermute | solution.py:299
  8.0 1.6 %collective-permute-start.5 = (bf16[136,1024]{1,0:T(8,128)(2,1)S(1)}, bf16[136,1024]{1,0:T(8,128)(2,1)S(1)}, u32[]{:S(2)}, u32[]{:S(2)}) collective-permute-start(bf16[136,1024]{1,0:T(8,128)(2,1)S(1)} %pack.2.refs_0_), channel_id=1, source_target_pairs={{0,4},{2,6},{4,0},{6,2},{8,12},{10,14},{12,8},{14,10},{1,5},{3,7},... | collective-permute-start | bytes 835592 | tf_op jit(solution)/shard_map/ppermute | solution.py:299
  9.5 1.6 %copy-done = bf16[1,1024,1024]{2,1,0:T(8,128)(2,1)S(1)} copy-done((bf16[1,1024,1024]{2,1,0:T(8,128)(2,1)S(1)}, bf16[1,1024,1024]{2,1,0:T(8,128)(2,1)}, u32[]{:S(2)}) %copy-start) | copy-done | bytes 2097176
  11.1 1.3 %norms.3.refs_4_.refs_3_ = f32[1,1024]{1,0:T(1,128)S(1)} custom-call(bf16[1024,1024]{1,0:T(8,128)(2,1)S(1)} %bitcast.9), custom_call_target="tpu_custom_call" | custom-call | flops 4000000000 | bytes 2097152 | tf_op jit(solution)/shard_map/norms/pallas_call | solution.py:167
  12.8 1.3 %norms.2 = (f32[1,1024]{1,0:T(1,128)S(1)}, bf16[1024,1024]{1,0:T(8,128)(2,1)S(1)}) custom-call(bf16[1024,1024]{1,0:T(8,128)(2,1)S(1)} %collective-permute-done.2.rows_ref), custom_call_target="tpu_custom_call" | custom-call | flops 4000000000 | bytes 4194304 | tf_op jit(solution)/shard_map/norms/pallas_call | solution.py:167
  14.1 1.1 %collective-permute-done.1.refs_1_ = bf16[136,1024]{1,0:T(8,128)(2,1)S(1)} collective-permute-done((bf16[136,1024]{1,0:T(8,128)(2,1)S(1)}, bf16[136,1024]{1,0:T(8,128)(2,1)S(1)}, u32[]{:S(2)}, u32[]{:S(2)}) %collective-permute-start.1) | collective-permute-done | bytes 278560 | tf_op jit(solution)/shard_map/ppermute | solution.py:299
  15.3 2.3 %score.5 = (bf16[128,512]{1,0:T(8,128)(2,1)S(1)}, bf16[128,512]{1,0:T(8,128)(2,1)S(1)}) custom-call(s32[2]{0:T(128)S(1)} %pad_add_fusion.where_ref, bf16[136,1024]{1,0:T(8,128)(2,1)S(1)} %pack.2.refs_0_, bf16[136,1024]{1,0:T(8,128)(2,1)S(1)} %collective-permute-done.1.refs_1_, bf16[1024,1024]{1,0:T(8,128)(2,1)S(1)} %bitcast.10, ...), custom_call_target="tpu_custom_call" | custom-call | flops 1073741824 | bytes 4980736 | tf_op jit(solution)/shard_map/score/pallas_call | solution.py:232
  17.6 1.6 %collective-permute-start.4 = (bf16[136,1024]{1,0:T(8,128)(2,1)S(1)}, bf16[136,1024]{1,0:T(8,128)(2,1)S(1)}, u32[]{:S(2)}, u32[]{:S(2)}) collective-permute-start(bf16[136,1024]{1,0:T(8,128)(2,1)S(1)} %pack.3.refs_0_), channel_id=1, source_target_pairs={{0,4},{2,6},{4,0},{6,2},{8,12},{10,14},{12,8},{14,10},{1,5},{3,7},... | collective-permute-start | bytes 835592 | tf_op jit(solution)/shard_map/ppermute | solution.py:299
  19.2 1.5 %collective-permute-start.12 = (bf16[136,1024]{1,0:T(8,128)(2,1)S(1)}, bf16[136,1024]{1,0:T(8,128)(2,1)S(1)}, u32[]{:S(2)}, u32[]{:S(2)}) collective-permute-start(bf16[136,1024]{1,0:T(8,128)(2,1)S(1)} %pack.3.refs_0_), channel_id=1, source_target_pairs={{0,2},{2,0},{4,6},{6,4},{8,10},{10,8},{12,14},{14,12},{1,3},{3,1},... | collective-permute-start | bytes 835592 | tf_op jit(solution)/shard_map/ppermute | solution.py:299
  20.7 1.4 %collective-permute-done.5.refs_1_ = bf16[136,1024]{1,0:T(8,128)(2,1)S(1)} collective-permute-done((bf16[136,1024]{1,0:T(8,128)(2,1)S(1)}, bf16[136,1024]{1,0:T(8,128)(2,1)S(1)}, u32[]{:S(2)}, u32[]{:S(2)}) %collective-permute-start.5) | collective-permute-done | bytes 278560 | tf_op jit(solution)/shard_map/ppermute | solution.py:299
  22.1 2.2 %score.6 = (bf16[128,512]{1,0:T(8,128)(2,1)S(1)}, bf16[128,512]{1,0:T(8,128)(2,1)S(1)}) custom-call(s32[2]{0:T(128)S(1)} %pad_add_fusion.where_ref, bf16[136,1024]{1,0:T(8,128)(2,1)S(1)} %pack.3.refs_0_, bf16[136,1024]{1,0:T(8,128)(2,1)S(1)} %collective-permute-done.5.refs_1_, bf16[1024,1024]{1,0:T(8,128)(2,1)S(1)} %bitcast.11, ...), custom_call_target="tpu_custom_call" | custom-call | flops 1073741824 | bytes 4980736 | tf_op jit(solution)/shard_map/score/pallas_call | solution.py:232
  25.7 2.6 %collective-permute-done.4.refs_1_ = bf16[136,1024]{1,0:T(8,128)(2,1)S(1)} collective-permute-done((bf16[136,1024]{1,0:T(8,128)(2,1)S(1)}, bf16[136,1024]{1,0:T(8,128)(2,1)S(1)}, u32[]{:S(2)}, u32[]{:S(2)}) %collective-permute-start.4) | collective-permute-done | bytes 278560 | tf_op jit(solution)/shard_map/ppermute | solution.py:299
  29.5 2.2 %score.9 = (bf16[128,512]{1,0:T(8,128)(2,1)S(1)}, bf16[128,512]{1,0:T(8,128)(2,1)S(1)}) custom-call(s32[2]{0:T(128)S(1)} %pad_add_fusion.where_ref, bf16[136,1024]{1,0:T(8,128)(2,1)S(1)} %collective-permute-done.12.refs_0_, bf16[136,1024]{1,0:T(8,128)(2,1)S(1)} %collective-permute-done.4.refs_1_, bf16[1024,1024]{1,0:T(8,128)(2,1)S(1)} %bitcast.12, ...), custom_call_target="tpu_custom_call" | custom-call | flops 10737418240 | bytes 4980736 | tf_op jit(solution)/shard_map/score/pallas_call | solution.py:232
  31.7 3.1 %collective-permute-start.14 = (bf16[128,512]{1,0:T(8,128)(2,1)S(1)}, bf16[128,512]{1,0:T(8,128)(2,1)S(1)}, u32[]{:S(2)}, u32[]{:S(2)}) collective-permute-start(bf16[128,512]{1,0:T(8,128)(2,1)S(1)} %get-tuple-element.43), channel_id=1, source_target_pairs={{0,10},{2,8},{4,14},{6,12},{8,2},{10,0},{12,6},{14,4},{1,11},{3,9}... | collective-permute-start | bytes 393224 | tf_op jit(solution)/shard_map/ppermute | solution.py:299
  35.5 1.5 %collective-permute-start.15 = (bf16[128,512]{1,0:T(8,128)(2,1)S(1)}, bf16[128,512]{1,0:T(8,128)(2,1)S(1)}, u32[]{:S(2)}, u32[]{:S(2)}) collective-permute-start(bf16[128,512]{1,0:T(8,128)(2,1)S(1)} %get-tuple-element.46), channel_id=1, source_target_pairs={{0,12},{2,14},{4,8},{6,10},{8,4},{10,6},{12,0},{14,2},{1,13},{3,15... | collective-permute-start | bytes 393224 | tf_op jit(solution)/shard_map/ppermute | solution.py:299
  37.9 2.2 %score.7 = bf16[128,512]{1,0:T(8,128)(2,1)S(1)} custom-call(s32[2]{0:T(128)S(1)} %pad_add_fusion.where_ref, bf16[136,1024]{1,0:T(8,128)(2,1)S(1)} %collective-permute-done.6.refs_0_, bf16[1024,1024]{1,0:T(8,128)(2,1)S(1)} %bitcast.13, bf16[1024,1024]{1,0:T(8,128)(2,1)S(1)} %get-tuple-element.26.refs_3_.refs_2_, f32[1,1024]{1,0:T(1,128)S(1)} %norms.3.refs_4_.refs_3_, ...), custom_call_target="tpu_custom_call" | custom-call | flops 536870912 | bytes 4587520 | tf_op jit(solution)/shard_map/score/pallas_call | solution.py:232
  40.1 3.7 %collective-permute-start.9 = (bf16[128,512]{1,0:T(8,128)(2,1)S(1)}, bf16[128,512]{1,0:T(8,128)(2,1)S(1)}, u32[]{:S(2)}, u32[]{:S(2)}) collective-permute-start(bf16[128,512]{1,0:T(8,128)(2,1)S(1)} %score.7), channel_id=1, source_target_pairs={{0,14},{2,12},{4,10},{6,8},{8,6},{10,4},{12,2},{14,0},{1,15},{3,13... | collective-permute-start | bytes 393224 | tf_op jit(solution)/shard_map/ppermute | solution.py:299
  43.8 2.2 %score.8 = bf16[128,512]{1,0:T(8,128)(2,1)S(1)} custom-call(s32[2]{0:T(128)S(1)} %pad_add_fusion.where_ref, bf16[136,1024]{1,0:T(8,128)(2,1)S(1)} %collective-permute-done.10.refs_0_, bf16[1024,1024]{1,0:T(8,128)(2,1)S(1)} %bitcast.14, bf16[1024,1024]{1,0:T(8,128)(2,1)S(1)} %get-tuple-element.26.refs_3_.refs_2_, f32[1,1024]{1,0:T(1,128)S(1)} %norms.3.refs_4_.refs_3_, ...), custom_call_target="tpu_custom_call" | custom-call | flops 536870912 | bytes 4587520 | tf_op jit(solution)/shard_map/score/pallas_call | solution.py:232
  46.1 2.5 %collective-permute-done.15.refs_5_ = bf16[128,512]{1,0:T(8,128)(2,1)S(1)} collective-permute-done((bf16[128,512]{1,0:T(8,128)(2,1)S(1)}, bf16[128,512]{1,0:T(8,128)(2,1)S(1)}, u32[]{:S(2)}, u32[]{:S(2)}) %collective-permute-start.15) | collective-permute-done | bytes 131104 | tf_op jit(solution)/shard_map/ppermute | solution.py:299
  49.1 1.6 %collective-permute-done.9.refs_1_ = bf16[128,512]{1,0:T(8,128)(2,1)S(1)} collective-permute-done((bf16[128,512]{1,0:T(8,128)(2,1)S(1)}, bf16[128,512]{1,0:T(8,128)(2,1)S(1)}, u32[]{:S(2)}, u32[]{:S(2)}) %collective-permute-start.9) | collective-permute-done | bytes 131104 | tf_op jit(solution)/shard_map/ppermute | solution.py:299
  50.7 1.4 %collective-permute-done.11.refs_0_ = bf16[128,512]{1,0:T(8,128)(2,1)S(1)} collective-permute-done((bf16[128,512]{1,0:T(8,128)(2,1)S(1)}, bf16[128,512]{1,0:T(8,128)(2,1)S(1)}, u32[]{:S(2)}, u32[]{:S(2)}) %collective-permute-start.11) | collective-permute-done | bytes 131104 | tf_op jit(solution)/shard_map/ppermute | solution.py:299
  52.1 1.4 %answer.3 = bf16[128,4,512]{2,1,0:T(4,128)(2,1)} custom-call(s32[4,128]{1,0:T(4,128)S(1)} %broadcast_xor_fusion.1.offset_ref, bf16[128,512]{1,0:T(8,128)(2,1)S(1)} %collective-permute-done.11.refs_0_, bf16[128,512]{1,0:T(8,128)(2,1)S(1)} %collective-permute-done.9.refs_1_, bf16[128,2048]{1,0:T(8,128)(2,1)S(1)} %answer.2.refs_2_), custom_call_target="tpu_custom_call" | custom-call | tf_op jit(solution)/shard_map/answer/pallas_call | solution.py:282
  (35 shorter events, 6.9 us)
Async XLA Ops:
  0.0 12.8 %collective-permute-start.2 = (bf16[1024,1024]{1,0:T(8,128)(2,1)}, bf16[1024,1024]{1,0:T(8,128)(2,1)S(1)}, u32[]{:S(2)}, u32[]{:S(2)}) collective-permute-start(bf16[1024,1024]{1,0:T(8,128)(2,1)} %bitcast.8), channel_id=1, source_target_pairs={{0,1},{1,0},{2,3},{3,2},{4,5},{5,4},{6,7},{7,6},{8,9},{9,8},{10,11... | collective-permute-start | bytes 6291464 | tf_op jit(solution)/shard_map/ppermute | solution.py:312
  0.5 17.1 %collective-permute-start = (bf16[128,1024]{1,0:T(8,128)(2,1)}, bf16[128,1024]{1,0:T(8,128)(2,1)S(1)}, u32[]{:S(2)}, u32[]{:S(2)}) collective-permute-start(bf16[128,1024]{1,0:T(8,128)(2,1)} %queries_ref.1), channel_id=1, source_target_pairs={{0,8},{2,10},{4,12},{6,14},{8,0},{10,2},{12,4},{14,6},{1,9},{3,11}... | collective-permute-start | bytes 786440 | tf_op jit(solution)/shard_map/ppermute | solution.py:299
  4.0 0.7 %copy-start.3 = (s32[128,4]{0,1:T(4,128)S(1)}, s32[128,4]{0,1:T(4,128)}, u32[]{:S(2)}) copy-start(s32[128,4]{0,1:T(4,128)} %param.5) | copy-start | bytes 6148
  4.7 0.7 %copy-start.5 = (s32[128,4,4]{0,2,1:T(4,128)S(1)}, s32[128,4,4]{0,2,1:T(4,128)}, u32[]{:S(2)}) copy-start(s32[128,4,4]{0,2,1:T(4,128)} %param.6) | copy-start | bytes 24580
  5.4 0.9 %copy-start.2 = (bf16[128,1024]{1,0:T(8,128)(2,1)S(1)}, bf16[128,1024]{1,0:T(8,128)(2,1)}, u32[]{:S(2)}) copy-start(bf16[128,1024]{1,0:T(8,128)(2,1)} %queries_ref.1) | copy-start | bytes 786436
  6.4 8.9 %collective-permute-start.1 = (bf16[136,1024]{1,0:T(8,128)(2,1)S(1)}, bf16[136,1024]{1,0:T(8,128)(2,1)S(1)}, u32[]{:S(2)}, u32[]{:S(2)}) collective-permute-start(bf16[136,1024]{1,0:T(8,128)(2,1)S(1)} %pack.2.refs_0_), channel_id=1, source_target_pairs={{0,2},{2,0},{4,6},{6,4},{8,10},{10,8},{12,14},{14,12},{1,3},{3,1},... | collective-permute-start | bytes 835592 | tf_op jit(solution)/shard_map/ppermute | solution.py:299
  8.0 14.2 %collective-permute-start.5 = (bf16[136,1024]{1,0:T(8,128)(2,1)S(1)}, bf16[136,1024]{1,0:T(8,128)(2,1)S(1)}, u32[]{:S(2)}, u32[]{:S(2)}) collective-permute-start(bf16[136,1024]{1,0:T(8,128)(2,1)S(1)} %pack.2.refs_0_), channel_id=1, source_target_pairs={{0,4},{2,6},{4,0},{6,2},{8,12},{10,14},{12,8},{14,10},{1,5},{3,7},... | collective-permute-start | bytes 835592 | tf_op jit(solution)/shard_map/ppermute | solution.py:299
  9.5 1.6 %copy-start = (bf16[1,1024,1024]{2,1,0:T(8,128)(2,1)S(1)}, bf16[1,1024,1024]{2,1,0:T(8,128)(2,1)}, u32[]{:S(2)}) copy-start(bf16[1,1024,1024]{2,1,0:T(8,128)(2,1)} %param.7) | copy-start | bytes 6291460
  12.4 5.1 %collective-permute-start.3 = (bf16[32,128]{1,0:T(8,128)(2,1)S(1)}, bf16[32,128]{1,0:T(8,128)(2,1)S(1)}, u32[]{:S(2)}, u32[]{:S(2)}) collective-permute-start(bf16[32,128]{1,0:T(8,128)(2,1)S(1)} %list_ids.1.ids_ref), channel_id=1, source_target_pairs={{0,8},{2,10},{4,12},{6,14},{8,0},{10,2},{12,4},{14,6},{1,9},{3,11}... | collective-permute-start | bytes 24584 | tf_op jit(solution)/shard_map/ppermute | solution.py:299
  12.8 2.4 %copy-start.1 = (bf16[1,1024,1024]{2,1,0:T(8,128)(2,1)S(1)}, bf16[1,1024,1024]{2,1,0:T(8,128)(2,1)}, u32[]{:S(2)}) copy-start(bf16[1,1024,1024]{2,1,0:T(8,128)(2,1)} %param.7) | copy-start | bytes 6291460
  17.6 10.8 %collective-permute-start.4 = (bf16[136,1024]{1,0:T(8,128)(2,1)S(1)}, bf16[136,1024]{1,0:T(8,128)(2,1)S(1)}, u32[]{:S(2)}, u32[]{:S(2)}) collective-permute-start(bf16[136,1024]{1,0:T(8,128)(2,1)S(1)} %pack.3.refs_0_), channel_id=1, source_target_pairs={{0,4},{2,6},{4,0},{6,2},{8,12},{10,14},{12,8},{14,10},{1,5},{3,7},... | collective-permute-start | bytes 835592 | tf_op jit(solution)/shard_map/ppermute | solution.py:299
  19.2 10.3 %collective-permute-start.12 = (bf16[136,1024]{1,0:T(8,128)(2,1)S(1)}, bf16[136,1024]{1,0:T(8,128)(2,1)S(1)}, u32[]{:S(2)}, u32[]{:S(2)}) collective-permute-start(bf16[136,1024]{1,0:T(8,128)(2,1)S(1)} %pack.3.refs_0_), channel_id=1, source_target_pairs={{0,2},{2,0},{4,6},{6,4},{8,10},{10,8},{12,14},{14,12},{1,3},{3,1},... | collective-permute-start | bytes 835592 | tf_op jit(solution)/shard_map/ppermute | solution.py:299
  24.4 10.5 %collective-permute-start.7 = (bf16[128,512]{1,0:T(8,128)(2,1)S(1)}, bf16[128,512]{1,0:T(8,128)(2,1)S(1)}, u32[]{:S(2)}, u32[]{:S(2)}) collective-permute-start(bf16[128,512]{1,0:T(8,128)(2,1)S(1)} %get-tuple-element.32), channel_id=1, source_target_pairs={{0,8},{2,10},{4,12},{6,14},{8,0},{10,2},{12,4},{14,6},{1,9},{3,11}... | collective-permute-start | bytes 393224 | tf_op jit(solution)/shard_map/ppermute | solution.py:299
  25.2 10.3 %collective-permute-start.8 = (bf16[128,512]{1,0:T(8,128)(2,1)S(1)}, bf16[128,512]{1,0:T(8,128)(2,1)S(1)}, u32[]{:S(2)}, u32[]{:S(2)}) collective-permute-start(bf16[128,512]{1,0:T(8,128)(2,1)S(1)} %get-tuple-element.34), channel_id=1, source_target_pairs={{0,2},{2,0},{4,6},{6,4},{8,10},{10,8},{12,14},{14,12},{1,3},{3,1},... | collective-permute-start | bytes 393224 | tf_op jit(solution)/shard_map/ppermute | solution.py:299
  28.3 9.6 %collective-permute-start.6 = (bf16[136,1024]{1,0:T(8,128)(2,1)S(1)}, bf16[136,1024]{1,0:T(8,128)(2,1)S(1)}, u32[]{:S(2)}, u32[]{:S(2)}) collective-permute-start(bf16[136,1024]{1,0:T(8,128)(2,1)S(1)} %collective-permute-done.4.refs_1_), channel_id=1, source_target_pairs={{0,2},{2,0},{4,6},{6,4},{8,10},{10,8},{12,14},{14,12},{1,3},{3,1},... | collective-permute-start | bytes 835592 | tf_op jit(solution)/shard_map/ppermute | solution.py:299
  29.2 14.6 %collective-permute-start.10 = (bf16[136,1024]{1,0:T(8,128)(2,1)S(1)}, bf16[136,1024]{1,0:T(8,128)(2,1)S(1)}, u32[]{:S(2)}, u32[]{:S(2)}) collective-permute-start(bf16[136,1024]{1,0:T(8,128)(2,1)S(1)} %collective-permute-done.1.refs_1_), channel_id=1, source_target_pairs={{0,4},{2,6},{4,0},{6,2},{8,12},{10,14},{12,8},{14,10},{1,5},{3,7},... | collective-permute-start | bytes 835592 | tf_op jit(solution)/shard_map/ppermute | solution.py:299
  31.7 14.4 %collective-permute-start.14 = (bf16[128,512]{1,0:T(8,128)(2,1)S(1)}, bf16[128,512]{1,0:T(8,128)(2,1)S(1)}, u32[]{:S(2)}, u32[]{:S(2)}) collective-permute-start(bf16[128,512]{1,0:T(8,128)(2,1)S(1)} %get-tuple-element.43), channel_id=1, source_target_pairs={{0,10},{2,8},{4,14},{6,12},{8,2},{10,0},{12,6},{14,4},{1,11},{3,9}... | collective-permute-start | bytes 393224 | tf_op jit(solution)/shard_map/ppermute | solution.py:299
  34.8 11.3 %collective-permute-start.13 = (bf16[128,512]{1,0:T(8,128)(2,1)S(1)}, bf16[128,512]{1,0:T(8,128)(2,1)S(1)}, u32[]{:S(2)}, u32[]{:S(2)}) collective-permute-start(bf16[128,512]{1,0:T(8,128)(2,1)S(1)} %get-tuple-element.44), channel_id=1, source_target_pairs={{0,4},{2,6},{4,0},{6,2},{8,12},{10,14},{12,8},{14,10},{1,5},{3,7},... | collective-permute-start | bytes 393224 | tf_op jit(solution)/shard_map/ppermute | solution.py:299
  35.5 8.3 %copy-start.4 = (s32[128,4]{0,1:T(4,128)S(1)}, s32[128,4]{0,1:T(4,128)}, u32[]{:S(2)}) copy-start(s32[128,4]{0,1:T(4,128)} %param.5) | copy-start | bytes 6148
  35.5 13.2 %collective-permute-start.15 = (bf16[128,512]{1,0:T(8,128)(2,1)S(1)}, bf16[128,512]{1,0:T(8,128)(2,1)S(1)}, u32[]{:S(2)}, u32[]{:S(2)}) collective-permute-start(bf16[128,512]{1,0:T(8,128)(2,1)S(1)} %get-tuple-element.46), channel_id=1, source_target_pairs={{0,12},{2,14},{4,8},{6,10},{8,4},{10,6},{12,0},{14,2},{1,13},{3,15... | collective-permute-start | bytes 393224 | tf_op jit(solution)/shard_map/ppermute | solution.py:299
  40.1 10.6 %collective-permute-start.9 = (bf16[128,512]{1,0:T(8,128)(2,1)S(1)}, bf16[128,512]{1,0:T(8,128)(2,1)S(1)}, u32[]{:S(2)}, u32[]{:S(2)}) collective-permute-start(bf16[128,512]{1,0:T(8,128)(2,1)S(1)} %score.7), channel_id=1, source_target_pairs={{0,14},{2,12},{4,10},{6,8},{8,6},{10,4},{12,2},{14,0},{1,15},{3,13... | collective-permute-start | bytes 393224 | tf_op jit(solution)/shard_map/ppermute | solution.py:299
  46.0 6.1 %collective-permute-start.11 = (bf16[128,512]{1,0:T(8,128)(2,1)S(1)}, bf16[128,512]{1,0:T(8,128)(2,1)S(1)}, u32[]{:S(2)}, u32[]{:S(2)}) collective-permute-start(bf16[128,512]{1,0:T(8,128)(2,1)S(1)} %score.8), channel_id=1, source_target_pairs={{0,6},{2,4},{4,2},{6,0},{8,14},{10,12},{12,10},{14,8},{1,7},{3,5},... | collective-permute-start | bytes 393224 | tf_op jit(solution)/shard_map/ppermute | solution.py:299

commit v4 on v3

--- a/solution.py
+++ b/solution.py
@@ -313,7 +313,7 @@
     factor = -0.5 / math.sqrt(width)
     (own_bias,) = norms(own, factor, False)
     other_bias, other = norms(other, factor, True)
-    late_ids, own_bias = lax.optimization_barrier((ids, own_bias))
+    late_ids, own_bias, other_bias = lax.optimization_barrier((ids, own_bias, other_bias))
     ids_4 = hop(late_ids, 4)
 
     def scored(*keys, weight=1):
@@ -335,9 +335,9 @@
     held[6], held[1], results[4] = barrier((held[6], held[1], results[4]))
     held[7] = hop(held[6], 1)
     held[3] = hop(held[1], 2)
-    results[5], results[6] = scored(5, 6, weight=W56)
+    results[6], results[5] = scored(6, 5, weight=W56)
+    back[6] = hop(results[6], 6)
     back[5] = hop(results[5], 5)
-    back[6] = hop(results[6], 6)
     results[2], results[5] = barrier((results[2], results[5]))
     back[2] = hop(results[2], 2)
     held[7], back[4], back[1] = barrier((held[7], back[4], back[1]))

time: 53.8 us -> 53.5 us (level)
  starting transfers between devices: 22.1 us -> 20.7 us
  waiting for transfers between devices: 11.5 us -> 12.8 us
    ppermute x15, starting transfers between devices: 21.7 us -> 20.2 us  [hop(): lax.ppermute(value, 'region', [(r, r ^ mask) for r in range(regions)])]
    ppermute x15, waiting for transfers between devices: 11.5 us -> 12.8 us  [hop(): lax.ppermute(value, 'region', [(r, r ^ mask) for r in range(regions)])]
  transfers between devices with their start and end apart: 16 -> 16, of which waited for: 7 -> 8; matrix products, arithmetic and copies ran while one was open for 0% -> 0% of each run, Pallas kernels for 27% -> 27%
where the time goes in v4:
time: 53.5 us; the launch traced here: 53.3 us
  starting transfers between devices  20.7 us (39%)
  Pallas kernels  15.7 us (29%)
  waiting for transfers between devices  12.8 us (24%)
  local copies, waits for them, and re-layouts  3.92 us (7%)
    ppermute x15, starting transfers between devices, hop(): lax.ppermute(value, 'region', [(r, r ^ mask) for r in range(regions)])  20.2 us
    ppermute x15, waiting for transfers between devices, hop(): lax.ppermute(value, 'region', [(r, r ^ mask) for r in range(regions)])  12.8 us
    pallas_call x5, Pallas kernels, score(): pl.pallas_call(functools.partial(score_kernel, n_sets, q_count, probe_cou...  11.2 us
    unnamed x12, local copies, waits for them, and re-layouts  3.92 us
    pallas_call x2, Pallas kernels, norms(): pl.pallas_call(functools.partial(norms_kernel, scale), out_shape=shapes,...  2.57 us
    pallas_call x2, Pallas kernels, answer(): pl.pallas_call(functools.partial(answer_kernel, names), out_shape=jax.Sha...  1.95 us
  transfers between devices with their start and end apart: 16, of which 8 were waited for; matrix products, arithmetic and copies ran while one was open for 0% of the time, Pallas kernels for 27%

profile of v4, /device:TPU:0, one launch (start us, length us, event | category | flops | bytes accessed | tf_op | source)
XLA Modules:
  0.0 53.3 jit_solution(13693152767161052627)
XLA Ops:
  0.5 3.6 %collective-permute-start = (bf16[128,1024]{1,0:T(8,128)(2,1)}, bf16[128,1024]{1,0:T(8,128)(2,1)S(1)}, u32[]{:S(2)}, u32[]{:S(2)}) collective-permute-start(bf16[128,1024]{1,0:T(8,128)(2,1)} %queries_ref.1), channel_id=1, source_target_pairs={{0,8},{2,10},{4,12},{6,14},{8,0},{10,2},{12,4},{14,6},{1,9},{3,11}... | collective-permute-start | bytes 786440 | tf_op jit(solution)/shard_map/ppermute | solution.py:299
  5.4 0.9 %copy-done.2 = bf16[128,1024]{1,0:T(8,128)(2,1)S(1)} copy-done((bf16[128,1024]{1,0:T(8,128)(2,1)S(1)}, bf16[128,1024]{1,0:T(8,128)(2,1)}, u32[]{:S(2)}) %copy-start.2) | copy-done | bytes 262168
  6.4 1.6 %collective-permute-start.1 = (bf16[136,1024]{1,0:T(8,128)(2,1)S(1)}, bf16[136,1024]{1,0:T(8,128)(2,1)S(1)}, u32[]{:S(2)}, u32[]{:S(2)}) collective-permute-start(bf16[136,1024]{1,0:T(8,128)(2,1)S(1)} %pack.2.refs_0_), channel_id=1, source_target_pairs={{0,2},{2,0},{4,6},{6,4},{8,10},{10,8},{12,14},{14,12},{1,3},{3,1},... | collective-permute-start | bytes 835592 | tf_op jit(solution)/shard_map/ppermute | solution.py:299
  8.0 1.6 %collective-permute-start.5 = (bf16[136,1024]{1,0:T(8,128)(2,1)S(1)}, bf16[136,1024]{1,0:T(8,128)(2,1)S(1)}, u32[]{:S(2)}, u32[]{:S(2)}) collective-permute-start(bf16[136,1024]{1,0:T(8,128)(2,1)S(1)} %pack.2.refs_0_), channel_id=1, source_target_pairs={{0,4},{2,6},{4,0},{6,2},{8,12},{10,14},{12,8},{14,10},{1,5},{3,7},... | collective-permute-start | bytes 835592 | tf_op jit(solution)/shard_map/ppermute | solution.py:299
  9.6 1.6 %copy-done = bf16[1,1024,1024]{2,1,0:T(8,128)(2,1)S(1)} copy-done((bf16[1,1024,1024]{2,1,0:T(8,128)(2,1)S(1)}, bf16[1,1024,1024]{2,1,0:T(8,128)(2,1)}, u32[]{:S(2)}) %copy-start) | copy-done | bytes 2097176
  11.2 1.3 %norms.3.refs_4_.refs_3_ = f32[1,1024]{1,0:T(1,128)S(1)} custom-call(bf16[1024,1024]{1,0:T(8,128)(2,1)S(1)} %bitcast.9), custom_call_target="tpu_custom_call" | custom-call | flops 4000000000 | bytes 2097152 | tf_op jit(solution)/shard_map/norms/pallas_call | solution.py:167
  12.5 1.3 %norms.2 = (f32[1,1024]{1,0:T(1,128)S(1)}, bf16[1024,1024]{1,0:T(8,128)(2,1)S(1)}) custom-call(bf16[1024,1024]{1,0:T(8,128)(2,1)S(1)} %collective-permute-done.2.rows_ref), custom_call_target="tpu_custom_call" | custom-call | flops 4000000000 | bytes 4194304 | tf_op jit(solution)/shard_map/norms/pallas_call | solution.py:167
  14.2 1.1 %collective-permute-done.1.refs_1_ = bf16[136,1024]{1,0:T(8,128)(2,1)S(1)} collective-permute-done((bf16[136,1024]{1,0:T(8,128)(2,1)S(1)}, bf16[136,1024]{1,0:T(8,128)(2,1)S(1)}, u32[]{:S(2)}, u32[]{:S(2)}) %collective-permute-start.1) | collective-permute-done | bytes 278560 | tf_op jit(solution)/shard_map/ppermute | solution.py:299
  15.3 2.3 %score.5 = (bf16[128,512]{1,0:T(8,128)(2,1)S(1)}, bf16[128,512]{1,0:T(8,128)(2,1)S(1)}) custom-call(s32[2]{0:T(128)S(1)} %pad_add_fusion.where_ref, bf16[136,1024]{1,0:T(8,128)(2,1)S(1)} %pack.2.refs_0_, bf16[136,1024]{1,0:T(8,128)(2,1)S(1)} %collective-permute-done.1.refs_1_, bf16[1024,1024]{1,0:T(8,128)(2,1)S(1)} %bitcast.10, ...), custom_call_target="tpu_custom_call" | custom-call | flops 1073741824 | bytes 4980736 | tf_op jit(solution)/shard_map/score/pallas_call | solution.py:232
  19.2 1.5 %collective-permute-start.12 = (bf16[136,1024]{1,0:T(8,128)(2,1)S(1)}, bf16[136,1024]{1,0:T(8,128)(2,1)S(1)}, u32[]{:S(2)}, u32[]{:S(2)}) collective-permute-start(bf16[136,1024]{1,0:T(8,128)(2,1)S(1)} %pack.3.refs_0_), channel_id=1, source_target_pairs={{0,2},{2,0},{4,6},{6,4},{8,10},{10,8},{12,14},{14,12},{1,3},{3,1},... | collective-permute-start | bytes 835592 | tf_op jit(solution)/shard_map/ppermute | solution.py:299
  22.1 2.2 %score.6 = (bf16[128,512]{1,0:T(8,128)(2,1)S(1)}, bf16[128,512]{1,0:T(8,128)(2,1)S(1)}) custom-call(s32[2]{0:T(128)S(1)} %pad_add_fusion.where_ref, bf16[136,1024]{1,0:T(8,128)(2,1)S(1)} %pack.3.refs_0_, bf16[136,1024]{1,0:T(8,128)(2,1)S(1)} %collective-permute-done.5.refs_1_, bf16[1024,1024]{1,0:T(8,128)(2,1)S(1)} %bitcast.11, ...), custom_call_target="tpu_custom_call" | custom-call | flops 1073741824 | bytes 4980736 | tf_op jit(solution)/shard_map/score/pallas_call | solution.py:232
  24.4 1.3 %collective-permute-start.7 = (bf16[128,512]{1,0:T(8,128)(2,1)S(1)}, bf16[128,512]{1,0:T(8,128)(2,1)S(1)}, u32[]{:S(2)}, u32[]{:S(2)}) collective-permute-start(bf16[128,512]{1,0:T(8,128)(2,1)S(1)} %get-tuple-element.34), channel_id=1, source_target_pairs={{0,8},{2,10},{4,12},{6,14},{8,0},{10,2},{12,4},{14,6},{1,9},{3,11}... | collective-permute-start | bytes 393224 | tf_op jit(solution)/shard_map/ppermute | solution.py:299
  25.7 2.6 %collective-permute-done.4.refs_0_ = bf16[136,1024]{1,0:T(8,128)(2,1)S(1)} collective-permute-done((bf16[136,1024]{1,0:T(8,128)(2,1)S(1)}, bf16[136,1024]{1,0:T(8,128)(2,1)S(1)}, u32[]{:S(2)}, u32[]{:S(2)}) %collective-permute-start.4) | collective-permute-done | bytes 278560 | tf_op jit(solution)/shard_map/ppermute | solution.py:299
  28.7 2.2 %score.9 = (bf16[128,512]{1,0:T(8,128)(2,1)S(1)}, bf16[128,512]{1,0:T(8,128)(2,1)S(1)}) custom-call(s32[2]{0:T(128)S(1)} %pad_add_fusion.where_ref, bf16[136,1024]{1,0:T(8,128)(2,1)S(1)} %collective-permute-done.4.refs_0_, bf16[136,1024]{1,0:T(8,128)(2,1)S(1)} %collective-permute-done.12.refs_1_, bf16[1024,1024]{1,0:T(8,128)(2,1)S(1)} %bitcast.12, ...), custom_call_target="tpu_custom_call" | custom-call | flops 10737418240 | bytes 4980736 | tf_op jit(solution)/shard_map/score/pallas_call | solution.py:232
  30.9 3.9 %collective-permute-start.14 = (bf16[128,512]{1,0:T(8,128)(2,1)S(1)}, bf16[128,512]{1,0:T(8,128)(2,1)S(1)}, u32[]{:S(2)}, u32[]{:S(2)}) collective-permute-start(bf16[128,512]{1,0:T(8,128)(2,1)S(1)} %get-tuple-element.45), channel_id=1, source_target_pairs={{0,10},{2,8},{4,14},{6,12},{8,2},{10,0},{12,6},{14,4},{1,11},{3,9}... | collective-permute-start | bytes 393224 | tf_op jit(solution)/shard_map/ppermute | solution.py:299
  35.5 1.1 %collective-permute-start.15 = (bf16[128,512]{1,0:T(8,128)(2,1)S(1)}, bf16[128,512]{1,0:T(8,128)(2,1)S(1)}, u32[]{:S(2)}, u32[]{:S(2)}) collective-permute-start(bf16[128,512]{1,0:T(8,128)(2,1)S(1)} %get-tuple-element.48), channel_id=1, source_target_pairs={{0,12},{2,14},{4,8},{6,10},{8,4},{10,6},{12,0},{14,2},{1,13},{3,15... | collective-permute-start | bytes 393224 | tf_op jit(solution)/shard_map/ppermute | solution.py:299
  36.6 1.2 %collective-permute-done.6.refs_0_ = bf16[136,1024]{1,0:T(8,128)(2,1)S(1)} collective-permute-done((bf16[136,1024]{1,0:T(8,128)(2,1)S(1)}, bf16[136,1024]{1,0:T(8,128)(2,1)S(1)}, u32[]{:S(2)}, u32[]{:S(2)}) %collective-permute-start.6) | collective-permute-done | bytes 278560 | tf_op jit(solution)/shard_map/ppermute | solution.py:299
  37.8 2.2 %score.7 = bf16[128,512]{1,0:T(8,128)(2,1)S(1)} custom-call(s32[2]{0:T(128)S(1)} %pad_add_fusion.where_ref, bf16[136,1024]{1,0:T(8,128)(2,1)S(1)} %collective-permute-done.6.refs_0_, bf16[1024,1024]{1,0:T(8,128)(2,1)S(1)} %bitcast.13, bf16[1024,1024]{1,0:T(8,128)(2,1)S(1)} %get-tuple-element.27.refs_3_.refs_2_, f32[1,1024]{1,0:T(1,128)S(1)} %norms.3.refs_4_.refs_3_, ...), custom_call_target="tpu_custom_call" | custom-call | flops 536870912 | bytes 4587520 | tf_op jit(solution)/shard_map/score/pallas_call | solution.py:232
  40.0 3.0 %collective-permute-start.9 = (bf16[128,512]{1,0:T(8,128)(2,1)S(1)}, bf16[128,512]{1,0:T(8,128)(2,1)S(1)}, u32[]{:S(2)}, u32[]{:S(2)}) collective-permute-start(bf16[128,512]{1,0:T(8,128)(2,1)S(1)} %score.7), channel_id=1, source_target_pairs={{0,14},{2,12},{4,10},{6,8},{8,6},{10,4},{12,2},{14,0},{1,15},{3,13... | collective-permute-start | bytes 393224 | tf_op jit(solution)/shard_map/ppermute | solution.py:299
  43.0 2.2 %score.8 = bf16[128,512]{1,0:T(8,128)(2,1)S(1)} custom-call(s32[2]{0:T(128)S(1)} %pad_add_fusion.where_ref, bf16[136,1024]{1,0:T(8,128)(2,1)S(1)} %collective-permute-done.10.refs_0_, bf16[1024,1024]{1,0:T(8,128)(2,1)S(1)} %bitcast.14, bf16[1024,1024]{1,0:T(8,128)(2,1)S(1)} %get-tuple-element.27.refs_3_.refs_2_, f32[1,1024]{1,0:T(1,128)S(1)} %norms.3.refs_4_.refs_3_, ...), custom_call_target="tpu_custom_call" | custom-call | flops 536870912 | bytes 4587520 | tf_op jit(solution)/shard_map/score/pallas_call | solution.py:232
  45.3 3.3 %collective-permute-done.15.refs_5_ = bf16[128,512]{1,0:T(8,128)(2,1)S(1)} collective-permute-done((bf16[128,512]{1,0:T(8,128)(2,1)S(1)}, bf16[128,512]{1,0:T(8,128)(2,1)S(1)}, u32[]{:S(2)}, u32[]{:S(2)}) %collective-permute-start.15) | collective-permute-done | bytes 131104 | tf_op jit(solution)/shard_map/ppermute | solution.py:299
  49.2 1.3 %collective-permute-done.9.refs_1_ = bf16[128,512]{1,0:T(8,128)(2,1)S(1)} collective-permute-done((bf16[128,512]{1,0:T(8,128)(2,1)S(1)}, bf16[128,512]{1,0:T(8,128)(2,1)S(1)}, u32[]{:S(2)}, u32[]{:S(2)}) %collective-permute-start.9) | collective-permute-done | bytes 131104 | tf_op jit(solution)/shard_map/ppermute | solution.py:299
  50.5 1.4 %collective-permute-done.11.refs_0_ = bf16[128,512]{1,0:T(8,128)(2,1)S(1)} collective-permute-done((bf16[128,512]{1,0:T(8,128)(2,1)S(1)}, bf16[128,512]{1,0:T(8,128)(2,1)S(1)}, u32[]{:S(2)}, u32[]{:S(2)}) %collective-permute-start.11) | collective-permute-done | bytes 131104 | tf_op jit(solution)/shard_map/ppermute | solution.py:299
  51.9 1.4 %answer.3 = bf16[128,4,512]{2,1,0:T(4,128)(2,1)} custom-call(s32[4,128]{1,0:T(4,128)S(1)} %broadcast_xor_fusion.1.offset_ref, bf16[128,512]{1,0:T(8,128)(2,1)S(1)} %collective-permute-done.11.refs_0_, bf16[128,512]{1,0:T(8,128)(2,1)S(1)} %collective-permute-done.9.refs_1_, bf16[128,2048]{1,0:T(8,128)(2,1)S(1)} %answer.2.refs_2_), custom_call_target="tpu_custom_call" | custom-call | tf_op jit(solution)/shard_map/answer/pallas_call | solution.py:282
  (35 shorter events, 7.0 us)
Async XLA Ops:
  0.0 12.5 %collective-permute-start.2 = (bf16[1024,1024]{1,0:T(8,128)(2,1)}, bf16[1024,1024]{1,0:T(8,128)(2,1)S(1)}, u32[]{:S(2)}, u32[]{:S(2)}) collective-permute-start(bf16[1024,1024]{1,0:T(8,128)(2,1)} %bitcast.8), channel_id=1, source_target_pairs={{0,1},{1,0},{2,3},{3,2},{4,5},{5,4},{6,7},{7,6},{8,9},{9,8},{10,11... | collective-permute-start | bytes 6291464 | tf_op jit(solution)/shard_map/ppermute | solution.py:312
  0.5 17.1 %collective-permute-start = (bf16[128,1024]{1,0:T(8,128)(2,1)}, bf16[128,1024]{1,0:T(8,128)(2,1)S(1)}, u32[]{:S(2)}, u32[]{:S(2)}) collective-permute-start(bf16[128,1024]{1,0:T(8,128)(2,1)} %queries_ref.1), channel_id=1, source_target_pairs={{0,8},{2,10},{4,12},{6,14},{8,0},{10,2},{12,4},{14,6},{1,9},{3,11}... | collective-permute-start | bytes 786440 | tf_op jit(solution)/shard_map/ppermute | solution.py:299
  4.0 0.7 %copy-start.3 = (s32[128,4]{0,1:T(4,128)S(1)}, s32[128,4]{0,1:T(4,128)}, u32[]{:S(2)}) copy-start(s32[128,4]{0,1:T(4,128)} %param.5) | copy-start | bytes 6148
  4.7 0.7 %copy-start.5 = (s32[128,4,4]{0,2,1:T(4,128)S(1)}, s32[128,4,4]{0,2,1:T(4,128)}, u32[]{:S(2)}) copy-start(s32[128,4,4]{0,2,1:T(4,128)} %param.6) | copy-start | bytes 24580
  5.4 0.9 %copy-start.2 = (bf16[128,1024]{1,0:T(8,128)(2,1)S(1)}, bf16[128,1024]{1,0:T(8,128)(2,1)}, u32[]{:S(2)}) copy-start(bf16[128,1024]{1,0:T(8,128)(2,1)} %queries_ref.1) | copy-start | bytes 786436
  6.4 8.9 %collective-permute-start.1 = (bf16[136,1024]{1,0:T(8,128)(2,1)S(1)}, bf16[136,1024]{1,0:T(8,128)(2,1)S(1)}, u32[]{:S(2)}, u32[]{:S(2)}) collective-permute-start(bf16[136,1024]{1,0:T(8,128)(2,1)S(1)} %pack.2.refs_0_), channel_id=1, source_target_pairs={{0,2},{2,0},{4,6},{6,4},{8,10},{10,8},{12,14},{14,12},{1,3},{3,1},... | collective-permute-start | bytes 835592 | tf_op jit(solution)/shard_map/ppermute | solution.py:299
  8.0 14.2 %collective-permute-start.5 = (bf16[136,1024]{1,0:T(8,128)(2,1)S(1)}, bf16[136,1024]{1,0:T(8,128)(2,1)S(1)}, u32[]{:S(2)}, u32[]{:S(2)}) collective-permute-start(bf16[136,1024]{1,0:T(8,128)(2,1)S(1)} %pack.2.refs_0_), channel_id=1, source_target_pairs={{0,4},{2,6},{4,0},{6,2},{8,12},{10,14},{12,8},{14,10},{1,5},{3,7},... | collective-permute-start | bytes 835592 | tf_op jit(solution)/shard_map/ppermute | solution.py:299
  9.6 1.6 %copy-start = (bf16[1,1024,1024]{2,1,0:T(8,128)(2,1)S(1)}, bf16[1,1024,1024]{2,1,0:T(8,128)(2,1)}, u32[]{:S(2)}) copy-start(bf16[1,1024,1024]{2,1,0:T(8,128)(2,1)} %param.7) | copy-start | bytes 6291460
  12.5 2.8 %copy-start.1 = (bf16[1,1024,1024]{2,1,0:T(8,128)(2,1)S(1)}, bf16[1,1024,1024]{2,1,0:T(8,128)(2,1)}, u32[]{:S(2)}) copy-start(bf16[1,1024,1024]{2,1,0:T(8,128)(2,1)} %param.7) | copy-start | bytes 6291460
  13.8 4.7 %collective-permute-start.3 = (bf16[32,128]{1,0:T(8,128)(2,1)S(1)}, bf16[32,128]{1,0:T(8,128)(2,1)S(1)}, u32[]{:S(2)}, u32[]{:S(2)}) collective-permute-start(bf16[32,128]{1,0:T(8,128)(2,1)S(1)} %list_ids.1.ids_ref), channel_id=1, source_target_pairs={{0,8},{2,10},{4,12},{6,14},{8,0},{10,2},{12,4},{14,6},{1,9},{3,11}... | collective-permute-start | bytes 24584 | tf_op jit(solution)/shard_map/ppermute | solution.py:299
  18.5 9.8 %collective-permute-start.4 = (bf16[136,1024]{1,0:T(8,128)(2,1)S(1)}, bf16[136,1024]{1,0:T(8,128)(2,1)S(1)}, u32[]{:S(2)}, u32[]{:S(2)}) collective-permute-start(bf16[136,1024]{1,0:T(8,128)(2,1)S(1)} %pack.3.refs_0_), channel_id=1, source_target_pairs={{0,4},{2,6},{4,0},{6,2},{8,12},{10,14},{12,8},{14,10},{1,5},{3,7},... | collective-permute-start | bytes 835592 | tf_op jit(solution)/shard_map/ppermute | solution.py:299
  19.2 9.5 %collective-permute-start.12 = (bf16[136,1024]{1,0:T(8,128)(2,1)S(1)}, bf16[136,1024]{1,0:T(8,128)(2,1)S(1)}, u32[]{:S(2)}, u32[]{:S(2)}) collective-permute-start(bf16[136,1024]{1,0:T(8,128)(2,1)S(1)} %pack.3.refs_0_), channel_id=1, source_target_pairs={{0,2},{2,0},{4,6},{6,4},{8,10},{10,8},{12,14},{14,12},{1,3},{3,1},... | collective-permute-start | bytes 835592 | tf_op jit(solution)/shard_map/ppermute | solution.py:299
  20.7 14.1 %collective-permute-start.8 = (bf16[128,512]{1,0:T(8,128)(2,1)S(1)}, bf16[128,512]{1,0:T(8,128)(2,1)S(1)}, u32[]{:S(2)}, u32[]{:S(2)}) collective-permute-start(bf16[128,512]{1,0:T(8,128)(2,1)S(1)} %get-tuple-element.36), channel_id=1, source_target_pairs={{0,2},{2,0},{4,6},{6,4},{8,10},{10,8},{12,14},{14,12},{1,3},{3,1},... | collective-permute-start | bytes 393224 | tf_op jit(solution)/shard_map/ppermute | solution.py:299
  24.4 11.1 %collective-permute-start.7 = (bf16[128,512]{1,0:T(8,128)(2,1)S(1)}, bf16[128,512]{1,0:T(8,128)(2,1)S(1)}, u32[]{:S(2)}, u32[]{:S(2)}) collective-permute-start(bf16[128,512]{1,0:T(8,128)(2,1)S(1)} %get-tuple-element.34), channel_id=1, source_target_pairs={{0,8},{2,10},{4,12},{6,14},{8,0},{10,2},{12,4},{14,6},{1,9},{3,11}... | collective-permute-start | bytes 393224 | tf_op jit(solution)/shard_map/ppermute | solution.py:299
  28.3 9.5 %collective-permute-start.6 = (bf16[136,1024]{1,0:T(8,128)(2,1)S(1)}, bf16[136,1024]{1,0:T(8,128)(2,1)S(1)}, u32[]{:S(2)}, u32[]{:S(2)}) collective-permute-start(bf16[136,1024]{1,0:T(8,128)(2,1)S(1)} %collective-permute-done.4.refs_0_), channel_id=1, source_target_pairs={{0,2},{2,0},{4,6},{6,4},{8,10},{10,8},{12,14},{14,12},{1,3},{3,1},... | collective-permute-start | bytes 835592 | tf_op jit(solution)/shard_map/ppermute | solution.py:299
  28.4 14.6 %collective-permute-start.10 = (bf16[136,1024]{1,0:T(8,128)(2,1)S(1)}, bf16[136,1024]{1,0:T(8,128)(2,1)S(1)}, u32[]{:S(2)}, u32[]{:S(2)}) collective-permute-start(bf16[136,1024]{1,0:T(8,128)(2,1)S(1)} %collective-permute-done.1.refs_1_), channel_id=1, source_target_pairs={{0,4},{2,6},{4,0},{6,2},{8,12},{10,14},{12,8},{14,10},{1,5},{3,7},... | collective-permute-start | bytes 835592 | tf_op jit(solution)/shard_map/ppermute | solution.py:299
  30.9 14.4 %collective-permute-start.14 = (bf16[128,512]{1,0:T(8,128)(2,1)S(1)}, bf16[128,512]{1,0:T(8,128)(2,1)S(1)}, u32[]{:S(2)}, u32[]{:S(2)}) collective-permute-start(bf16[128,512]{1,0:T(8,128)(2,1)S(1)} %get-tuple-element.45), channel_id=1, source_target_pairs={{0,10},{2,8},{4,14},{6,12},{8,2},{10,0},{12,6},{14,4},{1,11},{3,9}... | collective-permute-start | bytes 393224 | tf_op jit(solution)/shard_map/ppermute | solution.py:299
  34.8 10.5 %collective-permute-start.13 = (bf16[128,512]{1,0:T(8,128)(2,1)S(1)}, bf16[128,512]{1,0:T(8,128)(2,1)S(1)}, u32[]{:S(2)}, u32[]{:S(2)}) collective-permute-start(bf16[128,512]{1,0:T(8,128)(2,1)S(1)} %get-tuple-element.46), channel_id=1, source_target_pairs={{0,4},{2,6},{4,0},{6,2},{8,12},{10,14},{12,8},{14,10},{1,5},{3,7},... | collective-permute-start | bytes 393224 | tf_op jit(solution)/shard_map/ppermute | solution.py:299
  35.5 7.5 %copy-start.4 = (s32[128,4]{0,1:T(4,128)S(1)}, s32[128,4]{0,1:T(4,128)}, u32[]{:S(2)}) copy-start(s32[128,4]{0,1:T(4,128)} %param.5) | copy-start | bytes 6148
  35.5 13.2 %collective-permute-start.15 = (bf16[128,512]{1,0:T(8,128)(2,1)S(1)}, bf16[128,512]{1,0:T(8,128)(2,1)S(1)}, u32[]{:S(2)}, u32[]{:S(2)}) collective-permute-start(bf16[128,512]{1,0:T(8,128)(2,1)S(1)} %get-tuple-element.48), channel_id=1, source_target_pairs={{0,12},{2,14},{4,8},{6,10},{8,4},{10,6},{12,0},{14,2},{1,13},{3,15... | collective-permute-start | bytes 393224 | tf_op jit(solution)/shard_map/ppermute | solution.py:299
  40.0 10.5 %collective-permute-start.9 = (bf16[128,512]{1,0:T(8,128)(2,1)S(1)}, bf16[128,512]{1,0:T(8,128)(2,1)S(1)}, u32[]{:S(2)}, u32[]{:S(2)}) collective-permute-start(bf16[128,512]{1,0:T(8,128)(2,1)S(1)} %score.7), channel_id=1, source_target_pairs={{0,14},{2,12},{4,10},{6,8},{8,6},{10,4},{12,2},{14,0},{1,15},{3,13... | collective-permute-start | bytes 393224 | tf_op jit(solution)/shard_map/ppermute | solution.py:299
  45.2 6.7 %collective-permute-start.11 = (bf16[128,512]{1,0:T(8,128)(2,1)S(1)}, bf16[128,512]{1,0:T(8,128)(2,1)S(1)}, u32[]{:S(2)}, u32[]{:S(2)}) collective-permute-start(bf16[128,512]{1,0:T(8,128)(2,1)S(1)} %score.8), channel_id=1, source_target_pairs={{0,6},{2,4},{4,2},{6,0},{8,14},{10,12},{12,10},{14,8},{1,7},{3,5},... | collective-permute-start | bytes 393224 | tf_op jit(solution)/shard_map/ppermute | solution.py:299

commit v5 on v4

--- a/solution.py
+++ b/solution.py
@@ -86,8 +86,7 @@
     return answers.reshape(q_count, probe_count, -1)
 
 
-def choose(options, index):
-    bit = 1
+def choose(options, index, bit=1):
     while len(options) > 1:
         odd = (index & bit) != 0
         options = [
@@ -203,22 +202,35 @@
         columns.append(jnp.transpose(wanted).astype(jnp.int32) ^ (where_ref[1] * (block_total // 2)))
     rows = jnp.concatenate([r[0:q_count, :] for r in q_refs], axis=0)
     chunk = 512
-    for side, (c_ref, b_ref) in enumerate(sides):
-        for t in range(0, half, chunk):
-            inner = lax.dot_general(
-                rows,
-                c_ref[t : t + chunk, :],
-                (((1,), (1,)), ((), ())),
-                preferred_element_type=jnp.float32,
-            )
-            held[:, side * half + t : side * half + t + chunk] = inner + b_ref[:, t : t + chunk]
+    per = chunk // BLK
     step = 32
+    places = [(side, t) for side in range(2) for t in range(0, half, chunk)]
+    for i, (side, t) in enumerate(places):
+        c_ref, b_ref = sides[side]
+        inner = lax.dot_general(
+            rows,
+            c_ref[t : t + chunk, :],
+            (((1,), (1,)), ((), ())),
+            preferred_element_type=jnp.float32,
+        )
+        scored = inner + b_ref[:, t : t + chunk]
+        for s in range(n_sets):
+            for r in range(0, q_count, step):
+                row = s * q_count + r
+                options = [scored[row : row + step, b * BLK : (b + 1) * BLK] for b in range(per)]
+                for j in range(n_active):
+                    held[row : row + step, (i * n_active + j) * BLK : (i * n_active + j + 1) * BLK] = (
+                        choose(options, columns[s][r : r + step, j : j + 1])
+                    )
     for s in range(n_sets):
         for r in range(0, q_count, step):
             row = s * q_count + r
-            options = [held[row : row + step, b * BLK : (b + 1) * BLK] for b in range(block_total)]
             for j in range(n_active):
-                best = choose(options, columns[s][r : r + step, j : j + 1])
+                options = [
+                    held[row : row + step, (i * n_active + j) * BLK : (i * n_active + j + 1) * BLK]
+                    for i in range(len(places))
+                ]
+                best = choose(options, columns[s][r : r + step, j : j + 1], per)
                 out_refs[s][r : r + step, j * BLK : (j + 1) * BLK] = (best * scale).astype(
                     jnp.bfloat16
                 )
@@ -236,7 +248,9 @@
         out_shape=[out] * n_sets,
         in_specs=[pl.BlockSpec(memory_space=pltpu.SMEM)] + [in_vmem] * (n_sets + 4),
         out_specs=[in_vmem] * n_sets,
-        scratch_shapes=[pltpu.VMEM((n_sets * q_count, 2 * half), jnp.float32)],
+        scratch_shapes=[
+            pltpu.VMEM((n_sets * q_count, 2 * half // 512 * n_active * BLK), jnp.float32)
+        ],
         compiler_params=pltpu.CompilerParams(vmem_limit_bytes=24 * 1024 * 1024),
         cost_estimate=pl.CostEstimate(
             flops=weight * 2 * n_sets * q_count * 2 * half * width,
@@ -304,17 +318,16 @@
     own = centroids[0]
     probes = probes.T
     fine = fine_blocks.reshape(q_count, -1).T
-    held = {4: hop(queries, 4)}
+    held = {4: hop(queries, 4), 2: hop(queries, 2)}
     ids = list_ids(probes, fine)
     held[0] = pack(queries, ids, 8)
     held[1] = hop(held[0], 1)
-    held[2] = hop(held[0], 2)
     other = lax.ppermute(own, "narrow", [(0, 1), (1, 0)])
     factor = -0.5 / math.sqrt(width)
     (own_bias,) = norms(own, factor, False)
     other_bias, other = norms(other, factor, True)
     late_ids, own_bias, other_bias = lax.optimization_barrier((ids, own_bias, other_bias))
-    ids_4 = hop(late_ids, 4)
+    ids_4, ids_2 = hop(late_ids, 4), hop(late_ids, 2)
 
     def scored(*keys, weight=1):
         blocks = [held[k] for k in keys]
@@ -326,8 +339,9 @@
     results, back = {}, {}
     results[0], results[1] = scored(0, 1, weight=W01)
     back[1] = hop(results[1], 1)
-    held[4], results[0] = barrier((held[4], results[0]))
+    held[4], held[2], ids_2, results[0] = barrier((held[4], held[2], ids_2, results[0]))
     held[4] = pack(held[4], ids_4, 8)
+    held[2] = pack(held[2], ids_2, 8)
     held[6] = hop(held[4], 2)
     held[5] = hop(held[4], 1)
     results[4], results[2] = scored(4, 2, weight=W42)

time: 53.5 us -> 53.5 us (level)
  waiting for transfers between devices: 12.8 us -> 10 us
  starting transfers between devices: 20.7 us -> 23.3 us
    ppermute x15 -> x16, waiting for transfers between devices: 12.8 us -> 10 us  [hop(): lax.ppermute(value, 'region', [(r, r ^ mask) for r in range(regions)])]
    ppermute x15 -> x16, starting transfers between devices: 20.2 us -> 22.9 us  [hop(): lax.ppermute(value, 'region', [(r, r ^ mask) for r in range(regions)])]
  transfers between devices with their start and end apart: 16 -> 17, of which waited for: 8 -> 6; matrix products, arithmetic and copies ran while one was open for 0% -> 0% of each run, Pallas kernels for 27% -> 27%
where the time goes in v5:
time: 53.5 us; the launch traced here: 53.3 us
  starting transfers between devices  23.3 us (44%)
  Pallas kernels  15.8 us (30%)
  waiting for transfers between devices  10 us (19%)
  local copies, waits for them, and re-layouts  3.92 us (7%)
    ppermute x16, starting transfers between devices, hop(): lax.ppermute(value, 'region', [(r, r ^ mask) for r in range(regions)])  22.9 us
    pallas_call x5, Pallas kernels, score(): pl.pallas_call(functools.partial(score_kernel, n_sets, q_count, probe_cou...  11.2 us
    ppermute x16, waiting for transfers between devices, hop(): lax.ppermute(value, 'region', [(r, r ^ mask) for r in range(regions)])  10 us
    unnamed x12, local copies, waits for them, and re-layouts  3.92 us
    pallas_call x2, Pallas kernels, norms(): pl.pallas_call(functools.partial(norms_kernel, scale), out_shape=shapes,...  2.57 us
    pallas_call x2, Pallas kernels, answer(): pl.pallas_call(functools.partial(answer_kernel, names), out_shape=jax.Sha...  1.94 us
  transfers between devices with their start and end apart: 17, of which 6 were waited for; matrix products, arithmetic and copies ran while one was open for 0% of the time, Pallas kernels for 27%

profile of v5, /device:TPU:0, one launch (start us, length us, event | category | flops | bytes accessed | tf_op | source)
XLA Modules:
  0.0 53.3 jit_solution(9354177722162557014)
XLA Ops:
  0.5 3.6 %collective-permute-start = (bf16[128,1024]{1,0:T(8,128)(2,1)}, bf16[128,1024]{1,0:T(8,128)(2,1)S(1)}, u32[]{:S(2)}, u32[]{:S(2)}) collective-permute-start(bf16[128,1024]{1,0:T(8,128)(2,1)} %queries_ref.1), channel_id=1, source_target_pairs={{0,8},{2,10},{4,12},{6,14},{8,0},{10,2},{12,4},{14,6},{1,9},{3,11}... | collective-permute-start | bytes 786440 | tf_op jit(solution)/shard_map/ppermute | solution.py:313
  4.0 1.6 %collective-permute-start.1 = (bf16[128,1024]{1,0:T(8,128)(2,1)}, bf16[128,1024]{1,0:T(8,128)(2,1)S(1)}, u32[]{:S(2)}, u32[]{:S(2)}) collective-permute-start(bf16[128,1024]{1,0:T(8,128)(2,1)} %queries_ref.1), channel_id=1, source_target_pairs={{0,4},{2,6},{4,0},{6,2},{8,12},{10,14},{12,8},{14,10},{1,5},{3,7},... | collective-permute-start | bytes 786440 | tf_op jit(solution)/shard_map/ppermute | solution.py:313
  8.0 1.6 %collective-permute-start.4 = (bf16[136,1024]{1,0:T(8,128)(2,1)S(1)}, bf16[136,1024]{1,0:T(8,128)(2,1)S(1)}, u32[]{:S(2)}, u32[]{:S(2)}) collective-permute-start(bf16[136,1024]{1,0:T(8,128)(2,1)S(1)} %pack.3.refs_0_), channel_id=1, source_target_pairs={{0,2},{2,0},{4,6},{6,4},{8,10},{10,8},{12,14},{14,12},{1,3},{3,1},... | collective-permute-start | bytes 835592 | tf_op jit(solution)/shard_map/ppermute | solution.py:313
  9.6 1.6 %copy-done = bf16[1,1024,1024]{2,1,0:T(8,128)(2,1)S(1)} copy-done((bf16[1,1024,1024]{2,1,0:T(8,128)(2,1)S(1)}, bf16[1,1024,1024]{2,1,0:T(8,128)(2,1)}, u32[]{:S(2)}) %copy-start) | copy-done | bytes 2097176
  11.2 1.3 %norms.2.refs_4_.refs_3_ = f32[1,1024]{1,0:T(1,128)S(1)} custom-call(bf16[1024,1024]{1,0:T(8,128)(2,1)S(1)} %bitcast.9), custom_call_target="tpu_custom_call" | custom-call | flops 4000000000 | bytes 2097152 | tf_op jit(solution)/shard_map/norms/pallas_call | solution.py:166
  12.5 1.3 %norms.3 = (f32[1,1024]{1,0:T(1,128)S(1)}, bf16[1024,1024]{1,0:T(8,128)(2,1)S(1)}) custom-call(bf16[1024,1024]{1,0:T(8,128)(2,1)S(1)} %collective-permute-done.2.rows_ref), custom_call_target="tpu_custom_call" | custom-call | flops 4000000000 | bytes 4194304 | tf_op jit(solution)/shard_map/norms/pallas_call | solution.py:166
  14.6 1.9 %collective-permute-done.4.refs_1_ = bf16[136,1024]{1,0:T(8,128)(2,1)S(1)} collective-permute-done((bf16[136,1024]{1,0:T(8,128)(2,1)S(1)}, bf16[136,1024]{1,0:T(8,128)(2,1)S(1)}, u32[]{:S(2)}, u32[]{:S(2)}) %collective-permute-start.4) | collective-permute-done | bytes 278560 | tf_op jit(solution)/shard_map/ppermute | solution.py:313
  16.6 2.3 %score.5 = (bf16[128,512]{1,0:T(8,128)(2,1)S(1)}, bf16[128,512]{1,0:T(8,128)(2,1)S(1)}) custom-call(s32[2]{0:T(128)S(1)} %pad_add_fusion.where_ref, bf16[136,1024]{1,0:T(8,128)(2,1)S(1)} %pack.3.refs_0_, bf16[136,1024]{1,0:T(8,128)(2,1)S(1)} %collective-permute-done.4.refs_1_, bf16[1024,1024]{1,0:T(8,128)(2,1)S(1)} %bitcast.10, ...), custom_call_target="tpu_custom_call" | custom-call | flops 1073741824 | bytes 4980736 | tf_op jit(solution)/shard_map/score/pallas_call | solution.py:244
  18.9 1.6 %collective-permute-start.6 = (bf16[136,1024]{1,0:T(8,128)(2,1)S(1)}, bf16[136,1024]{1,0:T(8,128)(2,1)S(1)}, u32[]{:S(2)}, u32[]{:S(2)}) collective-permute-start(bf16[136,1024]{1,0:T(8,128)(2,1)S(1)} %pack.4.refs_0_), channel_id=1, source_target_pairs={{0,4},{2,6},{4,0},{6,2},{8,12},{10,14},{12,8},{14,10},{1,5},{3,7},... | collective-permute-start | bytes 835592 | tf_op jit(solution)/shard_map/ppermute | solution.py:313
  21.0 1.5 %collective-permute-start.9 = (bf16[128,512]{1,0:T(8,128)(2,1)S(1)}, bf16[128,512]{1,0:T(8,128)(2,1)S(1)}, u32[]{:S(2)}, u32[]{:S(2)}) collective-permute-start(bf16[128,512]{1,0:T(8,128)(2,1)S(1)} %get-tuple-element.40), channel_id=1, source_target_pairs={{0,2},{2,0},{4,6},{6,4},{8,10},{10,8},{12,14},{14,12},{1,3},{3,1},... | collective-permute-start | bytes 393224 | tf_op jit(solution)/shard_map/ppermute | solution.py:313
  22.5 2.2 %score.6 = (bf16[128,512]{1,0:T(8,128)(2,1)S(1)}, bf16[128,512]{1,0:T(8,128)(2,1)S(1)}) custom-call(s32[2]{0:T(128)S(1)} %pad_add_fusion.where_ref, bf16[136,1024]{1,0:T(8,128)(2,1)S(1)} %pack.4.refs_0_, bf16[136,1024]{1,0:T(8,128)(2,1)S(1)} %pack.5.refs_1_, bf16[1024,1024]{1,0:T(8,128)(2,1)S(1)} %bitcast.11, ...), custom_call_target="tpu_custom_call" | custom-call | flops 1073741824 | bytes 4980736 | tf_op jit(solution)/shard_map/score/pallas_call | solution.py:244
  24.8 1.0 %collective-permute-start.8 = (bf16[128,512]{1,0:T(8,128)(2,1)S(1)}, bf16[128,512]{1,0:T(8,128)(2,1)S(1)}, u32[]{:S(2)}, u32[]{:S(2)}) collective-permute-start(bf16[128,512]{1,0:T(8,128)(2,1)S(1)} %get-tuple-element.38), channel_id=1, source_target_pairs={{0,8},{2,10},{4,12},{6,14},{8,0},{10,2},{12,4},{14,6},{1,9},{3,11}... | collective-permute-start | bytes 393224 | tf_op jit(solution)/shard_map/ppermute | solution.py:313
  25.8 2.3 %collective-permute-done.6.refs_0_ = bf16[136,1024]{1,0:T(8,128)(2,1)S(1)} collective-permute-done((bf16[136,1024]{1,0:T(8,128)(2,1)S(1)}, bf16[136,1024]{1,0:T(8,128)(2,1)S(1)}, u32[]{:S(2)}, u32[]{:S(2)}) %collective-permute-start.6) | collective-permute-done | bytes 278560 | tf_op jit(solution)/shard_map/ppermute | solution.py:313
  28.0 1.7 %collective-permute-start.7 = (bf16[136,1024]{1,0:T(8,128)(2,1)S(1)}, bf16[136,1024]{1,0:T(8,128)(2,1)S(1)}, u32[]{:S(2)}, u32[]{:S(2)}) collective-permute-start(bf16[136,1024]{1,0:T(8,128)(2,1)S(1)} %collective-permute-done.6.refs_0_), channel_id=1, source_target_pairs={{0,2},{2,0},{4,6},{6,4},{8,10},{10,8},{12,14},{14,12},{1,3},{3,1},... | collective-permute-start | bytes 835592 | tf_op jit(solution)/shard_map/ppermute | solution.py:313
  29.8 2.2 %score.9 = (bf16[128,512]{1,0:T(8,128)(2,1)S(1)}, bf16[128,512]{1,0:T(8,128)(2,1)S(1)}) custom-call(s32[2]{0:T(128)S(1)} %pad_add_fusion.where_ref, bf16[136,1024]{1,0:T(8,128)(2,1)S(1)} %collective-permute-done.6.refs_0_, bf16[136,1024]{1,0:T(8,128)(2,1)S(1)} %collective-permute-done.13.refs_1_, bf16[1024,1024]{1,0:T(8,128)(2,1)S(1)} %bitcast.12, ...), custom_call_target="tpu_custom_call" | custom-call | flops 10737418240 | bytes 4980736 | tf_op jit(solution)/shard_map/score/pallas_call | solution.py:244
  32.0 2.9 %collective-permute-start.15 = (bf16[128,512]{1,0:T(8,128)(2,1)S(1)}, bf16[128,512]{1,0:T(8,128)(2,1)S(1)}, u32[]{:S(2)}, u32[]{:S(2)}) collective-permute-start(bf16[128,512]{1,0:T(8,128)(2,1)S(1)} %get-tuple-element.49), channel_id=1, source_target_pairs={{0,10},{2,8},{4,14},{6,12},{8,2},{10,0},{12,6},{14,4},{1,11},{3,9}... | collective-permute-start | bytes 393224 | tf_op jit(solution)/shard_map/ppermute | solution.py:313
  35.1 1.6 %collective-permute-start.16 = (bf16[128,512]{1,0:T(8,128)(2,1)S(1)}, bf16[128,512]{1,0:T(8,128)(2,1)S(1)}, u32[]{:S(2)}, u32[]{:S(2)}) collective-permute-start(bf16[128,512]{1,0:T(8,128)(2,1)S(1)} %get-tuple-element.52), channel_id=1, source_target_pairs={{0,12},{2,14},{4,8},{6,10},{8,4},{10,6},{12,0},{14,2},{1,13},{3,15... | collective-permute-start | bytes 393224 | tf_op jit(solution)/shard_map/ppermute | solution.py:313
  37.2 2.2 %score.7 = bf16[128,512]{1,0:T(8,128)(2,1)S(1)} custom-call(s32[2]{0:T(128)S(1)} %pad_add_fusion.where_ref, bf16[136,1024]{1,0:T(8,128)(2,1)S(1)} %collective-permute-done.7.refs_0_, bf16[1024,1024]{1,0:T(8,128)(2,1)S(1)} %bitcast.13, bf16[1024,1024]{1,0:T(8,128)(2,1)S(1)} %get-tuple-element.31.refs_3_.refs_2_, f32[1,1024]{1,0:T(1,128)S(1)} %norms.2.refs_4_.refs_3_, ...), custom_call_target="tpu_custom_call" | custom-call | flops 536870912 | bytes 4587520 | tf_op jit(solution)/shard_map/score/pallas_call | solution.py:244
  39.4 3.5 %collective-permute-start.10 = (bf16[128,512]{1,0:T(8,128)(2,1)S(1)}, bf16[128,512]{1,0:T(8,128)(2,1)S(1)}, u32[]{:S(2)}, u32[]{:S(2)}) collective-permute-start(bf16[128,512]{1,0:T(8,128)(2,1)S(1)} %score.7), channel_id=1, source_target_pairs={{0,14},{2,12},{4,10},{6,8},{8,6},{10,4},{12,2},{14,0},{1,15},{3,13... | collective-permute-start | bytes 393224 | tf_op jit(solution)/shard_map/ppermute | solution.py:313
  43.0 2.2 %score.8 = bf16[128,512]{1,0:T(8,128)(2,1)S(1)} custom-call(s32[2]{0:T(128)S(1)} %pad_add_fusion.where_ref, bf16[136,1024]{1,0:T(8,128)(2,1)S(1)} %collective-permute-done.11.refs_0_, bf16[1024,1024]{1,0:T(8,128)(2,1)S(1)} %bitcast.14, bf16[1024,1024]{1,0:T(8,128)(2,1)S(1)} %get-tuple-element.31.refs_3_.refs_2_, f32[1,1024]{1,0:T(1,128)S(1)} %norms.2.refs_4_.refs_3_, ...), custom_call_target="tpu_custom_call" | custom-call | flops 536870912 | bytes 4587520 | tf_op jit(solution)/shard_map/score/pallas_call | solution.py:244
  46.0 2.3 %collective-permute-done.16.refs_5_ = bf16[128,512]{1,0:T(8,128)(2,1)S(1)} collective-permute-done((bf16[128,512]{1,0:T(8,128)(2,1)S(1)}, bf16[128,512]{1,0:T(8,128)(2,1)S(1)}, u32[]{:S(2)}, u32[]{:S(2)}) %collective-permute-start.16) | collective-permute-done | bytes 131104 | tf_op jit(solution)/shard_map/ppermute | solution.py:313
  48.8 1.6 %collective-permute-done.10.refs_1_ = bf16[128,512]{1,0:T(8,128)(2,1)S(1)} collective-permute-done((bf16[128,512]{1,0:T(8,128)(2,1)S(1)}, bf16[128,512]{1,0:T(8,128)(2,1)S(1)}, u32[]{:S(2)}, u32[]{:S(2)}) %collective-permute-start.10) | collective-permute-done | bytes 131104 | tf_op jit(solution)/shard_map/ppermute | solution.py:313
  50.4 1.4 %collective-permute-done.12.refs_0_ = bf16[128,512]{1,0:T(8,128)(2,1)S(1)} collective-permute-done((bf16[128,512]{1,0:T(8,128)(2,1)S(1)}, bf16[128,512]{1,0:T(8,128)(2,1)S(1)}, u32[]{:S(2)}, u32[]{:S(2)}) %collective-permute-start.12) | collective-permute-done | bytes 131104 | tf_op jit(solution)/shard_map/ppermute | solution.py:313
  51.8 1.4 %answer.3 = bf16[128,4,512]{2,1,0:T(4,128)(2,1)} custom-call(s32[4,128]{1,0:T(4,128)S(1)} %broadcast_xor_fusion.1.offset_ref, bf16[128,512]{1,0:T(8,128)(2,1)S(1)} %collective-permute-done.12.refs_0_, bf16[128,512]{1,0:T(8,128)(2,1)S(1)} %collective-permute-done.10.refs_1_, bf16[128,2048]{1,0:T(8,128)(2,1)S(1)} %answer.2.refs_2_), custom_call_target="tpu_custom_call" | custom-call | tf_op jit(solution)/shard_map/answer/pallas_call | solution.py:296
  (38 shorter events, 6.2 us)
Async XLA Ops:
  0.0 12.5 %collective-permute-start.2 = (bf16[1024,1024]{1,0:T(8,128)(2,1)}, bf16[1024,1024]{1,0:T(8,128)(2,1)S(1)}, u32[]{:S(2)}, u32[]{:S(2)}) collective-permute-start(bf16[1024,1024]{1,0:T(8,128)(2,1)} %bitcast.8), channel_id=1, source_target_pairs={{0,1},{1,0},{2,3},{3,2},{4,5},{5,4},{6,7},{7,6},{8,9},{9,8},{10,11... | collective-permute-start | bytes 6291464 | tf_op jit(solution)/shard_map/ppermute | solution.py:325
  0.5 18.4 %collective-permute-start = (bf16[128,1024]{1,0:T(8,128)(2,1)}, bf16[128,1024]{1,0:T(8,128)(2,1)S(1)}, u32[]{:S(2)}, u32[]{:S(2)}) collective-permute-start(bf16[128,1024]{1,0:T(8,128)(2,1)} %queries_ref.1), channel_id=1, source_target_pairs={{0,8},{2,10},{4,12},{6,14},{8,0},{10,2},{12,4},{14,6},{1,9},{3,11}... | collective-permute-start | bytes 786440 | tf_op jit(solution)/shard_map/ppermute | solution.py:313
  4.0 14.8 %collective-permute-start.1 = (bf16[128,1024]{1,0:T(8,128)(2,1)}, bf16[128,1024]{1,0:T(8,128)(2,1)S(1)}, u32[]{:S(2)}, u32[]{:S(2)}) collective-permute-start(bf16[128,1024]{1,0:T(8,128)(2,1)} %queries_ref.1), channel_id=1, source_target_pairs={{0,4},{2,6},{4,0},{6,2},{8,12},{10,14},{12,8},{14,10},{1,5},{3,7},... | collective-permute-start | bytes 786440 | tf_op jit(solution)/shard_map/ppermute | solution.py:313
  5.6 0.7 %copy-start.3 = (s32[128,4]{0,1:T(4,128)S(1)}, s32[128,4]{0,1:T(4,128)}, u32[]{:S(2)}) copy-start(s32[128,4]{0,1:T(4,128)} %param.5) | copy-start | bytes 6148
  6.3 0.7 %copy-start.5 = (s32[128,4,4]{0,2,1:T(4,128)S(1)}, s32[128,4,4]{0,2,1:T(4,128)}, u32[]{:S(2)}) copy-start(s32[128,4,4]{0,2,1:T(4,128)} %param.6) | copy-start | bytes 24580
  7.0 0.9 %copy-start.2 = (bf16[128,1024]{1,0:T(8,128)(2,1)S(1)}, bf16[128,1024]{1,0:T(8,128)(2,1)}, u32[]{:S(2)}) copy-start(bf16[128,1024]{1,0:T(8,128)(2,1)} %queries_ref.1) | copy-start | bytes 786436
  8.0 8.6 %collective-permute-start.4 = (bf16[136,1024]{1,0:T(8,128)(2,1)S(1)}, bf16[136,1024]{1,0:T(8,128)(2,1)S(1)}, u32[]{:S(2)}, u32[]{:S(2)}) collective-permute-start(bf16[136,1024]{1,0:T(8,128)(2,1)S(1)} %pack.3.refs_0_), channel_id=1, source_target_pairs={{0,2},{2,0},{4,6},{6,4},{8,10},{10,8},{12,14},{14,12},{1,3},{3,1},... | collective-permute-start | bytes 835592 | tf_op jit(solution)/shard_map/ppermute | solution.py:313
  9.6 1.6 %copy-start = (bf16[1,1024,1024]{2,1,0:T(8,128)(2,1)S(1)}, bf16[1,1024,1024]{2,1,0:T(8,128)(2,1)}, u32[]{:S(2)}) copy-start(bf16[1,1024,1024]{2,1,0:T(8,128)(2,1)} %param.7) | copy-start | bytes 6291460
  12.5 4.1 %copy-start.1 = (bf16[1,1024,1024]{2,1,0:T(8,128)(2,1)S(1)}, bf16[1,1024,1024]{2,1,0:T(8,128)(2,1)}, u32[]{:S(2)}) copy-start(bf16[1,1024,1024]{2,1,0:T(8,128)(2,1)} %param.7) | copy-start | bytes 6291460
  13.8 5.1 %collective-permute-start.3 = (bf16[32,128]{1,0:T(8,128)(2,1)S(1)}, bf16[32,128]{1,0:T(8,128)(2,1)S(1)}, u32[]{:S(2)}, u32[]{:S(2)}) collective-permute-start(bf16[32,128]{1,0:T(8,128)(2,1)S(1)} %list_ids.1.ids_ref), channel_id=1, source_target_pairs={{0,4},{2,6},{4,0},{6,2},{8,12},{10,14},{12,8},{14,10},{1,5},{3,7},... | collective-permute-start | bytes 24584 | tf_op jit(solution)/shard_map/ppermute | solution.py:313
  14.3 4.6 %collective-permute-start.5 = (bf16[32,128]{1,0:T(8,128)(2,1)S(1)}, bf16[32,128]{1,0:T(8,128)(2,1)S(1)}, u32[]{:S(2)}, u32[]{:S(2)}) collective-permute-start(bf16[32,128]{1,0:T(8,128)(2,1)S(1)} %list_ids.1.ids_ref), channel_id=1, source_target_pairs={{0,8},{2,10},{4,12},{6,14},{8,0},{10,2},{12,4},{14,6},{1,9},{3,11}... | collective-permute-start | bytes 24584 | tf_op jit(solution)/shard_map/ppermute | solution.py:313
  18.9 9.1 %collective-permute-start.6 = (bf16[136,1024]{1,0:T(8,128)(2,1)S(1)}, bf16[136,1024]{1,0:T(8,128)(2,1)S(1)}, u32[]{:S(2)}, u32[]{:S(2)}) collective-permute-start(bf16[136,1024]{1,0:T(8,128)(2,1)S(1)} %pack.4.refs_0_), channel_id=1, source_target_pairs={{0,4},{2,6},{4,0},{6,2},{8,12},{10,14},{12,8},{14,10},{1,5},{3,7},... | collective-permute-start | bytes 835592 | tf_op jit(solution)/shard_map/ppermute | solution.py:313
  20.5 9.3 %collective-permute-start.13 = (bf16[136,1024]{1,0:T(8,128)(2,1)S(1)}, bf16[136,1024]{1,0:T(8,128)(2,1)S(1)}, u32[]{:S(2)}, u32[]{:S(2)}) collective-permute-start(bf16[136,1024]{1,0:T(8,128)(2,1)S(1)} %pack.4.refs_0_), channel_id=1, source_target_pairs={{0,2},{2,0},{4,6},{6,4},{8,10},{10,8},{12,14},{14,12},{1,3},{3,1},... | collective-permute-start | bytes 835592 | tf_op jit(solution)/shard_map/ppermute | solution.py:313
  21.0 13.9 %collective-permute-start.9 = (bf16[128,512]{1,0:T(8,128)(2,1)S(1)}, bf16[128,512]{1,0:T(8,128)(2,1)S(1)}, u32[]{:S(2)}, u32[]{:S(2)}) collective-permute-start(bf16[128,512]{1,0:T(8,128)(2,1)S(1)} %get-tuple-element.40), channel_id=1, source_target_pairs={{0,2},{2,0},{4,6},{6,4},{8,10},{10,8},{12,14},{14,12},{1,3},{3,1},... | collective-permute-start | bytes 393224 | tf_op jit(solution)/shard_map/ppermute | solution.py:313
  24.8 10.3 %collective-permute-start.8 = (bf16[128,512]{1,0:T(8,128)(2,1)S(1)}, bf16[128,512]{1,0:T(8,128)(2,1)S(1)}, u32[]{:S(2)}, u32[]{:S(2)}) collective-permute-start(bf16[128,512]{1,0:T(8,128)(2,1)S(1)} %get-tuple-element.38), channel_id=1, source_target_pairs={{0,8},{2,10},{4,12},{6,14},{8,0},{10,2},{12,4},{14,6},{1,9},{3,11}... | collective-permute-start | bytes 393224 | tf_op jit(solution)/shard_map/ppermute | solution.py:313
  28.0 9.2 %collective-permute-start.7 = (bf16[136,1024]{1,0:T(8,128)(2,1)S(1)}, bf16[136,1024]{1,0:T(8,128)(2,1)S(1)}, u32[]{:S(2)}, u32[]{:S(2)}) collective-permute-start(bf16[136,1024]{1,0:T(8,128)(2,1)S(1)} %collective-permute-done.6.refs_0_), channel_id=1, source_target_pairs={{0,2},{2,0},{4,6},{6,4},{8,10},{10,8},{12,14},{14,12},{1,3},{3,1},... | collective-permute-start | bytes 835592 | tf_op jit(solution)/shard_map/ppermute | solution.py:313
  29.8 13.2 %collective-permute-start.11 = (bf16[136,1024]{1,0:T(8,128)(2,1)S(1)}, bf16[136,1024]{1,0:T(8,128)(2,1)S(1)}, u32[]{:S(2)}, u32[]{:S(2)}) collective-permute-start(bf16[136,1024]{1,0:T(8,128)(2,1)S(1)} %collective-permute-done.4.refs_1_), channel_id=1, source_target_pairs={{0,4},{2,6},{4,0},{6,2},{8,12},{10,14},{12,8},{14,10},{1,5},{3,7},... | collective-permute-start | bytes 835592 | tf_op jit(solution)/shard_map/ppermute | solution.py:313
  32.0 13.9 %collective-permute-start.15 = (bf16[128,512]{1,0:T(8,128)(2,1)S(1)}, bf16[128,512]{1,0:T(8,128)(2,1)S(1)}, u32[]{:S(2)}, u32[]{:S(2)}) collective-permute-start(bf16[128,512]{1,0:T(8,128)(2,1)S(1)} %get-tuple-element.49), channel_id=1, source_target_pairs={{0,10},{2,8},{4,14},{6,12},{8,2},{10,0},{12,6},{14,4},{1,11},{3,9}... | collective-permute-start | bytes 393224 | tf_op jit(solution)/shard_map/ppermute | solution.py:313
  34.9 11.0 %collective-permute-start.14 = (bf16[128,512]{1,0:T(8,128)(2,1)S(1)}, bf16[128,512]{1,0:T(8,128)(2,1)S(1)}, u32[]{:S(2)}, u32[]{:S(2)}) collective-permute-start(bf16[128,512]{1,0:T(8,128)(2,1)S(1)} %get-tuple-element.50), channel_id=1, source_target_pairs={{0,4},{2,6},{4,0},{6,2},{8,12},{10,14},{12,8},{14,10},{1,5},{3,7},... | collective-permute-start | bytes 393224 | tf_op jit(solution)/shard_map/ppermute | solution.py:313
  35.1 7.8 %copy-start.4 = (s32[128,4]{0,1:T(4,128)S(1)}, s32[128,4]{0,1:T(4,128)}, u32[]{:S(2)}) copy-start(s32[128,4]{0,1:T(4,128)} %param.5) | copy-start | bytes 6148
  35.1 13.2 %collective-permute-start.16 = (bf16[128,512]{1,0:T(8,128)(2,1)S(1)}, bf16[128,512]{1,0:T(8,128)(2,1)S(1)}, u32[]{:S(2)}, u32[]{:S(2)}) collective-permute-start(bf16[128,512]{1,0:T(8,128)(2,1)S(1)} %get-tuple-element.52), channel_id=1, source_target_pairs={{0,12},{2,14},{4,8},{6,10},{8,4},{10,6},{12,0},{14,2},{1,13},{3,15... | collective-permute-start | bytes 393224 | tf_op jit(solution)/shard_map/ppermute | solution.py:313
  39.4 11.0 %collective-permute-start.10 = (bf16[128,512]{1,0:T(8,128)(2,1)S(1)}, bf16[128,512]{1,0:T(8,128)(2,1)S(1)}, u32[]{:S(2)}, u32[]{:S(2)}) collective-permute-start(bf16[128,512]{1,0:T(8,128)(2,1)S(1)} %score.7), channel_id=1, source_target_pairs={{0,14},{2,12},{4,10},{6,8},{8,6},{10,4},{12,2},{14,0},{1,15},{3,13... | collective-permute-start | bytes 393224 | tf_op jit(solution)/shard_map/ppermute | solution.py:313
  45.2 6.7 %collective-permute-start.12 = (bf16[128,512]{1,0:T(8,128)(2,1)S(1)}, bf16[128,512]{1,0:T(8,128)(2,1)S(1)}, u32[]{:S(2)}, u32[]{:S(2)}) collective-permute-start(bf16[128,512]{1,0:T(8,128)(2,1)S(1)} %score.8), channel_id=1, source_target_pairs={{0,6},{2,4},{4,2},{6,0},{8,14},{10,12},{12,10},{14,8},{1,7},{3,5},... | collective-permute-start | bytes 393224 | tf_op jit(solution)/shard_map/ppermute | solution.py:313

commit v6 on v5

--- a/solution.py
+++ b/solution.py
@@ -338,7 +338,6 @@
     barrier = lax.optimization_barrier
     results, back = {}, {}
     results[0], results[1] = scored(0, 1, weight=W01)
-    back[1] = hop(results[1], 1)
     held[4], held[2], ids_2, results[0] = barrier((held[4], held[2], ids_2, results[0]))
     held[4] = pack(held[4], ids_4, 8)
     held[2] = pack(held[2], ids_2, 8)
@@ -346,6 +345,8 @@
     held[5] = hop(held[4], 1)
     results[4], results[2] = scored(4, 2, weight=W42)
     back[4] = hop(results[4], 4)
+    results[1], results[4] = barrier((results[1], results[4]))
+    back[1] = hop(results[1], 1)
     held[6], held[1], results[4] = barrier((held[6], held[1], results[4]))
     held[7] = hop(held[6], 1)
     held[3] = hop(held[1], 2)

time: 53.5 us -> 54.1 us (1.011)
  starting transfers between devices: 23.3 us -> 24 us
    ppermute x16, starting transfers between devices: 22.9 us -> 23.5 us  [hop(): lax.ppermute(value, 'region', [(r, r ^ mask) for r in range(regions)])]
  transfers between devices with their start and end apart: 17 -> 17, of which waited for: 6 -> 5; matrix products, arithmetic and copies ran while one was open for 0% -> 0% of each run, Pallas kernels for 27% -> 27%
where the time goes in v6:
time: 54.1 us; the launch traced here: 53.8 us
  starting transfers between devices  24 us (44%)
  Pallas kernels  15.8 us (29%)
  waiting for transfers between devices  9.88 us (18%)
  local copies, waits for them, and re-layouts  3.92 us (7%)
    ppermute x16, starting transfers between devices, hop(): lax.ppermute(value, 'region', [(r, r ^ mask) for r in range(regions)])  23.5 us
    pallas_call x5, Pallas kernels, score(): pl.pallas_call(functools.partial(score_kernel, n_sets, q_count, probe_cou...  11.2 us
    ppermute x16, waiting for transfers between devices, hop(): lax.ppermute(value, 'region', [(r, r ^ mask) for r in range(regions)])  9.88 us
    unnamed x12, local copies, waits for them, and re-layouts  3.92 us
    pallas_call x2, Pallas kernels, norms(): pl.pallas_call(functools.partial(norms_kernel, scale), out_shape=shapes,...  2.57 us
    pallas_call x2, Pallas kernels, answer(): pl.pallas_call(functools.partial(answer_kernel, names), out_shape=jax.Sha...  1.94 us
  transfers between devices with their start and end apart: 17, of which 5 were waited for; matrix products, arithmetic and copies ran while one was open for 0% of the time, Pallas kernels for 27%

profile of v6, /device:TPU:0, one launch (start us, length us, event | category | flops | bytes accessed | tf_op | source)
XLA Modules:
  0.0 53.8 jit_solution(14444907566654564266)
XLA Ops:
  0.5 3.6 %collective-permute-start = (bf16[128,1024]{1,0:T(8,128)(2,1)}, bf16[128,1024]{1,0:T(8,128)(2,1)S(1)}, u32[]{:S(2)}, u32[]{:S(2)}) collective-permute-start(bf16[128,1024]{1,0:T(8,128)(2,1)} %queries_ref.1), channel_id=1, source_target_pairs={{0,8},{2,10},{4,12},{6,14},{8,0},{10,2},{12,4},{14,6},{1,9},{3,11}... | collective-permute-start | bytes 786440 | tf_op jit(solution)/shard_map/ppermute | solution.py:313
  4.0 1.6 %collective-permute-start.1 = (bf16[128,1024]{1,0:T(8,128)(2,1)}, bf16[128,1024]{1,0:T(8,128)(2,1)S(1)}, u32[]{:S(2)}, u32[]{:S(2)}) collective-permute-start(bf16[128,1024]{1,0:T(8,128)(2,1)} %queries_ref.1), channel_id=1, source_target_pairs={{0,4},{2,6},{4,0},{6,2},{8,12},{10,14},{12,8},{14,10},{1,5},{3,7},... | collective-permute-start | bytes 786440 | tf_op jit(solution)/shard_map/ppermute | solution.py:313
  7.0 0.9 %copy-done.2 = bf16[128,1024]{1,0:T(8,128)(2,1)S(1)} copy-done((bf16[128,1024]{1,0:T(8,128)(2,1)S(1)}, bf16[128,1024]{1,0:T(8,128)(2,1)}, u32[]{:S(2)}) %copy-start.2) | copy-done | bytes 262168
  8.0 1.6 %collective-permute-start.4 = (bf16[136,1024]{1,0:T(8,128)(2,1)S(1)}, bf16[136,1024]{1,0:T(8,128)(2,1)S(1)}, u32[]{:S(2)}, u32[]{:S(2)}) collective-permute-start(bf16[136,1024]{1,0:T(8,128)(2,1)S(1)} %pack.3.refs_0_), channel_id=1, source_target_pairs={{0,2},{2,0},{4,6},{6,4},{8,10},{10,8},{12,14},{14,12},{1,3},{3,1},... | collective-permute-start | bytes 835592 | tf_op jit(solution)/shard_map/ppermute | solution.py:313
  9.6 1.6 %copy-done = bf16[1,1024,1024]{2,1,0:T(8,128)(2,1)S(1)} copy-done((bf16[1,1024,1024]{2,1,0:T(8,128)(2,1)S(1)}, bf16[1,1024,1024]{2,1,0:T(8,128)(2,1)}, u32[]{:S(2)}) %copy-start) | copy-done | bytes 2097176
  11.2 1.3 %norms.2.refs_4_.refs_3_ = f32[1,1024]{1,0:T(1,128)S(1)} custom-call(bf16[1024,1024]{1,0:T(8,128)(2,1)S(1)} %bitcast.9), custom_call_target="tpu_custom_call" | custom-call | flops 4000000000 | bytes 2097152 | tf_op jit(solution)/shard_map/norms/pallas_call | solution.py:166
  12.5 1.3 %norms.3 = (f32[1,1024]{1,0:T(1,128)S(1)}, bf16[1024,1024]{1,0:T(8,128)(2,1)S(1)}) custom-call(bf16[1024,1024]{1,0:T(8,128)(2,1)S(1)} %collective-permute-done.2.rows_ref), custom_call_target="tpu_custom_call" | custom-call | flops 4000000000 | bytes 4194304 | tf_op jit(solution)/shard_map/norms/pallas_call | solution.py:166
  14.6 1.9 %collective-permute-done.4.refs_1_ = bf16[136,1024]{1,0:T(8,128)(2,1)S(1)} collective-permute-done((bf16[136,1024]{1,0:T(8,128)(2,1)S(1)}, bf16[136,1024]{1,0:T(8,128)(2,1)S(1)}, u32[]{:S(2)}, u32[]{:S(2)}) %collective-permute-start.4) | collective-permute-done | bytes 278560 | tf_op jit(solution)/shard_map/ppermute | solution.py:313
  16.6 2.3 %score.5 = (bf16[128,512]{1,0:T(8,128)(2,1)S(1)}, bf16[128,512]{1,0:T(8,128)(2,1)S(1)}) custom-call(s32[2]{0:T(128)S(1)} %pad_add_fusion.where_ref, bf16[136,1024]{1,0:T(8,128)(2,1)S(1)} %pack.3.refs_0_, bf16[136,1024]{1,0:T(8,128)(2,1)S(1)} %collective-permute-done.4.refs_1_, bf16[1024,1024]{1,0:T(8,128)(2,1)S(1)} %bitcast.10, ...), custom_call_target="tpu_custom_call" | custom-call | flops 1073741824 | bytes 4980736 | tf_op jit(solution)/shard_map/score/pallas_call | solution.py:244
  18.9 1.6 %collective-permute-start.6 = (bf16[136,1024]{1,0:T(8,128)(2,1)S(1)}, bf16[136,1024]{1,0:T(8,128)(2,1)S(1)}, u32[]{:S(2)}, u32[]{:S(2)}) collective-permute-start(bf16[136,1024]{1,0:T(8,128)(2,1)S(1)} %pack.4.refs_0_), channel_id=1, source_target_pairs={{0,4},{2,6},{4,0},{6,2},{8,12},{10,14},{12,8},{14,10},{1,5},{3,7},... | collective-permute-start | bytes 835592 | tf_op jit(solution)/shard_map/ppermute | solution.py:313
  21.0 2.2 %score.6 = (bf16[128,512]{1,0:T(8,128)(2,1)S(1)}, bf16[128,512]{1,0:T(8,128)(2,1)S(1)}) custom-call(s32[2]{0:T(128)S(1)} %pad_add_fusion.where_ref, bf16[136,1024]{1,0:T(8,128)(2,1)S(1)} %pack.4.refs_0_, bf16[136,1024]{1,0:T(8,128)(2,1)S(1)} %pack.5.refs_1_, bf16[1024,1024]{1,0:T(8,128)(2,1)S(1)} %bitcast.11, ...), custom_call_target="tpu_custom_call" | custom-call | flops 1073741824 | bytes 4980736 | tf_op jit(solution)/shard_map/score/pallas_call | solution.py:244
  23.3 1.9 %collective-permute-start.8 = (bf16[128,512]{1,0:T(8,128)(2,1)S(1)}, bf16[128,512]{1,0:T(8,128)(2,1)S(1)}, u32[]{:S(2)}, u32[]{:S(2)}) collective-permute-start(bf16[128,512]{1,0:T(8,128)(2,1)S(1)} %get-tuple-element.40), channel_id=1, source_target_pairs={{0,8},{2,10},{4,12},{6,14},{8,0},{10,2},{12,4},{14,6},{1,9},{3,11}... | collective-permute-start | bytes 393224 | tf_op jit(solution)/shard_map/ppermute | solution.py:313
  25.8 2.5 %collective-permute-done.6.refs_0_ = bf16[136,1024]{1,0:T(8,128)(2,1)S(1)} collective-permute-done((bf16[136,1024]{1,0:T(8,128)(2,1)S(1)}, bf16[136,1024]{1,0:T(8,128)(2,1)S(1)}, u32[]{:S(2)}, u32[]{:S(2)}) %collective-permute-start.6) | collective-permute-done | bytes 278560 | tf_op jit(solution)/shard_map/ppermute | solution.py:313
  28.2 2.2 %collective-permute-start.7 = (bf16[136,1024]{1,0:T(8,128)(2,1)S(1)}, bf16[136,1024]{1,0:T(8,128)(2,1)S(1)}, u32[]{:S(2)}, u32[]{:S(2)}) collective-permute-start(bf16[136,1024]{1,0:T(8,128)(2,1)S(1)} %collective-permute-done.6.refs_0_), channel_id=1, source_target_pairs={{0,2},{2,0},{4,6},{6,4},{8,10},{10,8},{12,14},{14,12},{1,3},{3,1},... | collective-permute-start | bytes 835592 | tf_op jit(solution)/shard_map/ppermute | solution.py:313
  30.4 2.2 %score.9 = (bf16[128,512]{1,0:T(8,128)(2,1)S(1)}, bf16[128,512]{1,0:T(8,128)(2,1)S(1)}) custom-call(s32[2]{0:T(128)S(1)} %pad_add_fusion.where_ref, bf16[136,1024]{1,0:T(8,128)(2,1)S(1)} %collective-permute-done.6.refs_0_, bf16[136,1024]{1,0:T(8,128)(2,1)S(1)} %collective-permute-done.13.refs_1_, bf16[1024,1024]{1,0:T(8,128)(2,1)S(1)} %bitcast.12, ...), custom_call_target="tpu_custom_call" | custom-call | flops 10737418240 | bytes 4980736 | tf_op jit(solution)/shard_map/score/pallas_call | solution.py:244
  32.6 2.9 %collective-permute-start.15 = (bf16[128,512]{1,0:T(8,128)(2,1)S(1)}, bf16[128,512]{1,0:T(8,128)(2,1)S(1)}, u32[]{:S(2)}, u32[]{:S(2)}) collective-permute-start(bf16[128,512]{1,0:T(8,128)(2,1)S(1)} %get-tuple-element.51), channel_id=1, source_target_pairs={{0,10},{2,8},{4,14},{6,12},{8,2},{10,0},{12,6},{14,4},{1,11},{3,9}... | collective-permute-start | bytes 393224 | tf_op jit(solution)/shard_map/ppermute | solution.py:313
  35.5 2.1 %collective-permute-start.16 = (bf16[128,512]{1,0:T(8,128)(2,1)S(1)}, bf16[128,512]{1,0:T(8,128)(2,1)S(1)}, u32[]{:S(2)}, u32[]{:S(2)}) collective-permute-start(bf16[128,512]{1,0:T(8,128)(2,1)S(1)} %get-tuple-element.54), channel_id=1, source_target_pairs={{0,12},{2,14},{4,8},{6,10},{8,4},{10,6},{12,0},{14,2},{1,13},{3,15... | collective-permute-start | bytes 393224 | tf_op jit(solution)/shard_map/ppermute | solution.py:313
  37.6 2.2 %score.7 = bf16[128,512]{1,0:T(8,128)(2,1)S(1)} custom-call(s32[2]{0:T(128)S(1)} %pad_add_fusion.where_ref, bf16[136,1024]{1,0:T(8,128)(2,1)S(1)} %collective-permute-done.7.refs_0_, bf16[1024,1024]{1,0:T(8,128)(2,1)S(1)} %bitcast.13, bf16[1024,1024]{1,0:T(8,128)(2,1)S(1)} %get-tuple-element.32.refs_3_.refs_2_, f32[1,1024]{1,0:T(1,128)S(1)} %norms.2.refs_4_.refs_3_, ...), custom_call_target="tpu_custom_call" | custom-call | flops 536870912 | bytes 4587520 | tf_op jit(solution)/shard_map/score/pallas_call | solution.py:244
  39.9 4.2 %collective-permute-start.10 = (bf16[128,512]{1,0:T(8,128)(2,1)S(1)}, bf16[128,512]{1,0:T(8,128)(2,1)S(1)}, u32[]{:S(2)}, u32[]{:S(2)}) collective-permute-start(bf16[128,512]{1,0:T(8,128)(2,1)S(1)} %score.7), channel_id=1, source_target_pairs={{0,14},{2,12},{4,10},{6,8},{8,6},{10,4},{12,2},{14,0},{1,15},{3,13... | collective-permute-start | bytes 393224 | tf_op jit(solution)/shard_map/ppermute | solution.py:313
  44.1 2.2 %score.8 = bf16[128,512]{1,0:T(8,128)(2,1)S(1)} custom-call(s32[2]{0:T(128)S(1)} %pad_add_fusion.where_ref, bf16[136,1024]{1,0:T(8,128)(2,1)S(1)} %collective-permute-done.11.refs_0_, bf16[1024,1024]{1,0:T(8,128)(2,1)S(1)} %bitcast.14, bf16[1024,1024]{1,0:T(8,128)(2,1)S(1)} %get-tuple-element.32.refs_3_.refs_2_, f32[1,1024]{1,0:T(1,128)S(1)} %norms.2.refs_4_.refs_3_, ...), custom_call_target="tpu_custom_call" | custom-call | flops 536870912 | bytes 4587520 | tf_op jit(solution)/shard_map/score/pallas_call | solution.py:244
  46.4 2.8 %collective-permute-done.16.refs_5_ = bf16[128,512]{1,0:T(8,128)(2,1)S(1)} collective-permute-done((bf16[128,512]{1,0:T(8,128)(2,1)S(1)}, bf16[128,512]{1,0:T(8,128)(2,1)S(1)}, u32[]{:S(2)}, u32[]{:S(2)}) %collective-permute-start.16) | collective-permute-done | bytes 131104 | tf_op jit(solution)/shard_map/ppermute | solution.py:313
  49.8 1.2 %collective-permute-done.10.refs_1_ = bf16[128,512]{1,0:T(8,128)(2,1)S(1)} collective-permute-done((bf16[128,512]{1,0:T(8,128)(2,1)S(1)}, bf16[128,512]{1,0:T(8,128)(2,1)S(1)}, u32[]{:S(2)}, u32[]{:S(2)}) %collective-permute-start.10) | collective-permute-done | bytes 131104 | tf_op jit(solution)/shard_map/ppermute | solution.py:313
  51.0 1.4 %collective-permute-done.12.refs_0_ = bf16[128,512]{1,0:T(8,128)(2,1)S(1)} collective-permute-done((bf16[128,512]{1,0:T(8,128)(2,1)S(1)}, bf16[128,512]{1,0:T(8,128)(2,1)S(1)}, u32[]{:S(2)}, u32[]{:S(2)}) %collective-permute-start.12) | collective-permute-done | bytes 131104 | tf_op jit(solution)/shard_map/ppermute | solution.py:313
  52.4 1.4 %answer.3 = bf16[128,4,512]{2,1,0:T(4,128)(2,1)} custom-call(s32[4,128]{1,0:T(4,128)S(1)} %broadcast_xor_fusion.1.offset_ref, bf16[128,512]{1,0:T(8,128)(2,1)S(1)} %collective-permute-done.12.refs_0_, bf16[128,512]{1,0:T(8,128)(2,1)S(1)} %collective-permute-done.10.refs_1_, bf16[128,2048]{1,0:T(8,128)(2,1)S(1)} %answer.2.refs_2_), custom_call_target="tpu_custom_call" | custom-call | tf_op jit(solution)/shard_map/answer/pallas_call | solution.py:296
  (38 shorter events, 4.5 us)
Async XLA Ops:
  0.0 12.5 %collective-permute-start.2 = (bf16[1024,1024]{1,0:T(8,128)(2,1)}, bf16[1024,1024]{1,0:T(8,128)(2,1)S(1)}, u32[]{:S(2)}, u32[]{:S(2)}) collective-permute-start(bf16[1024,1024]{1,0:T(8,128)(2,1)} %bitcast.8), channel_id=1, source_target_pairs={{0,1},{1,0},{2,3},{3,2},{4,5},{5,4},{6,7},{7,6},{8,9},{9,8},{10,11... | collective-permute-start | bytes 6291464 | tf_op jit(solution)/shard_map/ppermute | solution.py:325
  0.5 18.4 %collective-permute-start = (bf16[128,1024]{1,0:T(8,128)(2,1)}, bf16[128,1024]{1,0:T(8,128)(2,1)S(1)}, u32[]{:S(2)}, u32[]{:S(2)}) collective-permute-start(bf16[128,1024]{1,0:T(8,128)(2,1)} %queries_ref.1), channel_id=1, source_target_pairs={{0,8},{2,10},{4,12},{6,14},{8,0},{10,2},{12,4},{14,6},{1,9},{3,11}... | collective-permute-start | bytes 786440 | tf_op jit(solution)/shard_map/ppermute | solution.py:313
  4.0 14.8 %collective-permute-start.1 = (bf16[128,1024]{1,0:T(8,128)(2,1)}, bf16[128,1024]{1,0:T(8,128)(2,1)S(1)}, u32[]{:S(2)}, u32[]{:S(2)}) collective-permute-start(bf16[128,1024]{1,0:T(8,128)(2,1)} %queries_ref.1), channel_id=1, source_target_pairs={{0,4},{2,6},{4,0},{6,2},{8,12},{10,14},{12,8},{14,10},{1,5},{3,7},... | collective-permute-start | bytes 786440 | tf_op jit(solution)/shard_map/ppermute | solution.py:313
  5.6 0.7 %copy-start.3 = (s32[128,4]{0,1:T(4,128)S(1)}, s32[128,4]{0,1:T(4,128)}, u32[]{:S(2)}) copy-start(s32[128,4]{0,1:T(4,128)} %param.5) | copy-start | bytes 6148
  6.3 0.7 %copy-start.5 = (s32[128,4,4]{0,2,1:T(4,128)S(1)}, s32[128,4,4]{0,2,1:T(4,128)}, u32[]{:S(2)}) copy-start(s32[128,4,4]{0,2,1:T(4,128)} %param.6) | copy-start | bytes 24580
  7.0 0.9 %copy-start.2 = (bf16[128,1024]{1,0:T(8,128)(2,1)S(1)}, bf16[128,1024]{1,0:T(8,128)(2,1)}, u32[]{:S(2)}) copy-start(bf16[128,1024]{1,0:T(8,128)(2,1)} %queries_ref.1) | copy-start | bytes 786436
  8.0 8.6 %collective-permute-start.4 = (bf16[136,1024]{1,0:T(8,128)(2,1)S(1)}, bf16[136,1024]{1,0:T(8,128)(2,1)S(1)}, u32[]{:S(2)}, u32[]{:S(2)}) collective-permute-start(bf16[136,1024]{1,0:T(8,128)(2,1)S(1)} %pack.3.refs_0_), channel_id=1, source_target_pairs={{0,2},{2,0},{4,6},{6,4},{8,10},{10,8},{12,14},{14,12},{1,3},{3,1},... | collective-permute-start | bytes 835592 | tf_op jit(solution)/shard_map/ppermute | solution.py:313
  9.6 1.6 %copy-start = (bf16[1,1024,1024]{2,1,0:T(8,128)(2,1)S(1)}, bf16[1,1024,1024]{2,1,0:T(8,128)(2,1)}, u32[]{:S(2)}) copy-start(bf16[1,1024,1024]{2,1,0:T(8,128)(2,1)} %param.7) | copy-start | bytes 6291460
  12.5 4.1 %copy-start.1 = (bf16[1,1024,1024]{2,1,0:T(8,128)(2,1)S(1)}, bf16[1,1024,1024]{2,1,0:T(8,128)(2,1)}, u32[]{:S(2)}) copy-start(bf16[1,1024,1024]{2,1,0:T(8,128)(2,1)} %param.7) | copy-start | bytes 6291460
  13.8 5.1 %collective-permute-start.3 = (bf16[32,128]{1,0:T(8,128)(2,1)S(1)}, bf16[32,128]{1,0:T(8,128)(2,1)S(1)}, u32[]{:S(2)}, u32[]{:S(2)}) collective-permute-start(bf16[32,128]{1,0:T(8,128)(2,1)S(1)} %list_ids.1.ids_ref), channel_id=1, source_target_pairs={{0,4},{2,6},{4,0},{6,2},{8,12},{10,14},{12,8},{14,10},{1,5},{3,7},... | collective-permute-start | bytes 24584 | tf_op jit(solution)/shard_map/ppermute | solution.py:313
  14.3 4.6 %collective-permute-start.5 = (bf16[32,128]{1,0:T(8,128)(2,1)S(1)}, bf16[32,128]{1,0:T(8,128)(2,1)S(1)}, u32[]{:S(2)}, u32[]{:S(2)}) collective-permute-start(bf16[32,128]{1,0:T(8,128)(2,1)S(1)} %list_ids.1.ids_ref), channel_id=1, source_target_pairs={{0,8},{2,10},{4,12},{6,14},{8,0},{10,2},{12,4},{14,6},{1,9},{3,11}... | collective-permute-start | bytes 24584 | tf_op jit(solution)/shard_map/ppermute | solution.py:313
  18.9 9.3 %collective-permute-start.6 = (bf16[136,1024]{1,0:T(8,128)(2,1)S(1)}, bf16[136,1024]{1,0:T(8,128)(2,1)S(1)}, u32[]{:S(2)}, u32[]{:S(2)}) collective-permute-start(bf16[136,1024]{1,0:T(8,128)(2,1)S(1)} %pack.4.refs_0_), channel_id=1, source_target_pairs={{0,4},{2,6},{4,0},{6,2},{8,12},{10,14},{12,8},{14,10},{1,5},{3,7},... | collective-permute-start | bytes 835592 | tf_op jit(solution)/shard_map/ppermute | solution.py:313
  20.5 9.9 %collective-permute-start.13 = (bf16[136,1024]{1,0:T(8,128)(2,1)S(1)}, bf16[136,1024]{1,0:T(8,128)(2,1)S(1)}, u32[]{:S(2)}, u32[]{:S(2)}) collective-permute-start(bf16[136,1024]{1,0:T(8,128)(2,1)S(1)} %pack.4.refs_0_), channel_id=1, source_target_pairs={{0,2},{2,0},{4,6},{6,4},{8,10},{10,8},{12,14},{14,12},{1,3},{3,1},... | collective-permute-start | bytes 835592 | tf_op jit(solution)/shard_map/ppermute | solution.py:313
  23.3 12.2 %collective-permute-start.8 = (bf16[128,512]{1,0:T(8,128)(2,1)S(1)}, bf16[128,512]{1,0:T(8,128)(2,1)S(1)}, u32[]{:S(2)}, u32[]{:S(2)}) collective-permute-start(bf16[128,512]{1,0:T(8,128)(2,1)S(1)} %get-tuple-element.40), channel_id=1, source_target_pairs={{0,8},{2,10},{4,12},{6,14},{8,0},{10,2},{12,4},{14,6},{1,9},{3,11}... | collective-permute-start | bytes 393224 | tf_op jit(solution)/shard_map/ppermute | solution.py:313
  25.2 10.3 %collective-permute-start.9 = (bf16[128,512]{1,0:T(8,128)(2,1)S(1)}, bf16[128,512]{1,0:T(8,128)(2,1)S(1)}, u32[]{:S(2)}, u32[]{:S(2)}) collective-permute-start(bf16[128,512]{1,0:T(8,128)(2,1)S(1)} %get-tuple-element.42), channel_id=1, source_target_pairs={{0,2},{2,0},{4,6},{6,4},{8,10},{10,8},{12,14},{14,12},{1,3},{3,1},... | collective-permute-start | bytes 393224 | tf_op jit(solution)/shard_map/ppermute | solution.py:313
  28.2 9.4 %collective-permute-start.7 = (bf16[136,1024]{1,0:T(8,128)(2,1)S(1)}, bf16[136,1024]{1,0:T(8,128)(2,1)S(1)}, u32[]{:S(2)}, u32[]{:S(2)}) collective-permute-start(bf16[136,1024]{1,0:T(8,128)(2,1)S(1)} %collective-permute-done.6.refs_0_), channel_id=1, source_target_pairs={{0,2},{2,0},{4,6},{6,4},{8,10},{10,8},{12,14},{14,12},{1,3},{3,1},... | collective-permute-start | bytes 835592 | tf_op jit(solution)/shard_map/ppermute | solution.py:313
  30.4 13.7 %collective-permute-start.11 = (bf16[136,1024]{1,0:T(8,128)(2,1)S(1)}, bf16[136,1024]{1,0:T(8,128)(2,1)S(1)}, u32[]{:S(2)}, u32[]{:S(2)}) collective-permute-start(bf16[136,1024]{1,0:T(8,128)(2,1)S(1)} %collective-permute-done.4.refs_1_), channel_id=1, source_target_pairs={{0,4},{2,6},{4,0},{6,2},{8,12},{10,14},{12,8},{14,10},{1,5},{3,7},... | collective-permute-start | bytes 835592 | tf_op jit(solution)/shard_map/ppermute | solution.py:313
  32.6 13.8 %collective-permute-start.15 = (bf16[128,512]{1,0:T(8,128)(2,1)S(1)}, bf16[128,512]{1,0:T(8,128)(2,1)S(1)}, u32[]{:S(2)}, u32[]{:S(2)}) collective-permute-start(bf16[128,512]{1,0:T(8,128)(2,1)S(1)} %get-tuple-element.51), channel_id=1, source_target_pairs={{0,10},{2,8},{4,14},{6,12},{8,2},{10,0},{12,6},{14,4},{1,11},{3,9}... | collective-permute-start | bytes 393224 | tf_op jit(solution)/shard_map/ppermute | solution.py:313
  35.5 10.9 %collective-permute-start.14 = (bf16[128,512]{1,0:T(8,128)(2,1)S(1)}, bf16[128,512]{1,0:T(8,128)(2,1)S(1)}, u32[]{:S(2)}, u32[]{:S(2)}) collective-permute-start(bf16[128,512]{1,0:T(8,128)(2,1)S(1)} %get-tuple-element.52), channel_id=1, source_target_pairs={{0,4},{2,6},{4,0},{6,2},{8,12},{10,14},{12,8},{14,10},{1,5},{3,7},... | collective-permute-start | bytes 393224 | tf_op jit(solution)/shard_map/ppermute | solution.py:313
  35.5 8.6 %copy-start.4 = (s32[128,4]{0,1:T(4,128)S(1)}, s32[128,4]{0,1:T(4,128)}, u32[]{:S(2)}) copy-start(s32[128,4]{0,1:T(4,128)} %param.5) | copy-start | bytes 6148
  35.5 13.7 %collective-permute-start.16 = (bf16[128,512]{1,0:T(8,128)(2,1)S(1)}, bf16[128,512]{1,0:T(8,128)(2,1)S(1)}, u32[]{:S(2)}, u32[]{:S(2)}) collective-permute-start(bf16[128,512]{1,0:T(8,128)(2,1)S(1)} %get-tuple-element.54), channel_id=1, source_target_pairs={{0,12},{2,14},{4,8},{6,10},{8,4},{10,6},{12,0},{14,2},{1,13},{3,15... | collective-permute-start | bytes 393224 | tf_op jit(solution)/shard_map/ppermute | solution.py:313
  39.9 11.1 %collective-permute-start.10 = (bf16[128,512]{1,0:T(8,128)(2,1)S(1)}, bf16[128,512]{1,0:T(8,128)(2,1)S(1)}, u32[]{:S(2)}, u32[]{:S(2)}) collective-permute-start(bf16[128,512]{1,0:T(8,128)(2,1)S(1)} %score.7), channel_id=1, source_target_pairs={{0,14},{2,12},{4,10},{6,8},{8,6},{10,4},{12,2},{14,0},{1,15},{3,13... | collective-permute-start | bytes 393224 | tf_op jit(solution)/shard_map/ppermute | solution.py:313
  46.3 6.1 %collective-permute-start.12 = (bf16[128,512]{1,0:T(8,128)(2,1)S(1)}, bf16[128,512]{1,0:T(8,128)(2,1)S(1)}, u32[]{:S(2)}, u32[]{:S(2)}) collective-permute-start(bf16[128,512]{1,0:T(8,128)(2,1)S(1)} %score.8), channel_id=1, source_target_pairs={{0,6},{2,4},{4,2},{6,0},{8,14},{10,12},{12,10},{14,8},{1,7},{3,5},... | collective-permute-start | bytes 393224 | tf_op jit(solution)/shard_map/ppermute | solution.py:313
